TPU v7x, 32 devices: a whole 2x2x4 slice. The times are simulated.
32 devices in a mesh: seq: 8 (over z, core), batch: 4 (over y, x).
Axes of the slice: x: 2, y: 2, z: 4, core: 2. Of those that a mesh axis runs over, the one named last changes fastest.
Arguments:
- tokens: bfloat16 [8, 1024, 1024], P('batch', 'seq'), may hold values from -6 to 6
- cotangent: bfloat16 [8, 1024, 1024], P('batch', 'seq'), may hold values from -6 to 6
- ln_gain: float32 [1024], replicated, may hold values from 0.5 to 1.5
- ln_bias: float32 [1024], replicated, may hold values from -3 to 3
- w_in: bfloat16 [1024, 3072], replicated, may hold values from -0.1875 to 0.1875
- b_in: float32 [3072], replicated, may hold values from -3 to 3
- short_w: float32 [3, 3072], replicated, may hold values from -4 to 4
- short_b: float32 [3072], replicated, may hold values from -3 to 3
- w_one: float32 [33, 64], replicated, may hold values from -1 to 1
- b_one: float32 [64], replicated, may hold values from -3.140625 to 3.140625
- w_two: float32 [64, 64], replicated, may hold values from -0.75 to 0.75
- b_two: float32 [64], replicated, may hold values from -3 to 3
- w_three: float32 [64, 1024], replicated, may hold values from -0.046875 to 0.046875
- decay_rates: float32 [1024], replicated, may hold values from 0.5 to 200
- filt_bias: float32 [1024], replicated, may hold values from -4 to 4
- w_out: bfloat16 [1024, 1024], replicated, may hold values from -0.1875 to 0.1875
- b_out: float32 [1024], replicated, may hold values from -3 to 3
Outputs:
- block_out: bfloat16 [8, 1024, 1024], P('batch', 'seq')
- grad_tokens: float32 [8, 1024, 1024], P('batch', 'seq')
- grad_ln_gain: float32 [1024], P(('seq', 'batch'))
- grad_ln_bias: float32 [1024], P(('seq', 'batch'))
- grad_w_in: float32 [1024, 3072], P(('seq', 'batch'))
- grad_b_in: float32 [3072], P(('seq', 'batch'))
- grad_short_w: float32 [3, 3072], P(None, ('seq', 'batch'))
- grad_short_b: float32 [3072], P(('seq', 'batch'))
- grad_w_one: float32 [33, 64], replicated
- grad_b_one: float32 [64], replicated
- grad_w_two: float32 [64, 64], replicated
- grad_b_two: float32 [64], replicated
- grad_w_three: float32 [64, 1024], P(None, ('seq', 'batch'))
- grad_filt_bias: float32 [1024], P(('seq', 'batch'))
- grad_w_out: float32 [1024, 1024], P(('seq', 'batch'))
- grad_b_out: float32 [1024], P(('seq', 'batch'))
All inputs are finite; a program needn't handle non-finite values.
Results may differ from a plain program's by a relative error of at most 0.024.
Values may be sent and summed in bfloat16 or wider, within the bound.
A program may use at most 128 MiB of HBM per device.

v0:
```python
import jax
import jax.numpy as jnp
from jax import lax
from jax.sharding import PartitionSpec as P

highest = lax.Precision.HIGHEST
epsilon = 1e-05


def shifted(value, axis, steps):
    count = lax.axis_size(axis)
    first, last = (max(0, -steps), min(count, count - steps))
    return lax.ppermute(value, axis, [(source, source + steps) for source in range(first, last)])


def position_features(length, features):
    step_axis = jnp.arange(length).astype(jnp.float32)
    band_count = (features - 1) // 2
    band_rates = 0.0001 + jnp.arange(band_count).astype(jnp.float32) * (band_count - 1 - 0.0001) / (
        band_count - 1
    )
    phases = 2.0 * jnp.pi / length * step_axis[:, None] * band_rates[None, :]
    return jnp.concatenate(
        [(step_axis / length)[:, None], jnp.cos(phases), -jnp.sin(phases)], axis=1
    )


def filter_shape(positions, w_one, b_one, w_two, b_two, w_three, decay_rates):
    first_layer = jnp.sin(jnp.dot(positions, w_one, precision=highest) + b_one)
    second_layer = jnp.sin(jnp.dot(first_layer, w_two, precision=highest) + b_two)
    shaped = jnp.dot(second_layer, w_three, precision=highest)
    length = positions.shape[0]
    fraction = jnp.arange(length).astype(jnp.float32) / length
    return shaped * jnp.exp(-fraction[:, None] * decay_rates[None, :])


def lag_selector(rows, cols):
    width = rows + cols
    lag_index = jnp.arange(rows)[:, None] - jnp.arange(cols)[None, :] + cols
    return (jnp.arange(width)[:, None] == lag_index.reshape(1, rows * cols)).astype(jnp.bfloat16)


def lag_tile(kernel_t, base, rows, cols):
    width = rows + cols
    kernel_pad = jnp.pad(kernel_t, ((0, 0), (width, width)))
    window = lax.dynamic_slice_in_dim(kernel_pad, base - cols + width, width, 1)
    tiles = jnp.dot(window, lag_selector(rows, cols), preferred_element_type=jnp.float32)
    return tiles.astype(jnp.bfloat16).reshape(kernel_t.shape[0], rows, cols)


def local(
    tokens,
    cotangent,
    ln_gain,
    ln_bias,
    w_in,
    b_in,
    short_w,
    short_b,
    w_one,
    b_one,
    w_two,
    b_two,
    w_three,
    decay_rates,
    filt_bias,
    w_out,
    b_out,
):
    seq_count, block_len, model_width = tokens.shape
    seq_devices = lax.axis_size("seq")
    batch_devices = lax.axis_size("batch")
    length = block_len * seq_devices
    channels = model_width // batch_devices
    col_start = lax.axis_index("batch") * channels
    my_start = lax.axis_index("seq") * block_len
    inputs = tokens.astype(jnp.float32)
    average = jnp.mean(inputs, axis=-1, keepdims=True)
    centered = inputs - average
    inv_std = lax.rsqrt(jnp.mean(centered * centered, axis=-1, keepdims=True) + epsilon)
    whitened = centered * inv_std
    normed = (whitened * ln_gain + ln_bias).astype(jnp.bfloat16)
    mixed = jnp.einsum("btd,de->bte", normed, w_in, preferred_element_type=jnp.float32) + b_in
    prev_rows = shifted(mixed[:, block_len - 2 :], "seq", 1)
    padded = jnp.concatenate([prev_rows, mixed], axis=1)
    delay_one = padded[:, 1:-1]
    delay_two = padded[:, :-2]
    short_out = short_w[0] * mixed + short_w[1] * delay_one + short_w[2] * delay_two + short_b
    outer_gate = short_out[..., :model_width]
    inner_gate = short_out[..., model_width : 2 * model_width]
    values = short_out[..., 2 * model_width :]
    gated = (values * inner_gate).astype(jnp.bfloat16)
    gated_ex = lax.all_to_all(gated, "batch", split_axis=2, concat_axis=0, tiled=True)
    gated_ch = jnp.transpose(gated_ex, (2, 0, 1))
    positions = position_features(length, w_one.shape[0])
    w_three_part = lax.dynamic_slice_in_dim(w_three, col_start, channels, 1)
    decay_part = lax.dynamic_slice_in_dim(decay_rates, col_start, channels, 0)
    bias_part = lax.dynamic_slice_in_dim(filt_bias, col_start, channels, 0)[:, None, None]

    def kernel_of(first_w, first_b, second_w, second_b, third_w):
        return filter_shape(positions, first_w, first_b, second_w, second_b, third_w, decay_part)

    kernel_full, kernel_pull = jax.vjp(kernel_of, w_one, b_one, w_two, b_two, w_three_part)
    kernel_t = jnp.transpose(kernel_full).astype(jnp.bfloat16)

    def add_forward(running, portion, offset):
        amount = portion.shape[2]
        toeplitz = lag_tile(kernel_t, my_start - offset, block_len, amount)
        return running + jnp.einsum(
            "cts,cbs->cbt", toeplitz, portion, preferred_element_type=jnp.float32
        )

    def causal_forward(running, portion, offset):
        useful = (offset >= 0) & (offset <= my_start + block_len - 1)
        return lax.cond(useful, lambda: add_forward(running, portion, offset), lambda: running)

    zero_acc = jnp.zeros(gated_ch.shape, jnp.float32)

    def relay_turn(relay_step, state):
        running, current = state
        running = causal_forward(running, current, my_start - relay_step * block_len)
        current = shifted(current, "seq", 1)
        return (running, current)

    running, current = lax.fori_loop(0, seq_devices - 1, relay_turn, (zero_acc, gated_ch))
    long_out = causal_forward(running, current, my_start - (seq_devices - 1) * block_len)
    gated_float = gated_ch.astype(jnp.float32)
    summed_ch = (long_out + bias_part * gated_float).astype(jnp.bfloat16)
    summed = lax.all_to_all(
        jnp.transpose(summed_ch, (1, 2, 0)), "batch", split_axis=0, concat_axis=2, tiled=True
    ).astype(jnp.float32)
    product = (summed * outer_gate).astype(jnp.bfloat16)
    result = jnp.einsum("btd,de->bte", product, w_out, preferred_element_type=jnp.float32) + b_out
    block_out = (inputs + result).astype(jnp.bfloat16)
    grad_out = cotangent.astype(jnp.float32)
    g_w_out = jnp.einsum("btd,bte->de", product, cotangent, preferred_element_type=jnp.float32)
    g_b_out = jnp.sum(grad_out, axis=(0, 1))
    d_product = jnp.einsum(
        "bte,de->btd", cotangent, w_out, preferred_element_type=jnp.float32
    ).astype(jnp.bfloat16)
    d_prod_f = d_product.astype(jnp.float32)
    d_summed = (d_prod_f * outer_gate).astype(jnp.bfloat16)
    d_outer = d_prod_f * summed
    d_ex = lax.all_to_all(d_summed, "batch", split_axis=2, concat_axis=0, tiled=True)
    d_ch = jnp.transpose(d_ex, (2, 0, 1))

    def add_backward(state, portion, offset):
        grad_in, grad_taps = state
        amount = portion.shape[2]
        base = offset - my_start
        toeplitz = lag_tile(kernel_t, base, amount, block_len)
        grad_in = grad_in + jnp.einsum(
            "cts,cbt->cbs", toeplitz, portion, preferred_element_type=jnp.float32
        )
        cross = jnp.einsum("cbt,cbs->cts", portion, gated_ch, preferred_element_type=jnp.float32)
        selector = lag_selector(amount, block_len).astype(jnp.float32)
        diagonal = lax.dot_general(
            cross.reshape(channels, amount * block_len),
            selector,
            (((1,), (1,)), ((), ())),
            precision=highest,
            preferred_element_type=jnp.float32,
        )
        width = amount + block_len
        window = lax.dynamic_slice_in_dim(grad_taps, base, width, 1)
        grad_taps = lax.dynamic_update_slice_in_dim(grad_taps, window + diagonal, base, 1)
        return (grad_in, grad_taps)

    def causal_backward(state, portion, offset):
        useful = (offset < length) & (offset + portion.shape[2] > my_start)
        return lax.cond(useful, lambda: add_backward(state, portion, offset), lambda: state)

    zero_back = (
        jnp.zeros(gated_ch.shape, jnp.float32),
        jnp.zeros((channels, length + 2 * block_len), jnp.float32),
    )

    def relay_back(relay_step, state):
        inner, current = state
        inner = causal_backward(inner, current, my_start + relay_step * block_len)
        current = shifted(current, "seq", -1)
        return (inner, current)

    inner, current = lax.fori_loop(0, seq_devices - 1, relay_back, (zero_back, d_ch))
    grad_in, grad_taps = causal_backward(inner, current, my_start + (seq_devices - 1) * block_len)
    d_ch_float = d_ch.astype(jnp.float32)
    grad_in = grad_in + bias_part * d_ch_float
    g_bias_part = jnp.sum(d_ch_float * gated_float, axis=(1, 2))
    g_w_one, g_b_one, g_w_two, g_b_two, g_w_three_part = kernel_pull(
        jnp.transpose(grad_taps[:, block_len : block_len + length])
    )
    d_gated_ch = jnp.transpose(grad_in.astype(jnp.bfloat16), (1, 2, 0))
    d_gated = lax.all_to_all(d_gated_ch, "batch", split_axis=0, concat_axis=2, tiled=True).astype(
        jnp.float32
    )
    d_short = jnp.concatenate([d_outer, d_gated * values, d_gated * inner_gate], axis=-1)
    g_short_w = jnp.stack(
        [
            jnp.sum(d_short * mixed, axis=(0, 1)),
            jnp.sum(d_short * delay_one, axis=(0, 1)),
            jnp.sum(d_short * delay_two, axis=(0, 1)),
        ]
    )
    g_short_b = jnp.sum(d_short, axis=(0, 1))
    next_rows = shifted(d_short[:, :2], "seq", -1)
    extended = jnp.concatenate([d_short, next_rows], axis=1)
    d_mixed = (
        short_w[0] * extended[:, :block_len]
        + short_w[1] * extended[:, 1 : block_len + 1]
        + short_w[2] * extended[:, 2:]
    ).astype(jnp.bfloat16)
    g_w_in = jnp.einsum("btd,bte->de", normed, d_mixed, preferred_element_type=jnp.float32)
    g_b_in = jnp.sum(d_mixed.astype(jnp.float32), axis=(0, 1))
    d_normed = jnp.einsum("bte,de->btd", d_mixed, w_in, preferred_element_type=jnp.float32)
    g_ln_gain = jnp.sum(d_normed * whitened, axis=(0, 1))
    g_ln_bias = jnp.sum(d_normed, axis=(0, 1))
    d_white = d_normed * ln_gain
    grad_tokens = grad_out + inv_std * (
        d_white
        - jnp.mean(d_white, axis=-1, keepdims=True)
        - whitened * jnp.mean(d_white * whitened, axis=-1, keepdims=True)
    )
    g_w_three = lax.dynamic_update_slice_in_dim(
        jnp.zeros(w_three.shape, jnp.float32), g_w_three_part, col_start, 1
    )
    g_filt_bias = lax.dynamic_update_slice_in_dim(
        jnp.zeros(filt_bias.shape, jnp.float32), g_bias_part, col_start, 0
    )
    shared = (
        lax.psum_scatter(g_ln_gain, ("seq", "batch"), scatter_dimension=0, tiled=True),
        lax.psum_scatter(g_ln_bias, ("seq", "batch"), scatter_dimension=0, tiled=True),
        lax.psum_scatter(g_w_in, ("seq", "batch"), scatter_dimension=0, tiled=True),
        lax.psum_scatter(g_b_in, ("seq", "batch"), scatter_dimension=0, tiled=True),
        lax.psum_scatter(g_short_w, ("seq", "batch"), scatter_dimension=1, tiled=True),
        lax.psum_scatter(g_short_b, ("seq", "batch"), scatter_dimension=0, tiled=True),
        lax.psum_scatter(g_w_three, ("seq", "batch"), scatter_dimension=1, tiled=True),
        lax.psum_scatter(g_filt_bias, ("seq", "batch"), scatter_dimension=0, tiled=True),
        lax.psum_scatter(g_w_out, ("seq", "batch"), scatter_dimension=0, tiled=True),
        lax.psum_scatter(g_b_out, ("seq", "batch"), scatter_dimension=0, tiled=True),
    )
    net_grads = lax.psum((g_w_one, g_b_one, g_w_two, g_b_two), ("seq", "batch"))
    return (
        block_out,
        grad_tokens,
        shared[0],
        shared[1],
        shared[2],
        shared[3],
        shared[4],
        shared[5],
        net_grads[0],
        net_grads[1],
        net_grads[2],
        net_grads[3],
        shared[6],
        shared[7],
        shared[8],
        shared[9],
    )


def solution(mesh):
    in_specs = (
        P("batch", "seq", None),
        P("batch", "seq", None),
        P(),
        P(),
        P(),
        P(),
        P(),
        P(),
        P(),
        P(),
        P(),
        P(),
        P(),
        P(),
        P(),
        P(),
        P(),
    )
    out_specs = (
        P("batch", "seq", None),
        P("batch", "seq", None),
        P(("seq", "batch")),
        P(("seq", "batch")),
        P(("seq", "batch"), None),
        P(("seq", "batch")),
        P(None, ("seq", "batch")),
        P(("seq", "batch")),
        P(),
        P(),
        P(),
        P(),
        P(None, ("seq", "batch")),
        P(("seq", "batch")),
        P(("seq", "batch"), None),
        P(("seq", "batch")),
    )
    return jax.shard_map(local, mesh=mesh, in_specs=in_specs, out_specs=out_specs, check_vma=False)
```

profile of v0, /device:TPU:0, one launch (start us, length us, event | category | flops | bytes accessed | tf_op | source)
XLA Modules:
  0.0 1344.2 jit_solution(7296558151046338768)
XLA Ops:
  9.9 4.9 fusion.40
  23.9 4.5 all-to-all-start
  32.4 4.6 all-to-all-done
  55.7 389.0 %while.41 = (s32[]{:T(128)}, f32[256,8,128]{2,1,0:T(8,128)}, f32[256,1280]{1,0:T(8,128)}, bf16[256,8,128]{2,1,0:T(8,128)(2,1)}, s32[]{:T(128)}, /*index=5*/bf16[...) while((s32[]{:T(128)}, f32[256,8,128]{2,1,0:T(8,128)}, ...), condition=%wide.region_11.0_spmd, body=%wide.region_8.11_spmd.sunk | while | flops 15179546624 | bytes 75694472 | solution.py:184
  59.3 52.3 %conditional.9 = ((f32[256,8,128]{2,1,0:T(8,128)}, f32[256,1280]{1,0:T(8,128)})) conditional(s32[]{:T(128)} %convert_element_type.286, (f32[256,8,128]{2,1,0:T(8,128)}, f32[256,1280]{1,0:T(8,128)}) %tuple.134, (bf16[256,1024]{1,0:T(8,128)(2,1)S(1)}, s32[]{:T(128)}, s32[]{:T(128)}, bf16[256,8,128]{2,1,0:T(8,128)(2,1)}, f32[256,8,128]{2,1,0:T(8,128)}, ...), branch_computations={%region_9.9_spmd, %region_10.10_spmd} | conditional | flops 15179546624 | bytes 72548472 | solution.py:171
  62.8 23.1 %fusion.17 = f32[256,256]{1,0:T(8,128)S(1)} fusion(s32[16384]{0:T(1024)S(1)} %add_bitcast_fusion.2, f32[32,8,128,128]{3,2,1,0:T(8,128)S(1)} %bitcast.143, f32[256,1280]{1,0:T(8,128)} %get-tuple-element.337, s32[]{:T(128)S(6)} %select_n.15), kind=kOutput, calls=%fused_computation.30 | convolution fusion | flops 12889161728 | bytes 17367044 | tf_op jit(solution)/shard_map/while/body/eval_jaxpr/cond/branch_1_fun/dot_general | solution.py:157
  87.7 7.4 fusion.15
  95.1 9.3 copy.66
  104.4 7.2 fusion.16
  114.8 52.3 %conditional.9 = ((f32[256,8,128]{2,1,0:T(8,128)}, f32[256,1280]{1,0:T(8,128)})) conditional(s32[]{:T(128)} %convert_element_type.286, (f32[256,8,128]{2,1,0:T(8,128)}, f32[256,1280]{1,0:T(8,128)}) %tuple.134, (bf16[256,1024]{1,0:T(8,128)(2,1)S(1)}, s32[]{:T(128)}, s32[]{:T(128)}, bf16[256,8,128]{2,1,0:T(8,128)(2,1)}, f32[256,8,128]{2,1,0:T(8,128)}, ...), branch_computations={%region_9.9_spmd, %region_10.10_spmd} | conditional | flops 15179546624 | bytes 72548472 | solution.py:171
  118.3 23.1 %fusion.17 = f32[256,256]{1,0:T(8,128)S(1)} fusion(s32[16384]{0:T(1024)S(1)} %add_bitcast_fusion.2, f32[32,8,128,128]{3,2,1,0:T(8,128)S(1)} %bitcast.143, f32[256,1280]{1,0:T(8,128)} %get-tuple-element.337, s32[]{:T(128)S(6)} %select_n.15), kind=kOutput, calls=%fused_computation.30 | convolution fusion | flops 12889161728 | bytes 17367044 | tf_op jit(solution)/shard_map/while/body/eval_jaxpr/cond/branch_1_fun/dot_general | solution.py:157
  143.2 7.4 fusion.15
  150.6 9.3 copy.66
  159.9 7.2 fusion.16
  170.3 52.3 %conditional.9 = ((f32[256,8,128]{2,1,0:T(8,128)}, f32[256,1280]{1,0:T(8,128)})) conditional(s32[]{:T(128)} %convert_element_type.286, (f32[256,8,128]{2,1,0:T(8,128)}, f32[256,1280]{1,0:T(8,128)}) %tuple.134, (bf16[256,1024]{1,0:T(8,128)(2,1)S(1)}, s32[]{:T(128)}, s32[]{:T(128)}, bf16[256,8,128]{2,1,0:T(8,128)(2,1)}, f32[256,8,128]{2,1,0:T(8,128)}, ...), branch_computations={%region_9.9_spmd, %region_10.10_spmd} | conditional | flops 15179546624 | bytes 72548472 | solution.py:171
  173.8 23.1 %fusion.17 = f32[256,256]{1,0:T(8,128)S(1)} fusion(s32[16384]{0:T(1024)S(1)} %add_bitcast_fusion.2, f32[32,8,128,128]{3,2,1,0:T(8,128)S(1)} %bitcast.143, f32[256,1280]{1,0:T(8,128)} %get-tuple-element.337, s32[]{:T(128)S(6)} %select_n.15), kind=kOutput, calls=%fused_computation.30 | convolution fusion | flops 12889161728 | bytes 17367044 | tf_op jit(solution)/shard_map/while/body/eval_jaxpr/cond/branch_1_fun/dot_general | solution.py:157
  198.7 7.4 fusion.15
  206.2 9.3 copy.66
  215.4 7.2 fusion.16
  225.8 52.3 %conditional.9 = ((f32[256,8,128]{2,1,0:T(8,128)}, f32[256,1280]{1,0:T(8,128)})) conditional(s32[]{:T(128)} %convert_element_type.286, (f32[256,8,128]{2,1,0:T(8,128)}, f32[256,1280]{1,0:T(8,128)}) %tuple.134, (bf16[256,1024]{1,0:T(8,128)(2,1)S(1)}, s32[]{:T(128)}, s32[]{:T(128)}, bf16[256,8,128]{2,1,0:T(8,128)(2,1)}, f32[256,8,128]{2,1,0:T(8,128)}, ...), branch_computations={%region_9.9_spmd, %region_10.10_spmd} | conditional | flops 15179546624 | bytes 72548472 | solution.py:171
  229.3 23.1 %fusion.17 = f32[256,256]{1,0:T(8,128)S(1)} fusion(s32[16384]{0:T(1024)S(1)} %add_bitcast_fusion.2, f32[32,8,128,128]{3,2,1,0:T(8,128)S(1)} %bitcast.143, f32[256,1280]{1,0:T(8,128)} %get-tuple-element.337, s32[]{:T(128)S(6)} %select_n.15), kind=kOutput, calls=%fused_computation.30 | convolution fusion | flops 12889161728 | bytes 17367044 | tf_op jit(solution)/shard_map/while/body/eval_jaxpr/cond/branch_1_fun/dot_general | solution.py:157
  254.2 7.4 fusion.15
  261.6 9.3 copy.66
  270.9 7.2 fusion.16
  281.3 52.3 %conditional.9 = ((f32[256,8,128]{2,1,0:T(8,128)}, f32[256,1280]{1,0:T(8,128)})) conditional(s32[]{:T(128)} %convert_element_type.286, (f32[256,8,128]{2,1,0:T(8,128)}, f32[256,1280]{1,0:T(8,128)}) %tuple.134, (bf16[256,1024]{1,0:T(8,128)(2,1)S(1)}, s32[]{:T(128)}, s32[]{:T(128)}, bf16[256,8,128]{2,1,0:T(8,128)(2,1)}, f32[256,8,128]{2,1,0:T(8,128)}, ...), branch_computations={%region_9.9_spmd, %region_10.10_spmd} | conditional | flops 15179546624 | bytes 72548472 | solution.py:171
  284.8 23.1 %fusion.17 = f32[256,256]{1,0:T(8,128)S(1)} fusion(s32[16384]{0:T(1024)S(1)} %add_bitcast_fusion.2, f32[32,8,128,128]{3,2,1,0:T(8,128)S(1)} %bitcast.143, f32[256,1280]{1,0:T(8,128)} %get-tuple-element.337, s32[]{:T(128)S(6)} %select_n.15), kind=kOutput, calls=%fused_computation.30 | convolution fusion | flops 12889161728 | bytes 17367044 | tf_op jit(solution)/shard_map/while/body/eval_jaxpr/cond/branch_1_fun/dot_general | solution.py:157
  309.7 7.4 fusion.15
  317.1 9.3 copy.66
  326.4 7.2 fusion.16
  336.8 52.3 %conditional.9 = ((f32[256,8,128]{2,1,0:T(8,128)}, f32[256,1280]{1,0:T(8,128)})) conditional(s32[]{:T(128)} %convert_element_type.286, (f32[256,8,128]{2,1,0:T(8,128)}, f32[256,1280]{1,0:T(8,128)}) %tuple.134, (bf16[256,1024]{1,0:T(8,128)(2,1)S(1)}, s32[]{:T(128)}, s32[]{:T(128)}, bf16[256,8,128]{2,1,0:T(8,128)(2,1)}, f32[256,8,128]{2,1,0:T(8,128)}, ...), branch_computations={%region_9.9_spmd, %region_10.10_spmd} | conditional | flops 15179546624 | bytes 72548472 | solution.py:171
  340.2 23.1 %fusion.17 = f32[256,256]{1,0:T(8,128)S(1)} fusion(s32[16384]{0:T(1024)S(1)} %add_bitcast_fusion.2, f32[32,8,128,128]{3,2,1,0:T(8,128)S(1)} %bitcast.143, f32[256,1280]{1,0:T(8,128)} %get-tuple-element.337, s32[]{:T(128)S(6)} %select_n.15), kind=kOutput, calls=%fused_computation.30 | convolution fusion | flops 12889161728 | bytes 17367044 | tf_op jit(solution)/shard_map/while/body/eval_jaxpr/cond/branch_1_fun/dot_general | solution.py:157
  365.2 7.4 fusion.15
  372.6 9.3 copy.66
  381.9 7.2 fusion.16
  392.2 52.3 %conditional.9 = ((f32[256,8,128]{2,1,0:T(8,128)}, f32[256,1280]{1,0:T(8,128)})) conditional(s32[]{:T(128)} %convert_element_type.286, (f32[256,8,128]{2,1,0:T(8,128)}, f32[256,1280]{1,0:T(8,128)}) %tuple.134, (bf16[256,1024]{1,0:T(8,128)(2,1)S(1)}, s32[]{:T(128)}, s32[]{:T(128)}, bf16[256,8,128]{2,1,0:T(8,128)(2,1)}, f32[256,8,128]{2,1,0:T(8,128)}, ...), branch_computations={%region_9.9_spmd, %region_10.10_spmd} | conditional | flops 15179546624 | bytes 72548472 | solution.py:171
  395.7 23.1 %fusion.17 = f32[256,256]{1,0:T(8,128)S(1)} fusion(s32[16384]{0:T(1024)S(1)} %add_bitcast_fusion.2, f32[32,8,128,128]{3,2,1,0:T(8,128)S(1)} %bitcast.143, f32[256,1280]{1,0:T(8,128)} %get-tuple-element.337, s32[]{:T(128)S(6)} %select_n.15), kind=kOutput, calls=%fused_computation.30 | convolution fusion | flops 12889161728 | bytes 17367044 | tf_op jit(solution)/shard_map/while/body/eval_jaxpr/cond/branch_1_fun/dot_general | solution.py:157
  420.7 7.4 fusion.15
  428.1 9.3 copy.66
  437.4 7.2 fusion.16
  445.8 110.5 %while.40 = (s32[]{:T(128)}, f32[256,8,128]{2,1,0:T(8,128)}, bf16[256,8,128]{2,1,0:T(8,128)(2,1)S(1)}, s32[]{:T(128)}, s32[]{:T(128)}, /*index=5*/bf16[256,1024]{1,0:T(8,128)(2,1)S(1)}, s32[]{:T(128)}, s32[]{:T(128)}, s32[]{:T(128)}) while((s32[]{:T(128)}, f32[256,8,128]{2,1,0:T(8,128)}, bf16[256,8,128]{2,1,0:T(8,128)(2,1)S(1)}, s32[]{:T(128)}, ...), condition=%wide.region_5.6_spmd, body=%wide.region_2.5_spmd.sunk | while | flops 2223276032 | bytes 39977256 | solution.py:125
  446.6 6.9 collective-permute-start
  453.5 25.9 %conditional.8 = (f32[256,8,128]{2,1,0:T(8,128)}) conditional(s32[]{:T(128)} %convert_element_type.285, f32[256,8,128]{2,1,0:T(8,128)} %get-tuple-element.584, (bf16[256,1024]{1,0:T(8,128)(2,1)S(1)}, s32[]{:T(128)}, s32[]{:T(128)}, bf16[256,8,128]{2,1,0:T(8,128)(2,1)}, f32[256,8,128]{2,1,0:T(8,128)}) %tuple.132), branch_computations={%region_3.0_spmd, %region_4.4_spmd} | conditional | flops 2223276032 | bytes 36831304 | solution.py:115
  453.5 7.4 fusion.1
  461.0 9.2 copy.64
  470.2 9.2 fusion.2
  484.7 26.2 %collective-permute-start = (bf16[256,8,128]{2,1,0:T(8,128)(2,1)}, bf16[256,8,128]{2,1,0:T(8,128)(2,1)S(1)}, u32[]{:S(2)}, u32[]{:S(2)}) collective-permute-start(bf16[256,8,128]{2,1,0:T(8,128)(2,1)} %copy.97), channel_id=1, source_target_pairs={{0,4},{4,8},{8,12},{12,16},{16,20},{20,24},{24,28},{1,5},{5,9},{9,... | collective-permute-start | bytes 1572872 | tf_op jit(solution)/shard_map/while/body/eval_jaxpr/ppermute | solution.py:13
  513.4 6.6 collective-permute-start
  522.5 9.0 collective-permute-start
  534.1 9.0 collective-permute-start
  545.6 9.0 collective-permute-start
  558.9 53.0 %conditional.5 = (f32[256,1280]{1,0:T(8,128)}, f32[256,8,128]{2,0,1:T(8,128)}) conditional(s32[]{:T(128)} %convert_element_type.172, (f32[256,8,128]{2,1,0:T(8,128)}, f32[256,1280]{1,0:T(8,128)}) %tuple.78, (bf16[256,1024]{1,0:T(8,128)(2,1)S(1)}, s32[]{:T(128)}, s32[]{:T(128)}, bf16[256,8,128]{2,1,0:T(8,128)(2,1)}, f32[256,8,128]{2,1,0:T(8,128)}, ...), branch_computations={%region_12.13_spmd, %region_13.14_spmd} | conditional | flops 15179546624 | bytes 74645616 | solution.py:171
  562.5 23.1 %fusion.29 = f32[256,256]{1,0:T(8,128)S(1)} fusion(s32[16384]{0:T(1024)S(1)} %add_bitcast_fusion.3, f32[32,8,128,128]{3,2,1,0:T(8,128)S(1)} %bitcast.146, f32[256,1280]{1,0:T(8,128)} %get-tuple-element.354, s32[]{:T(128)S(6)} %select_n.20), kind=kOutput, calls=%fused_computation.45 | convolution fusion | flops 12889161728 | bytes 17367044 | tf_op jit(solution)/shard_map/cond/branch_1_fun/dot_general | solution.py:157
  587.8 7.5 fusion.27
  595.3 9.2 copy.69
  604.5 6.0 fusion.28
  612.0 4.2 fusion.81
  616.2 4.2 all-to-all-start.1
  646.7 4.4 slice_multiply_fusion.3
  677.5 8.0 convolution_bitcast_fusion.4
  688.1 104.4 %all-reduce.13.cloned.1.call-done = (f32[1024]{0:T(1024)}, f32[1024]{0:T(1024)}, f32[3072]{0:T(1024)}, f32[3072]{0:T(1024)}, f32[33,64]{1,0:T(8,128)}, /*index=5...) async-done(((f32[1024]{0:T(1024)}, f32[1024]{0:T(1024)}, f32[3072]{0:T(1024)}, f32[3072]{0:T(1024)}, f32[33,64]{1,0:T(8,128)}, ...) | async-done | bytes 66320
  800.1 96.5 %reduce-scatter.13.cloned.1.call-done = f32[96,3]{1,0:T(8,128)} async-done(((f32[3072,3]{1,0:T(8,128)}), f32[96,3]{1,0:T(8,128)}) %reduce-scatter.13.cloned.1.call-update) | async-done | bytes 1168
  898.1 134.4 %reduce-scatter.9.cloned.1.call-done = f32[64,32]{0,1:T(8,128)} async-done(((f32[64,1024]{0,1:T(8,128)}), f32[64,32]{0,1:T(8,128)}) %reduce-scatter.9.cloned.1.call-update) | async-done | bytes 8208 | tf_op jit(solution)/shard_map/reduce_scatter | solution.py:236
  1032.5 140.3 %reduce-scatter.11.cloned.1.call-done = f32[32,1024]{1,0:T(8,128)} async-done(((f32[1024,1024]{1,0:T(8,128)}), f32[32,1024]{1,0:T(8,128)}) %reduce-scatter.11.cloned.1.call-update) | async-done | bytes 131088 | tf_op jit(solution)/shard_map/reduce_scatter | solution.py:238
  1172.8 159.6 %reduce-scatter.7.cloned.1.call-done = f32[32,3072]{1,0:T(8,128)} async-done(((f32[1024,3072]{1,0:T(8,128)}), f32[32,3072]{1,0:T(8,128)}) %reduce-scatter.7.cloned.1.call-update) | async-done | bytes 393232 | tf_op jit(solution)/shard_map/reduce_scatter | solution.py:232
  (269 shorter events, 192.0 us)
Async XLA Ops:
  7.2 13.9 %copy-start = (bf16[1024,1024]{1,0:T(8,128)(2,1)S(1)}, bf16[1024,1024]{1,0:T(8,128)(2,1)}, u32[]{:S(2)}) copy-start(bf16[1024,1024]{1,0:T(8,128)(2,1)} %param.44) | copy-start | bytes 6291460
  8.5 6.3 copy-start.44
  9.9 4.9 copy-start.47
  9.9 7.5 copy-start.43
  9.9 8.3 copy-start.50
  14.8 7.9 copy-start.9
  14.8 6.2 copy-start.15
  14.9 3.4 collective-permute-start.2
  17.4 5.3 copy-start.31
  17.4 5.3 copy-start.33
  17.5 5.3 copy-start.35
  18.2 4.5 copy-start.27
  21.1 8.3 copy-start.46
  21.1 8.3 copy-start.54
  22.7 18.4 %copy-start.29 = (f32[64,64]{1,0:T(8,128)S(1)}, f32[64,64]{1,0:T(8,128)}, u32[]{:S(2)}) copy-start(f32[64,64]{1,0:T(8,128)} %param.39) | copy-start | bytes 49156
  22.8 18.4 %copy-start.55 = (f32[64]{0:T(128)S(1)}, f32[64]{0:T(128)}, u32[]{:S(2)}) copy-start(f32[64]{0:T(128)} %param.40) | copy-start | bytes 772
  23.9 13.1 all-to-all-start
  31.3 13.8 %copy-start.20 = (f32[1024,64]{0,1:T(8,128)}, f32[1024,64]{0,1:T(8,128)S(1)}, u32[]{:S(2)}) copy-start(f32[1024,64]{0,1:T(8,128)S(1)} %get-tuple-element.475) | copy-start | bytes 786436
  37.0 13.4 all-to-all-start.2
  43.0 4.1 copy-start.22
  43.8 3.3 copy-start.51
  58.0 53.6 %collective-permute-start.1 = (bf16[256,8,128]{2,1,0:T(8,128)(2,1)}, bf16[256,8,128]{2,1,0:T(8,128)(2,1)}, u32[]{:S(2)}, u32[]{:S(2)}) collective-permute-start(bf16[256,8,128]{2,1,0:T(8,128)(2,1)} %copy.110), channel_id=1, source_target_pairs={{4,0},{8,4},{12,8},{16,12},{20,16},{24,20},{28,24},{5,1},{9,5},{13... | collective-permute-start | bytes 1572872 | tf_op jit(solution)/shard_map/while/body/eval_jaxpr/ppermute | solution.py:13
  113.5 53.6 %collective-permute-start.1 = (bf16[256,8,128]{2,1,0:T(8,128)(2,1)}, bf16[256,8,128]{2,1,0:T(8,128)(2,1)}, u32[]{:S(2)}, u32[]{:S(2)}) collective-permute-start(bf16[256,8,128]{2,1,0:T(8,128)(2,1)} %copy.110), channel_id=1, source_target_pairs={{4,0},{8,4},{12,8},{16,12},{20,16},{24,20},{28,24},{5,1},{9,5},{13... | collective-permute-start | bytes 1572872 | tf_op jit(solution)/shard_map/while/body/eval_jaxpr/ppermute | solution.py:13
  169.0 53.6 %collective-permute-start.1 = (bf16[256,8,128]{2,1,0:T(8,128)(2,1)}, bf16[256,8,128]{2,1,0:T(8,128)(2,1)}, u32[]{:S(2)}, u32[]{:S(2)}) collective-permute-start(bf16[256,8,128]{2,1,0:T(8,128)(2,1)} %copy.110), channel_id=1, source_target_pairs={{4,0},{8,4},{12,8},{16,12},{20,16},{24,20},{28,24},{5,1},{9,5},{13... | collective-permute-start | bytes 1572872 | tf_op jit(solution)/shard_map/while/body/eval_jaxpr/ppermute | solution.py:13
  224.5 53.6 %collective-permute-start.1 = (bf16[256,8,128]{2,1,0:T(8,128)(2,1)}, bf16[256,8,128]{2,1,0:T(8,128)(2,1)}, u32[]{:S(2)}, u32[]{:S(2)}) collective-permute-start(bf16[256,8,128]{2,1,0:T(8,128)(2,1)} %copy.110), channel_id=1, source_target_pairs={{4,0},{8,4},{12,8},{16,12},{20,16},{24,20},{28,24},{5,1},{9,5},{13... | collective-permute-start | bytes 1572872 | tf_op jit(solution)/shard_map/while/body/eval_jaxpr/ppermute | solution.py:13
  280.0 53.6 %collective-permute-start.1 = (bf16[256,8,128]{2,1,0:T(8,128)(2,1)}, bf16[256,8,128]{2,1,0:T(8,128)(2,1)}, u32[]{:S(2)}, u32[]{:S(2)}) collective-permute-start(bf16[256,8,128]{2,1,0:T(8,128)(2,1)} %copy.110), channel_id=1, source_target_pairs={{4,0},{8,4},{12,8},{16,12},{20,16},{24,20},{28,24},{5,1},{9,5},{13... | collective-permute-start | bytes 1572872 | tf_op jit(solution)/shard_map/while/body/eval_jaxpr/ppermute | solution.py:13
  335.5 53.6 %collective-permute-start.1 = (bf16[256,8,128]{2,1,0:T(8,128)(2,1)}, bf16[256,8,128]{2,1,0:T(8,128)(2,1)}, u32[]{:S(2)}, u32[]{:S(2)}) collective-permute-start(bf16[256,8,128]{2,1,0:T(8,128)(2,1)} %copy.110), channel_id=1, source_target_pairs={{4,0},{8,4},{12,8},{16,12},{20,16},{24,20},{28,24},{5,1},{9,5},{13... | collective-permute-start | bytes 1572872 | tf_op jit(solution)/shard_map/while/body/eval_jaxpr/ppermute | solution.py:13
  390.9 53.6 %collective-permute-start.1 = (bf16[256,8,128]{2,1,0:T(8,128)(2,1)}, bf16[256,8,128]{2,1,0:T(8,128)(2,1)}, u32[]{:S(2)}, u32[]{:S(2)}) collective-permute-start(bf16[256,8,128]{2,1,0:T(8,128)(2,1)} %copy.110), channel_id=1, source_target_pairs={{4,0},{8,4},{12,8},{16,12},{20,16},{24,20},{28,24},{5,1},{9,5},{13... | collective-permute-start | bytes 1572872 | tf_op jit(solution)/shard_map/while/body/eval_jaxpr/ppermute | solution.py:13
  446.6 32.8 %collective-permute-start = (bf16[256,8,128]{2,1,0:T(8,128)(2,1)}, bf16[256,8,128]{2,1,0:T(8,128)(2,1)S(1)}, u32[]{:S(2)}, u32[]{:S(2)}) collective-permute-start(bf16[256,8,128]{2,1,0:T(8,128)(2,1)} %copy.97), channel_id=1, source_target_pairs={{0,4},{4,8},{8,12},{12,16},{16,20},{20,24},{24,28},{1,5},{5,9},{9,... | collective-permute-start | bytes 1572872 | tf_op jit(solution)/shard_map/while/body/eval_jaxpr/ppermute | solution.py:13
  480.2 3.6 collective-permute-start
  484.7 27.9 %collective-permute-start = (bf16[256,8,128]{2,1,0:T(8,128)(2,1)}, bf16[256,8,128]{2,1,0:T(8,128)(2,1)S(1)}, u32[]{:S(2)}, u32[]{:S(2)}) collective-permute-start(bf16[256,8,128]{2,1,0:T(8,128)(2,1)} %copy.97), channel_id=1, source_target_pairs={{0,4},{4,8},{8,12},{12,16},{16,20},{20,24},{24,28},{1,5},{5,9},{9,... | collective-permute-start | bytes 1572872 | tf_op jit(solution)/shard_map/while/body/eval_jaxpr/ppermute | solution.py:13
  513.4 8.3 collective-permute-start
  522.5 10.7 collective-permute-start
  534.1 10.7 collective-permute-start
  545.6 10.7 collective-permute-start
  557.9 54.0 %copy-start.53 = (f32[256]{0:T(256)S(1)}, f32[256]{0:T(256)}, u32[]{:S(2)}) copy-start(f32[256]{0:T(256)} %dynamic_slice.29) | copy-start | bytes 3076
  611.9 8.5 copy-start.1
  611.9 8.5 copy-start.40
  612.0 8.5 copy-start.52
  612.0 21.3 %copy-start.30 = (f32[64,64]{1,0:T(8,128)S(1)}, f32[64,64]{1,0:T(8,128)}, u32[]{:S(2)}) copy-start(f32[64,64]{1,0:T(8,128)} %param.39) | copy-start | bytes 49156
  616.2 10.8 all-to-all-start.1
  627.0 14.7 %all-to-all-start.3 = ((bf16[8,128,256]{1,2,0:T(8,128)(2,1)}), bf16[8,128,256]{1,2,0:T(8,128)(2,1)}, u32[]{:S(2)}, u32[]{:S(2)}) async-start(bf16[8,128,256]{1,2,0:T(8,128)(2,1)} %get-tuple-element.468), calls=%async_computation.3 | async-start | bytes 1048576 | tf_op jit(solution)/shard_map/all_to_all | solution.py:193
  631.2 161.3 %all-reduce.13.cloned.1.call-start = ((), (), s32[]{:S(2)}) async-start(), calls=%async_computation.12 | async-start | bytes 190464
  651.0 3.3 copy-start.3
  651.0 3.3 copy-start.5
  651.0 3.3 copy-start.7
  652.1 3.3 collective-permute-start.3
  654.3 3.5 copy-start.28
  654.3 3.5 copy-start.32
  654.4 3.5 copy-start.34
  654.4 3.5 copy-start.36
  655.3 6.9 copy-start.49
  655.3 2.8 copy-start.8
  655.3 3.8 copy-start.10
  655.4 6.8 slice-start
  659.1 3.1 copy-start.11
  659.1 3.1 copy-start.37
  659.1 3.1 copy-start.45
  659.1 3.1 copy-start.48
  659.1 3.1 slice-start.1
  667.0 229.6 %reduce-scatter.13.cloned.1.call-start = ((), (), s32[]{:S(2)}) async-start(), calls=%async_computation.11 | async-start | bytes 1622016
  668.8 363.7 %reduce-scatter.9.cloned.1.call-start = ((), (), s32[]{:S(2)}) async-start(), calls=%async_computation.9 | async-start | bytes 540672 | tf_op jit(solution)/shard_map/reduce_scatter | solution.py:236
  672.6 500.2 %reduce-scatter.11.cloned.1.call-start = ((), (), s32[]{:S(2)}) async-start(), calls=%async_computation.10 | async-start | bytes 4325376 | tf_op jit(solution)/shard_map/reduce_scatter | solution.py:238
  676.5 655.9 %reduce-scatter.7.cloned.1.call-start = ((), (), s32[]{:S(2)}) async-start(), calls=%async_computation.8 | async-start | bytes 12976128 | tf_op jit(solution)/shard_map/reduce_scatter | solution.py:232
  (20 other events, 35.8 us)
Sparse Core Ops, SparseCore 0:
  667.1 125.3 all-reduce.12
  798.6 98.0 reduce-scatter.12
  899.6 132.8 reduce-scatter.8
  1035.2 137.5 reduce-scatter.10
  1179.3 153.0 reduce-scatter.6
where the time goes:
time: 1360 us; the launch traced here: 1340 us
  waiting for transfers between devices  655 us (48%)
  matrix products  386 us (28%)
  local copies, waits for them, and re-layouts  167 us (12%)
  starting transfers between devices  98.7 us (7%)
  other arithmetic  20.8 us (2%)
  between operations  14.8 us (1%)
    unnamed x7, waiting for transfers between devices  201 us
    dot_general x8, matrix products, add_backward(): lax.dot_general(cross.reshape(channels, amount * block_len), selector, ((...  185 us
    reduce_scatter x1, waiting for transfers between devices, local(): lax.psum_scatter(g_w_in, ('seq', 'batch'), scatter_dimension=0, tiled=True)  160 us
    reduce_scatter x1, waiting for transfers between devices, local(): lax.psum_scatter(g_w_out, ('seq', 'batch'), scatter_dimension=0, tiled=True)  140 us
    reduce_scatter x1, waiting for transfers between devices, local(): lax.psum_scatter(g_w_three, ('seq', 'batch'), scatter_dimension=1, tiled=...  134 us
    cond x9, local copies, waits for them, and re-layouts  83.4 us
    ppermute x16, starting transfers between devices, shifted(): lax.ppermute(value, axis, [(source, source + steps) for source in range(f...  81.3 us
    dot_general x9, matrix products, lag_tile(): jnp.dot(window, lag_selector(rows, cols), preferred_element_type=jnp.floa...  66.9 us
  transfers between devices with their start and end apart: 25, of which 16 were waited for; matrix products, arithmetic and copies ran while one was open for 33% of the time, Pallas kernels for 0%

commit v1 on v0

v1 whole, which is shorter than its diff:
```python
import jax
import jax.numpy as jnp
import numpy as np
from jax import lax
from jax.sharding import PartitionSpec as P

highest = lax.Precision.HIGHEST
epsilon = 1e-05
f32, bf16 = jnp.float32, jnp.bfloat16


def dft_matrix(length):
    turns = ((2 * np.arange(length)[:, None] + 1) * np.arange(length)[None, :]) % (4 * length)
    phases = turns * (np.pi / (2 * length))
    return np.concatenate([np.cos(phases), np.sin(phases)], axis=0).astype(bf16)


def position_features(length, features):
    step_axis = np.arange(length, dtype=np.float64)
    band_count = (features - 1) // 2
    band_rates = 0.0001 + np.arange(band_count) * (band_count - 1 - 0.0001) / (band_count - 1)
    phases = 2.0 * np.pi / length * step_axis[:, None] * band_rates[None, :]
    return np.concatenate(
        [(step_axis / length)[:, None], np.cos(phases), -np.sin(phases)], axis=1
    ).astype(np.float32)


def filter_shape(positions, w_one, b_one, w_two, b_two, w_three, decay_rates):
    first_layer = jnp.sin(jnp.dot(positions, w_one, precision=highest) + b_one)
    second_layer = jnp.sin(jnp.dot(first_layer, w_two, precision=highest) + b_two)
    shaped = jnp.dot(second_layer, w_three, precision=highest)
    length = positions.shape[0]
    fraction = jnp.arange(length).astype(f32) / length
    return shaped * jnp.exp(-fraction[:, None] * decay_rates[None, :])


def shifted(value, axis, steps):
    count = lax.axis_size(axis)
    first, last = (max(0, -steps), min(count, count - steps))
    return lax.ppermute(value, axis, [(source, source + steps) for source in range(first, last)])


def reduce_scatter(value, dtype):
    out = lax.all_to_all(value.astype(dtype), "batch", split_axis=1, concat_axis=1, tiled=True)
    out = jnp.sum(out.astype(f32), axis=1)
    out = lax.all_to_all(out.astype(dtype), "seq", split_axis=0, concat_axis=0, tiled=True)
    return jnp.sum(out.astype(f32), axis=0)


def local(
    tokens,
    cotangent,
    ln_gain,
    ln_bias,
    w_in,
    b_in,
    short_w,
    short_b,
    w_one,
    b_one,
    w_two,
    b_two,
    w_three,
    decay_rates,
    filt_bias,
    w_out,
    b_out,
):
    seq_count, block_len, model_width = tokens.shape
    seq_devices = lax.axis_size("seq")
    batch_devices = lax.axis_size("batch")
    devices = seq_devices * batch_devices
    length = block_len * seq_devices
    channels = model_width // seq_devices
    col_start = lax.axis_index("seq") * channels
    inputs = tokens.astype(f32)
    average = jnp.mean(inputs, axis=-1, keepdims=True)
    centered = inputs - average
    inv_std = lax.rsqrt(jnp.mean(centered * centered, axis=-1, keepdims=True) + epsilon)
    whitened = centered * inv_std
    normed = (whitened * ln_gain + ln_bias).astype(bf16)
    mixed = jnp.einsum("btd,de->bte", normed, w_in, preferred_element_type=f32) + b_in
    prev_rows = shifted(mixed[:, block_len - 2 :], "seq", 1)
    padded = jnp.concatenate([prev_rows, mixed], axis=1)
    delay_one = padded[:, 1:-1]
    delay_two = padded[:, :-2]
    short_out = short_w[0] * mixed + short_w[1] * delay_one + short_w[2] * delay_two + short_b
    outer_gate = short_out[..., :model_width]
    inner_gate = short_out[..., model_width : 2 * model_width]
    values = short_out[..., 2 * model_width :]
    gated = (values * inner_gate).astype(bf16)
    d_product = jnp.einsum(
        "bte,de->btd", cotangent, w_out, preferred_element_type=f32
    ).astype(bf16)
    d_prod_f = d_product.astype(f32)
    d_summed = (d_prod_f * outer_gate).astype(bf16)

    def to_channels(value):
        return lax.all_to_all(value, "seq", split_axis=2, concat_axis=1, tiled=True)

    def to_tokens(value):
        return lax.all_to_all(value, "seq", split_axis=1, concat_axis=2, tiled=True)

    gated_ch = to_channels(gated)
    d_ch = to_channels(d_summed)
    positions = jnp.asarray(position_features(length, w_one.shape[0]))
    w_three_part = lax.dynamic_slice_in_dim(w_three, col_start, channels, 1)
    decay_part = lax.dynamic_slice_in_dim(decay_rates, col_start, channels, 0)
    bias_part = lax.dynamic_slice_in_dim(filt_bias, col_start, channels, 0)

    def kernel_of(first_w, first_b, second_w, second_b, third_w):
        return filter_shape(positions, first_w, first_b, second_w, second_b, third_w, decay_part)

    kernel_full, kernel_pull = jax.vjp(kernel_of, w_one, b_one, w_two, b_two, w_three_part)
    matrix = jnp.asarray(dft_matrix(length))

    def spectrum(value):
        return jnp.einsum("kt,btc->bkc", matrix, value, preferred_element_type=f32)

    def inverse(cosines, sines):
        both = jnp.concatenate([cosines, sines], axis=1).astype(bf16)
        return jnp.einsum("kt,bkc->btc", matrix, both, preferred_element_type=f32) * (1.0 / length)

    k_both = spectrum(kernel_full.astype(bf16)[None])
    g_both = spectrum(gated_ch)
    d_both = spectrum(d_ch)
    k_c, k_s = k_both[:, :length], k_both[:, length:]
    g_c, g_s = g_both[:, :length], g_both[:, length:]
    d_c, d_s = d_both[:, :length], d_both[:, length:]
    long_out = inverse(g_c * k_c - g_s * k_s, g_c * k_s + g_s * k_c)
    gated_float = gated_ch.astype(f32)
    d_ch_float = d_ch.astype(f32)
    summed_ch = (long_out + bias_part * gated_float).astype(bf16)
    summed = to_tokens(summed_ch).astype(f32)
    grad_in = inverse(k_c * d_c + k_s * d_s, k_c * d_s - k_s * d_c) + bias_part * d_ch_float
    d_gated = to_tokens(grad_in.astype(bf16)).astype(f32)
    d_kernel = inverse(
        jnp.sum(g_c * d_c + g_s * d_s, axis=0, keepdims=True),
        jnp.sum(g_c * d_s - g_s * d_c, axis=0, keepdims=True),
    )[0]
    g_bias_part = jnp.sum(d_ch_float * gated_float, axis=(0, 1))
    g_w_one, g_b_one, g_w_two, g_b_two, g_w_three_part = kernel_pull(d_kernel)

    product = (summed * outer_gate).astype(bf16)
    result = jnp.einsum("btd,de->bte", product, w_out, preferred_element_type=f32) + b_out
    block_out = (inputs + result).astype(bf16)
    grad_out = cotangent.astype(f32)
    g_w_out = jnp.einsum("btd,bte->de", product, cotangent, preferred_element_type=f32)
    g_b_out = jnp.sum(grad_out, axis=(0, 1))
    d_outer = d_prod_f * summed
    d_short = jnp.concatenate([d_outer, d_gated * values, d_gated * inner_gate], axis=-1)
    g_short_w = jnp.stack(
        [
            jnp.sum(d_short * mixed, axis=(0, 1)),
            jnp.sum(d_short * delay_one, axis=(0, 1)),
            jnp.sum(d_short * delay_two, axis=(0, 1)),
        ]
    )
    g_short_b = jnp.sum(d_short, axis=(0, 1))
    next_rows = shifted(d_short[:, :2], "seq", -1)
    extended = jnp.concatenate([d_short, next_rows], axis=1)
    d_mixed = (
        short_w[0] * extended[:, :block_len]
        + short_w[1] * extended[:, 1 : block_len + 1]
        + short_w[2] * extended[:, 2:]
    ).astype(bf16)
    g_w_in = jnp.einsum("btd,bte->de", normed, d_mixed, preferred_element_type=f32)
    g_b_in = jnp.sum(d_mixed.astype(f32), axis=(0, 1))
    d_normed = jnp.einsum("bte,de->btd", d_mixed, w_in, preferred_element_type=f32)
    g_ln_gain = jnp.sum(d_normed * whitened, axis=(0, 1))
    g_ln_bias = jnp.sum(d_normed, axis=(0, 1))
    d_white = d_normed * ln_gain
    grad_tokens = grad_out + inv_std * (
        d_white
        - jnp.mean(d_white, axis=-1, keepdims=True)
        - whitened * jnp.mean(d_white * whitened, axis=-1, keepdims=True)
    )
    rows = model_width // devices
    big = jnp.concatenate([g_w_in, g_w_out], axis=1)
    big = reduce_scatter(big.reshape(seq_devices, batch_devices, rows, -1), bf16)
    out_w_in, out_w_out = big[:, : 3 * model_width], big[:, 3 * model_width :]
    g_w_three = lax.dynamic_update_slice_in_dim(
        jnp.zeros(w_three.shape, f32), g_w_three_part, col_start, 1
    )
    g_filt_bias = lax.dynamic_update_slice_in_dim(
        jnp.zeros(filt_bias.shape, f32), g_bias_part, col_start, 0
    )
    vectors = jnp.concatenate(
        [
            g_ln_gain[None],
            g_ln_bias[None],
            g_b_out[None],
            g_filt_bias[None],
            g_w_three,
        ],
        axis=0,
    )
    vectors = jnp.transpose(vectors.reshape(-1, devices, rows), (1, 0, 2)).reshape(devices, -1)
    wides = jnp.concatenate([g_b_in[None], g_short_w, g_short_b[None]], axis=0)
    wides = jnp.transpose(wides.reshape(-1, devices, 3 * rows), (1, 0, 2)).reshape(devices, -1)
    net = jnp.concatenate([v.reshape(-1) for v in (g_w_one, g_b_one, g_w_two, g_b_two)])
    net_size = net.shape[0]
    net_part = -(-net_size // devices)
    net = jnp.pad(net, (0, net_part * devices - net_size)).reshape(devices, net_part)
    small = jnp.concatenate([vectors, wides, net], axis=1)
    small = reduce_scatter(small.reshape(seq_devices, batch_devices, -1), f32)
    hidden = w_two.shape[0]
    cut = rows * (4 + hidden)
    vectors = small[:cut].reshape(4 + hidden, rows)
    wides = small[cut : cut + 15 * rows].reshape(5, 3 * rows)
    net = lax.all_gather(small[cut + 15 * rows :], ("seq", "batch"), tiled=True)
    features = w_one.shape[0]
    edges = [features * hidden, (features + 1) * hidden, (features + 1 + hidden) * hidden]
    return (
        block_out,
        grad_tokens,
        vectors[0],
        vectors[1],
        out_w_in,
        wides[0],
        wides[1:4],
        wides[4],
        net[: edges[0]].reshape(features, hidden),
        net[edges[0] : edges[1]],
        net[edges[1] : edges[2]].reshape(hidden, hidden),
        net[edges[2] : net_size],
        vectors[4:],
        vectors[3],
        out_w_out,
        vectors[2],
    )


def solution(mesh):
    tokens_spec = P("batch", "seq", None)
    both = ("seq", "batch")
    in_specs = (tokens_spec, tokens_spec) + (P(),) * 15
    out_specs = (
        tokens_spec,
        tokens_spec,
        P(both),
        P(both),
        P(both, None),
        P(both),
        P(None, both),
        P(both),
        P(),
        P(),
        P(),
        P(),
        P(None, both),
        P(both),
        P(both, None),
        P(both),
    )
    return jax.shard_map(local, mesh=mesh, in_specs=in_specs, out_specs=out_specs, check_vma=False)
```

time: 1360 us -> 384 us (0.28)
  waiting for transfers between devices: 655 us -> 112 us
  matrix products: 386 us -> 53.8 us
  local copies, waits for them, and re-layouts: 167 us -> 62.1 us
  blocking collectives: 0 us -> 66.6 us
  starting transfers between devices: 98.7 us -> 43.8 us
  other arithmetic: 20.8 us -> 37.4 us
    reduce_scatter x3 -> x0, waiting for transfers between devices: 434 us -> none  [the longest x1 160 us: local(): lax.psum_scatter(g_w_in, ('seq', 'batch'), scatter_dimension=0, tiled=True)]
    dot_general x40 -> x13, matrix products: 367 us -> 39.4 us  [the longest x3 11.6 us: spectrum(): return jnp.einsum('kt,btc->bkc', matrix, value, preferred_element_type=f32)]
    unnamed x7 -> x0, waiting for transfers between devices: 201 us -> none
    all_to_all x4 -> x8, waiting for transfers between devices: 9.13 us -> 111 us  [the longest x2 92.9 us: reduce_scatter(): lax.all_to_all(value.astype(dtype), 'batch', split_axis=1, concat_axis=1,...]
    cond x11 -> x0, local copies, waits for them, and re-layouts: 86.1 us -> none
    ppermute x16 -> x2, starting transfers between devices: 81.3 us -> 4.06 us  [shifted(): lax.ppermute(value, axis, [(source, source + steps) for source in range(f...]
    unnamed x0 -> x1, blocking collectives: none -> 66.6 us
    all_to_all x4 -> x8, starting transfers between devices: 17 us -> 39.7 us  [the longest x2 12.2 us: to_channels(): return lax.all_to_all(value, 'seq', split_axis=2, concat_axis=1, tiled=True)]
  transfers between devices with their start and end apart: 25 -> 10, of which waited for: 16 -> 5; matrix products, arithmetic and copies ran while one was open for 33% -> 21% of each run, Pallas kernels for 0% -> 0%
where the time goes in v1:
time: 384 us; the launch traced here: 377 us
  waiting for transfers between devices  112 us (29%)
  blocking collectives  66.6 us (17%)
  local copies, waits for them, and re-layouts  62.1 us (16%)
  matrix products  53.8 us (14%)
  starting transfers between devices  43.8 us (11%)
  other arithmetic  37.4 us (10%)
    all_to_all x2, waiting for transfers between devices, reduce_scatter(): lax.all_to_all(value.astype(dtype), 'batch', split_axis=1, concat_axis=1,...  92.9 us
    unnamed x1, blocking collectives  66.6 us
    all_to_all x2, waiting for transfers between devices, to_channels(): return lax.all_to_all(value, 'seq', split_axis=2, concat_axis=1, tiled=True)  12.5 us
    all_to_all x2, starting transfers between devices, to_channels(): return lax.all_to_all(value, 'seq', split_axis=2, concat_axis=1, tiled=True)  12.2 us
    dot_general x3, matrix products, spectrum(): return jnp.einsum('kt,btc->bkc', matrix, value, preferred_element_type=f32)  11.6 us
    dot_general x4, matrix products, inverse(): jnp.einsum('kt,bkc->btc', matrix, both, preferred_element_type=f32)  9.84 us
    all_to_all x2, starting transfers between devices, to_tokens(): return lax.all_to_all(value, 'seq', split_axis=1, concat_axis=2, tiled=True)  9.45 us
    all_to_all x2, starting transfers between devices, reduce_scatter(): lax.all_to_all(value.astype(dtype), 'batch', split_axis=1, concat_axis=1,...  9.37 us
  transfers between devices with their start and end apart: 10, of which 5 were waited for; matrix products, arithmetic and copies ran while one was open for 21% of the time, Pallas kernels for 0%

profile of v1, /device:TPU:0, one launch (start us, length us, event | category | flops | bytes accessed | tf_op | source)
XLA Modules:
  0.0 376.9 jit_solution(17441243850110117770)
XLA Ops:
  0.7 1.3 convert_reduce_fusion.2
  2.0 1.3 fusion.48
  3.4 4.8 %fusion.4 = f32[2,128,3072]{2,1,0:T(8,128)S(1)} fusion(bf16[1024,3072]{1,0:T(8,128)(2,1)} %param.23, f32[3072]{0:T(1024)} %param.24, bf16[2,128,1024]{2,1,0:T(8,128)(2,1)} %param.19, f32[1024]{0:T(1024)} %param.22, f32[1024]{0:T(1024)} %param.21, f32[2,128]{1,0:T(2,128)S(1)} %add_rsqrt_fusion, f32[2,128]{1,0:T(2,128)S(1)} %broadcast_multiply_fusion.2), kind=kOutput, calls=%fused_computation.8 | convolution fusion | flops 1612972032 | bytes 9984000 | tf_op jit(solution)/shard_map/btd,de->bte/dot_general | solution.py:82
  8.2 2.4 collective-permute-start
  11.5 1.1 add_add_fusion
  12.6 1.7 copy-done.2
  14.4 1.8 fusion.49
  17.3 8.5 %all-to-all-start.2 = ((bf16[2,128,1024]{1,0,2:T(2,128)(2,1)}), bf16[2,128,1024]{1,0,2:T(2,128)(2,1)S(1)}, u32[]{:S(2)}, u32[]{:S(2)}) async-start(bf16[2,128,1024]{1,0,2:T(2,128)(2,1)} %copy.128), calls=%async_computation.2 | async-start | bytes 1048576 | tf_op jit(solution)/shard_map/all_to_all | solution.py:99
  27.3 2.9 fusion.69
  30.2 1.9 fusion.70
  32.1 2.0 copy.122
  34.1 7.0 %all-to-all-done.2 = bf16[2,128,1024]{1,0,2:T(2,128)(2,1)S(1)} async-done(((bf16[2,128,1024]{1,0,2:T(2,128)(2,1)}), bf16[2,128,1024]{1,0,2:T(2,128)(2,1)S(1)}, u32[]{:S(2)}, u32[]{:S(2)}) %all-to-all-start.2) | async-done | bytes 524320 | tf_op jit(solution)/shard_map/all_to_all | solution.py:99
  41.2 3.7 all-to-all-start
  44.8 1.8 fusion.41
  46.6 3.7 convolution_bitcast_fusion.2
  52.6 2.1 reshape.196
  54.6 5.5 %all-to-all-done = bf16[2,128,1024]{1,0,2:T(2,128)(2,1)S(1)} async-done(((bf16[2,128,1024]{1,0,2:T(2,128)(2,1)}), bf16[2,128,1024]{1,0,2:T(2,128)(2,1)S(1)}, u32[]{:S(2)}, u32[]{:S(2)}) %all-to-all-start) | async-done | bytes 524320 | tf_op jit(solution)/shard_map/all_to_all | solution.py:99
  61.2 2.1 reshape.193
  63.3 5.1 %convolution_bitcast_fusion = f32[2,2048,128]{1,2,0:T(8,128)} fusion(bf16[2,1024,128]{2,1,0:T(8,128)(2,1)} %reshape.196, bf16[2048,1024,1]{1,0,2:T(8,128)(2,1)} %constant.48), kind=kOutput, calls=%fused_computation.25 | convolution fusion | flops 1073741824 | bytes 6815744 | tf_op jit(solution)/shard_map/kt,btc->bkc/dot_general | solution.py:118
  68.5 2.7 convolution_bitcast_fusion.1
  71.2 1.3 copy.162
  72.4 2.4 reshape.203
  74.8 5.4 %subtract_reduce_fusion = (bf16[1024,128]{0,1:T(8,128)(2,1)}, bf16[1024,128]{0,1:T(8,128)(2,1)}, bf16[2,1024,128]{1,2,0:T(8,128)(2,1)}, bf16[2,1024,128]{1,2,0:T...) fusion(f32[2,2048,128]{1,2,0:T(8,128)} %convolution_bitcast_fusion, ...), kind=kLoop, calls=%fused_computation.84 | loop fusion | flops 6029312 | bytes 7864320 | tf_op jit(solution)/shard_map/reduce_sum | solution.py:139
  80.2 2.1 fusion.24
  82.2 2.0 copy.132
  84.2 4.4 %all-to-all-start.3 = ((bf16[2,1024,128]{2,0,1:T(2,128)(2,1)}), bf16[2,1024,128]{2,0,1:T(2,128)(2,1)}, u32[]{:S(2)}, u32[]{:S(2)}) async-start(bf16[2,1024,128]{2,0,1:T(2,128)(2,1)} %copy.132), calls=%async_computation.3 | async-start | bytes 1048576 | tf_op jit(solution)/shard_map/all_to_all | solution.py:102
  88.6 1.3 copy.164
  89.9 2.4 reshape.201
  92.3 2.2 multiply_reduce_fusion.3
  94.5 4.1 %fusion.25 = bf16[2,1024,128]{1,2,0:T(8,128)(2,1)S(1)} fusion(bf16[2048,1024,1]{1,0,2:T(8,128)(2,1)} %constant.49, bf16[2,1024,128]{1,2,0:T(8,128)(2,1)} %get-tuple-element.119, bf16[2,1024,128]{1,2,0:T(8,128)(2,1)} %get-tuple-element.120, f32[2,1024,128]{1,2,0:T(8,128)} %reshape.201, f32[128]{0:T(128)S(1)} %dynamic_slice.11), kind=kOutput, calls=%fused_computation.47 | convolution fusion | flops 1076887552 | bytes 6816256 | tf_op jit(solution)/shard_map/kt,bkc->btc/dot_general | solution.py:122
  102.1 2.7 fusion.75
  105.8 2.3 fusion.72
  108.1 5.1 %all-to-all-start.1 = ((bf16[2,1024,128]{2,0,1:T(2,128)(2,1)}), bf16[2,1024,128]{2,0,1:T(2,128)(2,1)}, u32[]{:S(2)}, u32[]{:S(2)}) async-start(bf16[2,1024,128]{2,0,1:T(2,128)(2,1)} %copy.126), calls=%async_computation.1 | async-start | bytes 1048576 | tf_op jit(solution)/shard_map/all_to_all | solution.py:102
  113.1 2.2 fusion.71
  115.3 2.0 fusion.73
  119.1 2.5 copy.161
  121.6 1.4 reshape.204
  123.0 5.6 %all-to-all-done.1 = bf16[2,1024,128]{2,0,1:T(2,128)(2,1)} async-done(((bf16[2,1024,128]{2,0,1:T(2,128)(2,1)}), bf16[2,1024,128]{2,0,1:T(2,128)(2,1)}, u32[]{:S(2)}, u32[]{:S(2)}) %all-to-all-start.1) | async-done | bytes 524320 | tf_op jit(solution)/shard_map/all_to_all | solution.py:102
  128.6 2.3 copy.163
  130.9 2.4 reshape.202
  133.3 2.9 slice_multiply_fusion.3
  136.6 1.7 collective-permute-start.1
  138.4 2.1 bitcast_convert_fusion.1
  140.8 1.5 copy-done.4
  142.3 2.5 multiply_reduce_fusion
  144.9 3.0 fusion.47
  147.9 4.7 %bitcast_convert_fusion = bf16[1024,3072]{1,0:T(8,128)(2,1)} fusion(bf16[2,128,3072]{2,1,0:T(8,128)(2,1)S(1)} %get-tuple-element.111, bf16[2,128,1024]{2,1,0:T(8,128)(2,1)S(1)} %copy-done.5, f32[1024]{0:T(1024)S(1)} %copy-done.22, f32[1024]{0:T(1024)S(1)} %copy-done.21, f32[2,128]{1,0:T(2,128)S(1)} %add_rsqrt_fusion, f32[2,128]{1,0:T(2,128)S(1)} %broadcast_multiply_fusion.2), kind=kOutput, calls=%fused_computation | convolution fusion | flops 1615331328 | bytes 8398848 | tf_op jit(solution)/shard_map/btd,bte->de/dot_general | solution.py:167
  152.6 1.1 concatenate.93
  153.7 1.1 concatenate.94
  154.9 2.7 convert_reduce_fusion.3
  157.9 2.6 concatenate.80
  160.5 2.5 copy.141
  163.0 1.6 concatenate.81
  166.3 3.7 all-to-all-start.4
  170.0 7.6 %pad_maximum_fusion = bf16[1024,4096]{1,0:T(8,128)(2,1)} fusion(bf16[1024,1024]{1,0:T(8,128)(2,1)} %bitcast_convert_fusion.1, bf16[1024,3072]{1,0:T(8,128)(2,1)} %bitcast_convert_fusion), kind=kLoop, calls=%fused_computation.1 | loop fusion | flops 16777216 | bytes 16777216 | tf_op jit(solution)/shard_map/concatenate | solution.py:179
  177.6 7.7 %copy.146 = bf16[8,4,32,4096]{3,2,0,1:T(8,128)(2,1)} copy(bf16[8,4,32,4096]{3,2,1,0:T(8,128)(2,1)} %bitcast.137) | data formatting | bytes 16777216 | tf_op jit(solution)/shard_map/convert_element_type | solution.py:44
  185.3 5.7 %all-to-all-start.6 = ((bf16[8,4,32,4096]{3,2,0,1:T(8,128)(2,1)}), bf16[8,4,32,4096]{3,2,0,1:T(8,128)(2,1)}, u32[]{:S(2)}, u32[]{:S(2)}) async-start(bf16[8,4,32,4096]{3,2,0,1:T(8,128)(2,1)} %copy.146), calls=%async_computation.6 | async-start | bytes 16777216 | tf_op jit(solution)/shard_map/all_to_all | solution.py:44
  191.7 92.9 %all-to-all-done.6 = bf16[8,4,32,4096]{3,2,0,1:T(8,128)(2,1)} async-done(((bf16[8,4,32,4096]{3,2,0,1:T(8,128)(2,1)}), bf16[8,4,32,4096]{3,2,0,1:T(8,128)(2,1)}, u32[]{:S(2)}, u32[]{:S(2)}) %all-to-all-start.6) | async-done | bytes 8388640 | tf_op jit(solution)/shard_map/all_to_all | solution.py:44
  284.6 3.5 all-to-all-start.5
  288.2 7.0 %reduce_sum.219 = bf16[8,32,4096]{2,1,0:T(8,128)(2,1)} reduce(bf16[8,4,32,4096]{3,2,0,1:T(8,128)(2,1)} %all-to-all-done.6, bf16[]{:T(256)} %constant.34.clone.1), dimensions={1}, to_apply=%region_19.0 | reduce | flops 3145728 | bytes 10485762 | tf_op jit(solution)/shard_map/reduce_sum | solution.py:45
  295.1 5.2 %all-to-all-start.7 = ((bf16[8,32,4096]{2,1,0:T(8,128)(2,1)}), bf16[8,32,4096]{2,1,0:T(8,128)(2,1)}, u32[]{:S(2)}, u32[]{:S(2)}) async-start(bf16[8,32,4096]{2,1,0:T(8,128)(2,1)} %reduce_sum.219), calls=%async_computation.7 | async-start | bytes 4194304 | tf_op jit(solution)/shard_map/all_to_all | solution.py:46
  300.3 1.5 fusion.29
  302.2 66.6 %all-reduce = f32[6336]{0:T(1024)S(1)} all-reduce(f32[6336]{0:T(1024)S(1)} %slice_dynamic-update-slice_fusion), channel_id=1, replica_groups=mesh['seq'=8,'batch'=4] {'seq','batch'}, use_global_device_ids=true, to_apply=%add | all-reduce | flops 6336 | bytes 50688
  373.3 1.9 convert_reduce_fusion
  (126 shorter events, 22.8 us)
Async XLA Ops:
  0.6 13.7 %copy-start = (bf16[1024,1024]{1,0:T(8,128)(2,1)S(1)}, bf16[1024,1024]{1,0:T(8,128)(2,1)}, u32[]{:S(2)}) copy-start(bf16[1024,1024]{1,0:T(8,128)(2,1)} %param.34) | copy-start | bytes 6291460
  3.3 7.2 %copy-start.23 = (f32[3,3072]{1,0:T(4,128)S(1)}, f32[3,3072]{1,0:T(4,128)}, u32[]{:S(2)}) copy-start(f32[3,3072]{1,0:T(4,128)} %param.25) | copy-start | bytes 110596
  3.4 8.1 %copy-start.24 = (f32[3072]{0:T(1024)S(1)}, f32[3072]{0:T(1024)}, u32[]{:S(2)}) copy-start(f32[3072]{0:T(1024)} %param.26) | copy-start | bytes 36868
  8.2 4.4 %copy-start.3 = (f32[2,128,3072]{2,1,0:T(8,128)}, f32[2,128,3072]{2,1,0:T(8,128)S(1)}, u32[]{:S(2)}) copy-start(f32[2,128,3072]{2,1,0:T(8,128)S(1)} %fusion.4) | copy-start | bytes 9437188
  8.2 3.2 collective-permute-start
  11.5 2.9 copy-start.6
  12.6 1.7 copy-start.2
  14.3 13.0 %copy-start.12 = (f32[1024,33]{1,0:T(8,128)S(1)}, f32[1024,33]{1,0:T(8,128)}, u32[]{:S(2)}) copy-start(f32[1024,33]{1,0:T(8,128)} %constant.35.clone) | copy-start | bytes 405508
  14.3 13.0 %copy-start.25 = (f32[64]{0:T(128)S(1)}, f32[64]{0:T(128)}, u32[]{:S(2)}) copy-start(f32[64]{0:T(128)} %param.28) | copy-start | bytes 772
  14.3 15.9 %copy-start.20 = (f32[64,64]{1,0:T(8,128)S(1)}, f32[64,64]{1,0:T(8,128)}, u32[]{:S(2)}) copy-start(f32[64,64]{1,0:T(8,128)} %param.29) | copy-start | bytes 49156
  14.4 15.9 %copy-start.26 = (f32[64]{0:T(128)S(1)}, f32[64]{0:T(128)}, u32[]{:S(2)}) copy-start(f32[64]{0:T(128)} %param.30) | copy-start | bytes 772
  17.3 23.9 %all-to-all-start.2 = ((bf16[2,128,1024]{1,0,2:T(2,128)(2,1)}), bf16[2,128,1024]{1,0,2:T(2,128)(2,1)S(1)}, u32[]{:S(2)}, u32[]{:S(2)}) async-start(bf16[2,128,1024]{1,0,2:T(2,128)(2,1)} %copy.128), calls=%async_computation.2 | async-start | bytes 1048576 | tf_op jit(solution)/shard_map/all_to_all | solution.py:99
  30.2 10.9 %copy-start.9 = (f32[1024,64]{0,1:T(8,128)}, f32[1024,64]{0,1:T(8,128)S(1)}, u32[]{:S(2)}) copy-start(f32[1024,64]{0,1:T(8,128)S(1)} %get-tuple-element.140) | copy-start | bytes 786436
  41.2 18.9 %all-to-all-start = ((bf16[2,128,1024]{1,0,2:T(2,128)(2,1)}), bf16[2,128,1024]{1,0,2:T(2,128)(2,1)S(1)}, u32[]{:S(2)}, u32[]{:S(2)}) async-start(bf16[2,128,1024]{1,0,2:T(2,128)(2,1)} %copy.122), calls=%async_computation | async-start | bytes 1048576 | tf_op jit(solution)/shard_map/all_to_all | solution.py:99
  63.3 5.1 %copy-start.1 = (bf16[2048,1024,1]{1,0,2:T(8,128)(2,1)S(1)}, bf16[2048,1024,1]{1,0,2:T(8,128)(2,1)}, u32[]{:S(2)}) copy-start(bf16[2048,1024,1]{1,0,2:T(8,128)(2,1)} %constant.48) | copy-start | bytes 12582916
  63.3 5.1 %copy-start.8 = (bf16[2,1024,128]{2,1,0:T(8,128)(2,1)S(1)}, bf16[2,1024,128]{2,1,0:T(8,128)(2,1)}, u32[]{:S(2)}) copy-start(bf16[2,1024,128]{2,1,0:T(8,128)(2,1)} %reshape.193) | copy-start | bytes 1572868
  74.8 5.4 %copy-start.17 = (f32[2,1024,128]{1,2,0:T(8,128)S(1)}, f32[2,1024,128]{1,2,0:T(8,128)}, u32[]{:S(2)}) copy-start(f32[2,1024,128]{1,2,0:T(8,128)} %reshape.203) | copy-start | bytes 3145732
  74.8 5.4 %copy-start.28 = (bf16[2048,1024,1]{1,0,2:T(8,128)(2,1)S(1)}, bf16[2048,1024,1]{1,0,2:T(8,128)(2,1)}, u32[]{:S(2)}) copy-start(bf16[2048,1024,1]{1,0,2:T(8,128)(2,1)} %constant.49) | copy-start | bytes 12582916
  84.2 23.8 %all-to-all-start.3 = ((bf16[2,1024,128]{2,0,1:T(2,128)(2,1)}), bf16[2,1024,128]{2,0,1:T(2,128)(2,1)}, u32[]{:S(2)}, u32[]{:S(2)}) async-start(bf16[2,1024,128]{2,0,1:T(2,128)(2,1)} %copy.132), calls=%async_computation.3 | async-start | bytes 1048576 | tf_op jit(solution)/shard_map/all_to_all | solution.py:102
  94.5 7.6 %copy-start.19 = (bf16[1024,128]{0,1:T(8,128)(2,1)S(1)}, bf16[1024,128]{0,1:T(8,128)(2,1)}, u32[]{:S(2)}) copy-start(bf16[1024,128]{0,1:T(8,128)(2,1)} %get-tuple-element.100) | copy-start | bytes 786436
  98.6 6.1 %copy-start.16 = (bf16[1024,128]{0,1:T(8,128)(2,1)S(1)}, bf16[1024,128]{0,1:T(8,128)(2,1)}, u32[]{:S(2)}) copy-start(bf16[1024,128]{0,1:T(8,128)(2,1)} %get-tuple-element.99) | copy-start | bytes 786436
  102.1 2.7 copy-start.11
  102.1 3.7 copy-start.18
  104.8 12.6 %copy-start.10 = (f32[1024,64]{0,1:T(8,128)S(1)}, f32[1024,64]{0,1:T(8,128)}, u32[]{:S(2)}) copy-start(f32[1024,64]{0,1:T(8,128)} %copy-done.9) | copy-start | bytes 786436
  108.1 20.5 %all-to-all-start.1 = ((bf16[2,1024,128]{2,0,1:T(2,128)(2,1)}), bf16[2,1024,128]{2,0,1:T(2,128)(2,1)}, u32[]{:S(2)}, u32[]{:S(2)}) async-start(bf16[2,1024,128]{2,0,1:T(2,128)(2,1)} %copy.126), calls=%async_computation.1 | async-start | bytes 1048576 | tf_op jit(solution)/shard_map/all_to_all | solution.py:102
  119.1 2.5 copy-start.15
  136.3 2.1 copy-start.13
  136.3 2.1 copy-start.7
  136.6 3.8 %collective-permute-start.1 = (f32[2,2,3072]{2,1,0:T(2,128)S(1)}, f32[2,2,3072]{2,1,0:T(2,128)S(1)}, u32[]{:S(2)}, u32[]{:S(2)}) collective-permute-start(f32[2,2,3072]{2,1,0:T(2,128)S(1)} %slice.193), channel_id=1, source_target_pairs={{4,0},{8,4},{12,8},{16,12},{20,16},{24,20},{28,24},{5,1},{9,5},{13... | collective-permute-start | bytes 147464 | tf_op jit(solution)/shard_map/ppermute | solution.py:40
  140.4 1.9 copy-start.4
  140.4 4.4 %slice-start = ((s8[6291456]{0:T(1024)(128)(4,1)}), s8[4194304]{0:T(1024)(128)(4,1)S(1)}, s32[]{:S(2)}) async-start(s8[6291456]{0:T(1024)(128)(4,1)} %bitcast.153), calls=%async_computation.8 | async-start | bytes 8388608
  142.3 2.5 copy-start.5
  142.3 2.5 copy-start.21
  142.3 2.5 slice-start.1
  144.9 3.0 copy-start.22
  166.3 19.0 %all-to-all-start.4 = ((f32[8,4,2854]{2,0,1:T(8,128)}), f32[8,4,2854]{2,0,1:T(8,128)S(1)}, u32[]{:S(2)}, u32[]{:S(2)}) async-start(f32[8,4,2854]{2,0,1:T(8,128)} %copy.142), calls=%async_computation.4 | async-start | bytes 753664 | tf_op jit(solution)/shard_map/all_to_all | solution.py:44
  185.3 99.3 %all-to-all-start.6 = ((bf16[8,4,32,4096]{3,2,0,1:T(8,128)(2,1)}), bf16[8,4,32,4096]{3,2,0,1:T(8,128)(2,1)}, u32[]{:S(2)}, u32[]{:S(2)}) async-start(bf16[8,4,32,4096]{3,2,0,1:T(8,128)(2,1)} %copy.146), calls=%async_computation.6 | async-start | bytes 16777216 | tf_op jit(solution)/shard_map/all_to_all | solution.py:44
  284.6 10.5 %all-to-all-start.5 = ((f32[8,1,2854]{2,1,0:T(1,128)}), f32[8,1,2854]{2,1,0:T(1,128)S(1)}, u32[]{:S(2)}, u32[]{:S(2)}) async-start(f32[8,1,2854]{2,1,0:T(1,128)} %all_to_all.66), calls=%async_computation.5 | async-start | bytes 188416 | tf_op jit(solution)/shard_map/all_to_all | solution.py:46
  295.1 5.2 %copy-start.14 = (bf16[2,128,1024]{2,1,0:T(8,128)(2,1)S(1)}, bf16[2,128,1024]{2,1,0:T(8,128)(2,1)}, u32[]{:S(2)}) copy-start(bf16[2,128,1024]{2,1,0:T(8,128)(2,1)} %copy-done.13) | copy-start | bytes 1572868
  295.1 5.2 %copy-start.27 = (f32[1024]{0:T(1024)S(1)}, f32[1024]{0:T(1024)}, u32[]{:S(2)}) copy-start(f32[1024]{0:T(1024)} %param.35) | copy-start | bytes 12292
  295.1 78.2 %all-to-all-start.7 = ((bf16[8,32,4096]{2,1,0:T(8,128)(2,1)}), bf16[8,32,4096]{2,1,0:T(8,128)(2,1)}, u32[]{:S(2)}, u32[]{:S(2)}) async-start(bf16[8,32,4096]{2,1,0:T(8,128)(2,1)} %reduce_sum.219), calls=%async_computation.7 | async-start | bytes 4194304 | tf_op jit(solution)/shard_map/all_to_all | solution.py:46

commit v2 on v1

--- a/solution.py
+++ b/solution.py
@@ -2,6 +2,8 @@
 import jax.numpy as jnp
 import numpy as np
 from jax import lax
+from jax.experimental import pallas as pl
+from jax.experimental.pallas import tpu as pltpu
 from jax.sharding import PartitionSpec as P
 
 highest = lax.Precision.HIGHEST
@@ -231,6 +233,805 @@
     )
 
 
+MESH = pl.DeviceIdType.MESH
+HALF_TURN = (1.5703125, 4.837512969970703125e-4, 7.549789948768648e-8)
+
+
+def sin_cos(x):
+    turns = jnp.floor(x * 0.6366197723675814 + 0.5)
+    r = ((x - turns * HALF_TURN[0]) - turns * HALF_TURN[1]) - turns * HALF_TURN[2]
+    q = turns.astype(jnp.int32)
+    r2 = r * r
+    sine = r + r * r2 * (
+        -1.6666654611e-1 + r2 * (8.3321608736e-3 + r2 * -1.9515295891e-4)
+    )
+    cosine = 1.0 - 0.5 * r2 + r2 * r2 * (
+        4.166664568298827e-2 + r2 * (-1.388731625493765e-3 + r2 * 2.443315711809948e-5)
+    )
+    odd = (q & 1) == 1
+    s_abs, c_abs = jnp.where(odd, cosine, sine), jnp.where(odd, sine, cosine)
+    s_neg, c_neg = (q & 2) == 2, ((q + 1) & 2) == 2
+    return jnp.where(s_neg, -s_abs, s_abs), jnp.where(c_neg, -c_abs, c_abs)
+
+
+def mm(a, b, dims=((1,), (0,))):
+    return lax.dot_general(a, b, (dims, ((), ())), preferred_element_type=f32)
+
+
+def mm_full(a, b, dims=((1,), (0,))):
+    return lax.dot_general(
+        a, b, (dims, ((), ())), precision=highest, preferred_element_type=f32
+    )
+
+
+def twice(v):
+    return jnp.concatenate([v, v], axis=1)
+
+
+def lanes(start, size):
+    return pl.ds(pl.multiple_of(start, size), size)
+
+
+NT, TN = ((1,), (1,)), ((0,), (0,))
+
+
+def whole_kernel(
+    tok_ref,
+    cot_ref,
+    gain_ref,
+    beta_ref,
+    win_ref,
+    bin_ref,
+    sw_ref,
+    sb_ref,
+    w1_ref,
+    b1_ref,
+    w2_ref,
+    b2_ref,
+    w3_ref,
+    decay_ref,
+    fb_ref,
+    wout_ref,
+    bout_ref,
+    pos_ref,
+    f_ref,
+    ft_ref,
+    out_ref,
+    gtok_ref,
+    gwin_ref,
+    gwout_ref,
+    oa_ref,
+    ob_ref,
+    oc_ref,
+    w_in,
+    w_out,
+    fm,
+    ft,
+    halo,
+    white,
+    istd,
+    normed,
+    mx,
+    oiv,
+    dpr,
+    gsend,
+    gch,
+    dsend,
+    dch,
+    ysend,
+    yrecv,
+    qsend,
+    qrecv,
+    first,
+    first_c,
+    second,
+    second_c,
+    window,
+    ksp,
+    gsp,
+    zs,
+    es,
+    dk,
+    product,
+    pts,
+    dsx,
+    dms,
+    dn,
+    nt,
+    pt,
+    dm,
+    cot,
+    core_send,
+    core_recv,
+    core_send_o,
+    core_recv_o,
+    z_send,
+    z_recv,
+    z_send_o,
+    z_recv_o,
+    own,
+    last_send,
+    last_recv,
+    sa,
+    sb,
+    sc,
+    load_sem,
+    halo_sem,
+    a_sem,
+    b_sem,
+    c_sem,
+    zed_sem,
+    l_sem,
+    s_sem,
+):
+    s, b = lax.axis_index("seq"), lax.axis_index("batch")
+    zed, core = s // 2, s % 2
+    other = (zed * 2 + 1 - core, b)
+
+    loads = [
+        pltpu.make_async_copy(src, dst, load_sem.at[i])
+        for i, (src, dst) in enumerate(
+            ((win_ref, w_in), (wout_ref, w_out), (f_ref, fm), (ft_ref, ft))
+        )
+    ]
+    for load in loads:
+        load.start()
+
+    def batch_peer(p):
+        return (s, (b + p) % 4)
+
+    def zed_peer(p):
+        return (((zed + p) % 4) * 2 + core, b)
+
+    barrier = pltpu.get_barrier_semaphore()
+    for p in range(1, 8):
+        pl.semaphore_signal(
+            barrier, inc=1, device_id=((s + p) % 8, b), device_id_type=MESH
+        )
+    for p in range(1, 4):
+        pl.semaphore_signal(barrier, inc=1, device_id=batch_peer(p), device_id_type=MESH)
+    pl.semaphore_wait(barrier, 10)
+
+    def remote(src, dst, sems, index, peer, start=True):
+        copy = pltpu.make_async_remote_copy(
+            src_ref=src,
+            dst_ref=dst,
+            send_sem=sems.at[(0,) + index],
+            recv_sem=sems.at[(1,) + index],
+            device_id=peer,
+            device_id_type=MESH,
+        )
+        if start:
+            copy.start()
+        return copy
+
+    edge = remote(
+        tok_ref.at[:, 112:128],
+        halo,
+        halo_sem,
+        (0,),
+        ((s + 1) % 8, b),
+        start=False,
+    )
+
+    @pl.when(s < 7)
+    def _():
+        edge.start()
+
+    moves = {}
+    for p in (1, 2, 3):
+        moves["c", p] = remote(cot_ref, cot.at[b], b_sem, (1, p), batch_peer(p))
+
+    gain, beta = gain_ref[...], beta_ref[...]
+
+    def white_of(x):
+        x = x.astype(f32)
+        centered = x - jnp.mean(x, axis=-1, keepdims=True)
+        inv = lax.rsqrt(jnp.mean(centered * centered, axis=-1, keepdims=True) + epsilon)
+        return centered * inv, inv
+
+    def norm_rows(i, _):
+        q, r = i // 4, (i % 4) * 32
+        rows = lanes(i * 32, 32)
+        w, inv = white_of(tok_ref[q, lanes(r, 32)])
+        white[rows] = w
+        istd[rows] = jnp.broadcast_to(inv, (32, 128))
+        normed[rows] = (w * gain + beta).astype(bf16)
+        return 0
+
+    lax.fori_loop(0, 8, norm_rows, 0)
+
+    @pl.when(s == 0)
+    def _():
+        halo[...] = jnp.zeros_like(halo)
+
+    @pl.when(s > 0)
+    def _():
+        edge.wait_recv()
+
+    w, _inv = white_of(halo[...].reshape(32, 1024))
+    normed[256:288] = (w * gain + beta).astype(bf16)
+
+    pairs = ((gsend, gch), (dsend, dch), (ysend, yrecv), (qsend, qrecv))
+
+    def exchange(kind, p):
+        src, dst = pairs[kind]
+        to = (s + p) % 8
+        return remote(src.at[to], dst.at[s], a_sem, (kind, p), (to, b), start=False)
+
+    def send_tile(kind, tile):
+        p = (tile - s + 8) % 8
+
+        @pl.when(p != 0)
+        def _():
+            exchange(kind, p).start()
+
+        @pl.when(p == 0)
+        def _():
+            src, dst = pairs[kind]
+            dst[s] = src[s]
+
+    def wait_tiles(kind):
+        for p in range(1, 8):
+            exchange(kind, p).wait_recv()
+
+    loads[0].wait()
+
+    def project(i, _):
+        t = (zed + 2 + i) % 4
+        for g in range(3):
+            cols = lanes(g * 1024 + t * 256, 256)
+            m = mm(normed[...], w_in[:, cols]) + bin_ref[:, cols]
+            for h in range(2):
+                at = slice(h * 128, h * 128 + 128)
+                tile = 2 * t + h
+                edge_rows = jnp.concatenate([m[264:272, at], m[280:288, at]], axis=1)
+                mx[g, tile, 0:8] = jnp.where(s > 0, edge_rows, 0.0)
+                mx[g, tile, 8:136] = jnp.concatenate([m[0:128, at], m[128:256, at]], axis=1)
+        for h in range(2):
+            tile = 2 * t + h
+            got = []
+            for g in range(3):
+                cols = lanes(g * 1024 + tile * 128, 128)
+                taps = sw_ref[:, cols]
+                value = (
+                    twice(taps[0:1]) * mx[g, tile, 8:136]
+                    + twice(taps[1:2]) * mx[g, tile, 7:135]
+                    + twice(taps[2:3]) * mx[g, tile, 6:134]
+                    + twice(sb_ref[:, cols])
+                )
+                oiv[g, tile] = value
+                got.append(value)
+            gsend[tile] = (got[2] * got[1]).astype(bf16)
+            send_tile(0, tile)
+        return 0
+
+    lax.fori_loop(0, 4, project, 0)
+
+    loads[1].wait()
+    cot_here = cot_ref[...]
+
+    def backproject(i, _):
+        t = (zed + 2 + i) % 4
+        m = mm(cot_here, w_out[lanes(t * 256, 256)], NT).astype(bf16)
+        for h in range(2):
+            at = slice(h * 128, h * 128 + 128)
+            tile = 2 * t + h
+            value = jnp.concatenate([m[0:128, at], m[128:256, at]], axis=1)
+            dpr[tile] = value
+            dsend[tile] = (value.astype(f32) * oiv[0, tile]).astype(bf16)
+            send_tile(1, tile)
+        return 0
+
+    lax.fori_loop(0, 4, backproject, 0)
+
+    nt[b] = normed[0:256].T
+    for p in (1, 2, 3):
+        moves["n", p] = remote(nt.at[b], nt.at[b], b_sem, (0, p), batch_peer(p))
+    cot[b] = cot_here
+    sa[0] = jnp.zeros(sa.shape[1:], f32)
+    sa[0, 2:3] = jnp.sum(cot_here.astype(f32), axis=0, keepdims=True)
+
+    mine = lanes(s * 128, 128)
+    pos = pos_ref[...]
+    one, one_c = sin_cos(mm_full(pos, w1_ref[...]) + b1_ref[...])
+    first[...] = one
+    first_c[...] = one_c
+    two, two_c = sin_cos(mm_full(one, w2_ref[...]) + b2_ref[...])
+    second[...] = two
+    second_c[...] = two_c
+    fraction = lax.broadcasted_iota(jnp.int32, (1024, 128), 0).astype(f32) * (1.0 / 1024)
+    wind = jnp.exp(-fraction * decay_ref[:, mine])
+    window[...] = wind
+    taps_bf = (mm_full(two, w3_ref[:, mine]) * wind).astype(bf16)
+    loads[2].wait()
+
+    def filter_rows(i, _):
+        rows = lanes(i * 256, 256)
+        ksp[rows] = mm(fm[rows], taps_bf)
+        return 0
+
+    lax.fori_loop(0, 8, filter_rows, 0)
+
+    bias = twice(fb_ref[:, mine])
+    wait_tiles(0)
+    gated = gch[...].reshape(1024, 256)
+
+    def forward_rows(i, _):
+        lo, hi = lanes(i * 256, 256), lanes(1024 + i * 256, 256)
+        gc, gs = mm(fm[lo], gated), mm(fm[hi], gated)
+        kc, ks = twice(ksp[lo]), twice(ksp[hi])
+        gsp[lo] = gc
+        gsp[hi] = gs
+        zs[lo] = (gc * kc - gs * ks).astype(bf16)
+        zs[hi] = (gc * ks + gs * kc).astype(bf16)
+        return 0
+
+    lax.fori_loop(0, 4, forward_rows, 0)
+    loads[3].wait()
+
+    def inverse_to(kind, send, inputs):
+        def rows_of(i, _):
+            t = (zed + 2 + i) % 4
+            y = mm(ft[lanes(t * 256, 256)], zs[...]) * (1.0 / 1024)
+            for h in range(2):
+                tile = 2 * t + h
+                here = y[h * 128 : h * 128 + 128] + bias * inputs[tile].astype(f32)
+                send[tile] = here.astype(bf16)
+                send_tile(kind, tile)
+            return 0
+
+        lax.fori_loop(0, 4, rows_of, 0)
+
+    inverse_to(2, ysend, gch)
+
+    wait_tiles(1)
+    d_here = dch[...].reshape(1024, 256)
+
+    def backward_rows(i, _):
+        lo, hi = lanes(i * 256, 256), lanes(1024 + i * 256, 256)
+        dc, ds = mm(fm[lo], d_here), mm(fm[hi], d_here)
+        kc, ks = twice(ksp[lo]), twice(ksp[hi])
+        gc, gs = gsp[lo], gsp[hi]
+        zs[lo] = (kc * dc + ks * ds).astype(bf16)
+        zs[hi] = (kc * ds - ks * dc).astype(bf16)
+        ec, e_s = gc * dc + gs * ds, gc * ds - gs * dc
+        es[lo] = (ec[:, :128] + ec[:, 128:]).astype(bf16)
+        es[hi] = (e_s[:, :128] + e_s[:, 128:]).astype(bf16)
+        return 0
+
+    lax.fori_loop(0, 4, backward_rows, 0)
+    inverse_to(3, qsend, dch)
+
+    def kernel_rows(i, total):
+        rows = lanes(i * 256, 256)
+        dk[rows] = mm(ft[rows], es[...]) * (1.0 / 1024) * window[rows]
+        for h in range(2):
+            tile = 2 * i + h
+            total += jnp.sum(dch[tile].astype(f32) * gch[tile].astype(f32), axis=0, keepdims=True)
+        return total
+
+    total = lax.fori_loop(0, 4, kernel_rows, jnp.zeros((1, 256), f32))
+    sb[0] = jnp.zeros(sb.shape[1:], f32)
+    sc[0] = jnp.zeros(sc.shape[1:], f32)
+    sb[0, 64:65] = total[:, :128] + total[:, 128:]
+    d_shaped = dk[...]
+    sb[0, 0:64] = mm_full(second[...], d_shaped, TN)
+    d_two = mm_full(d_shaped, w3_ref[:, mine], NT) * second_c[...]
+    sc[0, 40:104, 0:64] = mm_full(first[...], d_two, TN)
+    sc[0, 104:105, 0:64] = jnp.sum(d_two, axis=0, keepdims=True)
+    d_one = mm_full(d_two, w2_ref[...], NT) * first_c[...]
+    sc[0, 0:33, 0:64] = mm_full(pos_ref[...], d_one, TN)
+    sc[0, 105:106, 0:64] = jnp.sum(d_one, axis=0, keepdims=True)
+
+    x, y = b % 2, b // 2
+    steps = [
+        other,
+        (s, y * 2 + 1 - x),
+        (s, (1 - y) * 2 + x),
+        (((zed // 2) * 2 + 1 - zed % 2) * 2 + core, b),
+        (((1 - zed // 2) * 2 + zed % 2) * 2 + core, b),
+    ]
+
+    def small_start(array, which, i, k):
+        return remote(array.at[2 * k], array.at[2 * k + 1], s_sem, (which, i), steps[i])
+
+    def small_end(array, k, move):
+        move.wait()
+        array[2 * k + 2] = array[2 * k] + array[2 * k + 1]
+
+    wait_tiles(2)
+
+    def product_tile(j, _):
+        value = yrecv[j].astype(f32)
+        made = (value * oiv[0, j]).astype(bf16)
+        cols = lanes(j * 128, 128)
+        product[0:128, cols] = made[:, :128]
+        product[128:256, cols] = made[:, 128:]
+        dsx[0, j, 0:128] = dpr[j].astype(f32) * value
+        return 0
+
+    lax.fori_loop(0, 8, product_tile, 0)
+
+    def edges_of(groups, index):
+        return remote(
+            dsx.at[groups, :, 0:8],
+            dsx.at[groups, :, 128:136],
+            halo_sem,
+            (index,),
+            ((s + 7) % 8, b),
+            start=False,
+        )
+
+    def send_edges(groups, index):
+        @pl.when(s > 0)
+        def _():
+            edges_of(groups, index).start()
+
+    def wait_edges(groups, index):
+        @pl.when(s == 7)
+        def _():
+            for g in range(groups.start, groups.stop):
+                for j in range(8):
+                    dsx[g, j, 128:136] = jnp.zeros((8, 256), f32)
+
+        @pl.when(s < 7)
+        def _():
+            edges_of(groups, index).wait_recv()
+
+    send_edges(slice(0, 1), 1)
+    pts[...] = product[...].T.reshape(4, 2, 4, 32, 256)
+    for p in (1, 2, 3):
+        peer, to = batch_peer(p), (b + p) % 4
+        for half in range(2):
+            moves["p", half, p] = remote(
+                pts.at[:, half, to], pt.at[b, half], b_sem, (2 + half, p), peer
+            )
+    for half in range(2):
+        pt[b, half] = pts[:, half, b]
+
+    def out_cols(i, _):
+        cols = lanes(i * 256, 256)
+        r = mm(product[...], w_out[:, cols]) + bout_ref[:, cols]
+        for q in range(2):
+            rows = slice(q * 128, q * 128 + 128)
+            out_ref[q, :, cols] = (tok_ref[q, :, cols].astype(f32) + r[rows]).astype(bf16)
+        return 0
+
+    lax.fori_loop(0, 4, out_cols, 0)
+    wait_edges(slice(0, 1), 1)
+
+    def mixed_tile(g):
+        def one_tile(j, _):
+            q, cols = j // 2, lanes((j % 2) * 128, 128)
+            wide = lanes(g * 1024 + j * 128, 128)
+            narrow = lanes(j * 128, 128)
+            taps = sw_ref[:, wide]
+            here = dsx[g, j, 0:128]
+            value = (
+                twice(taps[0:1]) * here
+                + twice(taps[1:2]) * dsx[g, j, 1:129]
+                + twice(taps[2:3]) * dsx[g, j, 2:130]
+            ).astype(bf16)
+            dms[g, q, 0:128, cols] = value[:, :128]
+            dms[g, q, 128:256, cols] = value[:, 128:]
+
+            def column_sum(v):
+                v = jnp.sum(v, axis=0, keepdims=True)
+                return v[:, :128] + v[:, 128:]
+
+            sa[0, 3 + g : 4 + g, narrow] = column_sum(value.astype(f32))
+            for k in range(3):
+                row = 6 + 3 * k + g
+                sa[0, row : row + 1, narrow] = column_sum(here * mx[g, j, 8 - k : 136 - k])
+            sa[0, 15 + g : 16 + g, narrow] = column_sum(here)
+            return 0
+
+        lax.fori_loop(0, 8, one_tile, 0)
+        for p in (1, 2, 3):
+            to = (b + p) % 4
+            moves["d", g, p] = remote(
+                dms.at[g, to], dm.at[g, b], b_sem, (4 + g, p), batch_peer(p)
+            )
+        dm[g, b] = dms[g, b]
+
+    mixed_tile(0)
+    mb, mc = None, small_start(sc, 1, 0, 0)
+
+    def part_out(half):
+        total = jnp.zeros((128, 1024), f32)
+        for i in range(4):
+            total += mm(pt[i, half].reshape(128, 256), cot[i])
+        return total
+
+    def part_in(g, to, half):
+        rows = lanes(to * 256 + half * 128, 128)
+        total = jnp.zeros((128, 256), f32)
+        for i in range(4):
+            total += mm(nt[i, rows], dm[g, i])
+        return total
+
+    order = (2, 1, 3, 0)
+
+    def done(key):
+        moves[key].wait()
+
+    def core_half(g):
+        for p in (1, 2, 3):
+            done(("d", g, p))
+        for p in order:
+            core_send[g, p] = part_in(g, (zed + p) % 4, 1 - core).astype(bf16)
+            moves["e", g, p] = remote(
+                core_send.at[g, p], core_recv.at[g, p], c_sem, (g, p), other
+            )
+
+    def zed_half(g):
+        for p in order:
+            done(("e", g, p))
+            total = part_in(g, (zed + p) % 4, core) + core_recv[g, p].astype(f32)
+            if p == 0:
+                own[g] = total
+            else:
+                z_send[g, p] = total.astype(bf16)
+                moves["z", g, p] = remote(
+                    z_send.at[g, p], z_recv.at[g, p], zed_sem, (g, p), zed_peer(p)
+                )
+
+    def last_half(g):
+        total = own[g]
+        for p in (2, 1, 3):
+            done(("z", g, p))
+            total += z_recv[g, p].astype(f32)
+        last_send[g] = total.reshape(4, 32, 256)
+        for p in (1, 2, 3):
+            moves["l", g, p] = remote(
+                last_send.at[g, (b + p) % 4], last_recv.at[g, b], l_sem, (g, p), batch_peer(p)
+            )
+        last_recv[g, b] = last_send[g, b]
+
+    for p in (1, 2, 3):
+        for key in (("n", p), ("c", p), ("p", 0, p), ("p", 1, p)):
+            done(key)
+    core_send_o[...] = part_out(1 - core).astype(bf16)
+    moves["co"] = remote(core_send_o, core_recv_o, c_sem, (3, 0), other)
+    core_half(0)
+    small_end(sc, 0, mc)
+    mb, mc = small_start(sb, 0, 1, 0), small_start(sc, 1, 1, 1)
+
+    wait_tiles(3)
+
+    def gate_tile(j, _):
+        value = qrecv[j].astype(f32)
+        dsx[1, j, 0:128] = value * oiv[2, j]
+        dsx[2, j, 0:128] = value * oiv[1, j]
+        return 0
+
+    lax.fori_loop(0, 8, gate_tile, 0)
+    send_edges(slice(1, 3), 2)
+    done("co")
+    out_own = part_out(core) + core_recv_o[...].astype(f32)
+    z_send_o[...] = out_own.astype(bf16).reshape(4, 32, 1024)
+    for p in (2, 1, 3):
+        moves["zo", p] = remote(
+            z_send_o.at[(zed + p) % 4], z_recv_o.at[p], zed_sem, (3, p), zed_peer(p)
+        )
+    wait_edges(slice(1, 3), 2)
+    mixed_tile(1)
+    mixed_tile(2)
+    small_end(sb, 0, mb)
+    small_end(sc, 1, mc)
+    mb, mc = small_start(sb, 0, 2, 1), small_start(sc, 1, 2, 2)
+    zed_half(0)
+
+    def normed_cols(i, _):
+        at = lanes(i * 256, 256)
+        total = jnp.zeros((256, 256), f32)
+        for g in range(3):
+            for q in range(4):
+                c = g * 1024 + q * 256
+                total += mm(dms[g, q], w_in[at, c : c + 256], NT)
+        dn[:, at] = total
+        return 0
+
+    lax.fori_loop(0, 4, normed_cols, 0)
+    core_half(1)
+    core_half(2)
+
+    def token_rows(i, sums):
+        q, r = i // 4, lanes((i % 4) * 32, 32)
+        rows = lanes(i * 32, 32)
+        d, w = dn[rows], white[rows]
+        dw = d * w
+        d_white = d * gain
+        grad = cot_ref[rows].astype(f32) + istd[rows, 0:1] * (
+            d_white
+            - jnp.mean(d_white, axis=-1, keepdims=True)
+            - w * jnp.mean(d_white * w, axis=-1, keepdims=True)
+        )
+        gtok_ref[q, r] = grad
+        return (
+            sums[0] + jnp.sum(dw, axis=0, keepdims=True),
+            sums[1] + jnp.sum(d, axis=0, keepdims=True),
+        )
+
+    zero = jnp.zeros((1, 1024), f32)
+    sums = lax.fori_loop(0, 8, token_rows, (zero, zero))
+    sa[0, 0:1] = sums[0]
+    sa[0, 1:2] = sums[1]
+    ma = small_start(sa, 2, 0, 0)
+    small_end(sb, 1, mb)
+    small_end(sc, 2, mc)
+    mc = small_start(sc, 1, 3, 3)
+    zed_half(1)
+    small_end(sa, 0, ma)
+    ma = small_start(sa, 2, 1, 1)
+    zed_half(2)
+    small_end(sa, 1, ma)
+    ma = small_start(sa, 2, 2, 2)
+    small_end(sc, 3, mc)
+    mc = small_start(sc, 1, 4, 4)
+    total = z_send_o[zed].astype(f32)
+    for p in (2, 1, 3):
+        done(("zo", p))
+        total += z_recv_o[p].astype(f32)
+    gwout_ref[...] = total
+    last_half(0)
+    small_end(sa, 2, ma)
+    ma = small_start(sa, 2, 3, 3)
+    last_half(1)
+    last_half(2)
+    small_end(sa, 3, ma)
+    ma = small_start(sa, 2, 4, 4)
+    small_end(sc, 4, mc)
+    for g in range(3):
+        for p in (1, 2, 3):
+            done(("l", g, p))
+        for i in range(4):
+            gwin_ref[:, g * 1024 + i * 256 : g * 1024 + (i + 1) * 256] = last_recv[g, i]
+    small_end(sa, 4, ma)
+    oa_ref[...] = sa[10]
+    ob_ref[...] = sb[4]
+    oc_ref[...] = sc[10]
+    for kind in range(4):
+        for p in range(1, 8):
+            exchange(kind, p).wait_send()
+
+    @pl.when(s < 7)
+    def _():
+        edge.wait_send()
+
+    @pl.when(s > 0)
+    def _():
+        edges_of(slice(0, 1), 1).wait_send()
+        edges_of(slice(1, 3), 2).wait_send()
+
+
+def whole(args, positions, matrix):
+    vmem, anywhere = (pl.BlockSpec(memory_space=m) for m in (pltpu.VMEM, pl.ANY))
+    dma = pltpu.SemaphoreType.DMA
+    specs = [vmem] * 20
+    for i in (4, 15, 18, 19):
+        specs[i] = anywhere
+    shape = jax.ShapeDtypeStruct
+
+    def v(dtype, *dims):
+        return pltpu.VMEM(dims, dtype)
+
+    return pl.pallas_call(
+        whole_kernel,
+        out_shape=(
+            shape((2, 128, 1024), bf16),
+            shape((2, 128, 1024), f32),
+            shape((32, 3072), f32),
+            shape((32, 1024), f32),
+            shape((24, 1024), f32),
+            shape((72, 128), f32),
+            shape((112, 128), f32),
+        ),
+        in_specs=specs,
+        out_specs=(vmem,) * 7,
+        scratch_shapes=[
+            v(bf16, 1024, 3072),
+            v(bf16, 1024, 1024),
+            v(bf16, 2048, 1024),
+            v(bf16, 1024, 2048),
+            v(bf16, 2, 16, 1024),
+            v(f32, 256, 1024),
+            v(f32, 256, 128),
+            v(bf16, 288, 1024),
+            v(f32, 3, 8, 136, 256),
+            v(f32, 3, 8, 128, 256),
+            v(bf16, 8, 128, 256),
+            v(bf16, 8, 128, 256),
+            v(bf16, 8, 128, 256),
+            v(bf16, 8, 128, 256),
+            v(bf16, 8, 128, 256),
+            v(bf16, 8, 128, 256),
+            v(bf16, 8, 128, 256),
+            v(bf16, 8, 128, 256),
+            v(bf16, 8, 128, 256),
+            v(f32, 1024, 64),
+            v(f32, 1024, 64),
+            v(f32, 1024, 64),
+            v(f32, 1024, 64),
+            v(f32, 1024, 128),
+            v(f32, 2048, 128),
+            v(f32, 2048, 256),
+            v(bf16, 2048, 256),
+            v(bf16, 2048, 128),
+            v(f32, 1024, 128),
+            v(bf16, 256, 1024),
+            v(bf16, 4, 2, 4, 32, 256),
+            v(f32, 3, 8, 136, 256),
+            v(bf16, 3, 4, 256, 256),
+            v(f32, 256, 1024),
+            v(bf16, 4, 1024, 256),
+            v(bf16, 4, 2, 4, 32, 256),
+            v(bf16, 3, 4, 256, 256),
+            v(bf16, 4, 256, 1024),
+            v(bf16, 3, 4, 128, 256),
+            v(bf16, 3, 4, 128, 256),
+            v(bf16, 128, 1024),
+            v(bf16, 128, 1024),
+            v(bf16, 3, 4, 128, 256),
+            v(bf16, 3, 4, 128, 256),
+            v(bf16, 4, 32, 1024),
+            v(bf16, 4, 32, 1024),
+            v(f32, 3, 128, 256),
+            v(f32, 3, 4, 32, 256),
+            v(f32, 3, 4, 32, 256),
+            v(f32, 11, 24, 1024),
+            v(f32, 5, 72, 128),
+            v(f32, 11, 112, 128),
+            dma((4,)),
+            dma((2, 3)),
+            dma((2, 4, 8)),
+            dma((2, 7, 4)),
+            dma((2, 4, 4)),
+            dma((2, 4, 4)),
+            dma((2, 3, 4)),
+            dma((2, 3, 5)),
+        ],
+        compiler_params=pltpu.CompilerParams(
+            collective_id=0, has_side_effects=True, vmem_limit_bytes=63 * 1024 * 1024
+        ),
+    )(*args, positions, matrix, np.ascontiguousarray(matrix.T))
+
+
+def local_small(*args):
+    tokens, cotangent = args[:2]
+    row = lambda v: v.reshape(1, -1)
+    vectors = {2, 3, 5, 7, 9, 11, 13, 14, 16}
+    given = [row(a) if i in vectors else a for i, a in enumerate(args)]
+    given[1] = cotangent.reshape(256, 1024)
+    features, hidden = args[8].shape
+    out, gtok, gwin, gwout, sa, sb, sc = whole(
+        given, position_features(1024, features), dft_matrix(1024)
+    )
+    place = lax.axis_index("seq") * 4 + lax.axis_index("batch")
+    narrow = lax.dynamic_slice_in_dim(sa[:3], place * 32, 32, 1)
+    wide = lax.dynamic_slice_in_dim(sa[3:18].reshape(5, 3072), place * 96, 96, 1)
+    third = lax.dynamic_slice_in_dim(sb, lax.axis_index("batch") * 32, 32, 1)
+    return (
+        out,
+        gtok,
+        narrow[0],
+        narrow[1],
+        gwin,
+        wide[0],
+        wide[1:4],
+        wide[4],
+        sc[0:features, :hidden],
+        sc[105, :hidden],
+        sc[40 : 40 + hidden, :hidden],
+        sc[104, :hidden],
+        third[:hidden],
+        third[hidden],
+        gwout,
+        narrow[2],
+    )
+
+
 def solution(mesh):
     tokens_spec = P("batch", "seq", None)
     both = ("seq", "batch")
@@ -253,4 +1054,11 @@
         P(both, None),
         P(both),
     )
-    return jax.shard_map(local, mesh=mesh, in_specs=in_specs, out_specs=out_specs, check_vma=False)
+
+    def per_device(*args):
+        tokens, w_one = args[0], args[8]
+        sizes = (mesh.shape["seq"], mesh.shape["batch"]) + tokens.shape + w_one.shape
+        fits = sizes == (8, 4, 2, 128, 1024, 33, 64)
+        return (local_small if fits else local)(*args)
+
+    return jax.shard_map(per_device, mesh=mesh, in_specs=in_specs, out_specs=out_specs, check_vma=False)

time: 384 us -> 127 us (0.33); the launches traced: 377 us -> 126 us
  waiting for transfers between devices: 112 us -> 0 us
  Pallas kernels: 0 us -> 109 us
  blocking collectives: 66.6 us -> 0 us
  matrix products: 53.8 us -> 0 us
  local copies, waits for them, and re-layouts: 62.1 us -> 16.3 us
  starting transfers between devices: 43.8 us -> 0 us
  other arithmetic: 37.4 us -> 0 us
    all_to_all x8 -> x0, waiting for transfers between devices: 111 us -> none  [the longest x2 92.9 us: reduce_scatter(): lax.all_to_all(value.astype(dtype), 'batch', split_axis=1, concat_axis=1,...]
    pallas_call x0 -> x1, Pallas kernels: none -> 109 us  [whole(): pl.pallas_call(whole_kernel, out_shape=(shape((2, 128, 1024), bf16), shap...]
    unnamed x1 -> x0, blocking collectives: 66.6 us -> none
    dot_general x21 -> x0, matrix products: 53.8 us -> none  [the longest x3 11.6 us: spectrum(): return jnp.einsum('kt,btc->bkc', matrix, value, preferred_element_type=f32)]
    all_to_all x8 -> x0, starting transfers between devices: 39.7 us -> none  [the longest x2 12.2 us: to_channels(): return lax.all_to_all(value, 'seq', split_axis=2, concat_axis=1, tiled=True)]
    convert_element_type x13 -> x0, local copies, waits for them, and re-layouts: 29.8 us -> none  [the longest x1 7.7 us: reduce_scatter(): value.astype(dtype)]
    reduce_sum x11 -> x0, other arithmetic: 24.3 us -> none  [the longest x2 6.99 us: reduce_scatter(): out = jnp.sum(out.astype(f32), axis=1)]
    concatenate x17 -> x0, local copies, waits for them, and re-layouts: 9.86 us -> none  [the longest x5 6.32 us: local(): jnp.concatenate([g_ln_gain[None], g_ln_bias[None], g_b_out[None], g_filt_...]
  transfers between devices with their start and end apart: 10 -> 0, of which waited for: 5 -> 0; matrix products, arithmetic and copies ran while one was open for 21% -> 0% of each run, Pallas kernels for 0% -> 0%
where the time goes in v2:
time: 127 us; the launch traced here: 126 us
  Pallas kernels  109 us (86%)
  local copies, waits for them, and re-layouts  16.3 us (13%)
    pallas_call x1, Pallas kernels, whole(): pl.pallas_call(whole_kernel, out_shape=(shape((2, 128, 1024), bf16), shap...  109 us
    unnamed x7, local copies, waits for them, and re-layouts  7.28 us

profile of v2, /device:TPU:0, one launch (start us, length us, event | category | flops | bytes accessed | tf_op | source)
XLA Modules:
  0.0 126.2 jit_solution(11378041413642759579)
XLA Ops:
  0.7 109.2 %shard_map.315 = (bf16[2,128,1024]{2,1,0:T(8,128)(2,1)}, f32[2,128,1024]{2,1,0:T(8,128)}, f32[32,3072]{1,0:T(8,128)}, f32[32,1024]{1,0:T(8,128)}, f32[24,1024]{1...) custom-call(bf16[2,128,1024]{2,1,0:T(8,128)(2,1)} %tok_ref.1, bf16[256,1024]{1,0:T(8,128)(2,1)} %bitcast.26, ...), custom_call_target="tpu_custom_call" | custom-call | tf_op jit(solution)/shard_map/pallas_call | solution.py:920
  109.9 0.0 copy-start
  109.9 1.3 %slice_bitcast_fusion.1 = (f32[64]{0:T(128)}, f32[64]{0:T(128)}) fusion(f32[112,128]{1,0:T(8,128)} %get-tuple-element.27), kind=kLoop, calls=%fused_computation.5 | loop fusion | bytes 1024 | tf_op jit(solution)/shard_map/squeeze | solution.py:1027
  111.1 0.8 slice.42
  111.9 0.9 slice.45
  112.8 0.1 constant_dynamic-slice_fusion.2
  112.9 1.3 slice_bitcast_fusion
  114.1 0.8 constant_dynamic-slice_fusion
  115.0 0.7 copy.36
  115.6 1.3 %slice.49 = f32[33,64]{1,0:T(8,128)} slice(f32[112,128]{1,0:T(8,128)} %get-tuple-element.27), slice={[0:33], [0:64]} | slice | bytes 16896 | tf_op jit(solution)/shard_map/slice | solution.py:1024
  117.0 1.4 %slice.51 = f32[64,64]{1,0:T(8,128)} slice(f32[112,128]{1,0:T(8,128)} %get-tuple-element.27), slice={[40:104], [0:64]} | slice | bytes 32768 | tf_op jit(solution)/shard_map/slice | solution.py:1026
  118.4 0.1 constant_dynamic-slice_fusion.1
  118.5 0.5 slice_bitcast_fusion.3
  119.0 0.6 slice.47
  119.6 1.9 %copy.41 = bf16[2,128,1024]{2,1,0:T(8,128)(2,1)} copy(bf16[2,128,1024]{2,1,0:T(8,128)(2,1)} %get-tuple-element.70) | data formatting | bytes 1048576
  121.4 2.3 %copy.42 = f32[2,128,1024]{2,1,0:T(8,128)} copy(f32[2,128,1024]{2,1,0:T(8,128)} %get-tuple-element.71) | data formatting | bytes 2097152
  123.7 1.8 %copy.43 = f32[32,3072]{1,0:T(8,128)} copy(f32[32,3072]{1,0:T(8,128)} %get-tuple-element.74) | data formatting | bytes 786432
  125.5 0.0 copy-done
  125.5 0.7 copy.44
  (1 shorter events, 0.0 us)
Async XLA Ops:
  109.9 15.6 %copy-start = (f32[32,1024]{1,0:T(8,128)S(1)}, f32[32,1024]{1,0:T(8,128)}, u32[]{:S(2)}) copy-start(f32[32,1024]{1,0:T(8,128)} %get-tuple-element.84) | copy-start | bytes 393220

commit v3 on v2

--- a/solution.py
+++ b/solution.py
@@ -318,9 +318,7 @@
     gch,
     dsend,
     dch,
-    ysend,
     yrecv,
-    qsend,
     qrecv,
     first,
     first_c,
@@ -336,7 +334,6 @@
     pts,
     dsx,
     dms,
-    dn,
     nt,
     pt,
     dm,
@@ -345,6 +342,9 @@
     core_recv,
     core_send_o,
     core_recv_o,
+    own_o,
+    outv,
+    gtokv,
     z_send,
     z_recv,
     z_send_o,
@@ -353,9 +353,13 @@
     last_send,
     last_recv,
     sa,
+    sr,
+    sf,
     sb,
     sc,
     load_sem,
+    in_sem,
+    v_sem,
     halo_sem,
     a_sem,
     b_sem,
@@ -370,12 +374,19 @@
 
     loads = [
         pltpu.make_async_copy(src, dst, load_sem.at[i])
-        for i, (src, dst) in enumerate(
-            ((win_ref, w_in), (wout_ref, w_out), (f_ref, fm), (ft_ref, ft))
-        )
+        for i, (src, dst) in enumerate(((wout_ref, w_out), (f_ref, fm), (ft_ref, ft)))
     ]
-    for load in loads:
-        load.start()
+
+    def load_in(g, i):
+        cols = lanes(g * 1024 + (zed + 2 + i) % 4 * 256, 256)
+        return pltpu.make_async_copy(win_ref.at[:, cols], w_in.at[:, cols], in_sem.at[g, i])
+
+    loads[0].start()
+    for i in range(4):
+        for g in range(3):
+            load_in(g, i).start()
+    loads[1].start()
+    loads[2].start()
 
     def batch_peer(p):
         return (s, (b + p) % 4)
@@ -390,7 +401,6 @@
         )
     for p in range(1, 4):
         pl.semaphore_signal(barrier, inc=1, device_id=batch_peer(p), device_id_type=MESH)
-    pl.semaphore_wait(barrier, 10)
 
     def remote(src, dst, sems, index, peer, start=True):
         copy = pltpu.make_async_remote_copy(
@@ -405,6 +415,26 @@
             copy.start()
         return copy
 
+    gain, beta = gain_ref[...], beta_ref[...]
+
+    def white_of(x):
+        x = x.astype(f32)
+        centered = x - jnp.mean(x, axis=-1, keepdims=True)
+        inv = lax.rsqrt(jnp.mean(centered * centered, axis=-1, keepdims=True) + epsilon)
+        return centered * inv, inv
+
+    def norm_rows(i, _):
+        q, r = i // 4, (i % 4) * 32
+        rows = lanes(i * 32, 32)
+        w, inv = white_of(tok_ref[q, lanes(r, 32)])
+        white[rows] = w
+        istd[rows] = jnp.broadcast_to(inv, (32, 128))
+        normed[rows] = (w * gain + beta).astype(bf16)
+        return 0
+
+    lax.fori_loop(0, 8, norm_rows, 0)
+
+    pl.semaphore_wait(barrier, 10)
     edge = remote(
         tok_ref.at[:, 112:128],
         halo,
@@ -418,28 +448,30 @@
     def _():
         edge.start()
 
+    nt[b] = normed[0:256].T
     moves = {}
-    for p in (1, 2, 3):
-        moves["c", p] = remote(cot_ref, cot.at[b], b_sem, (1, p), batch_peer(p))
-
-    gain, beta = gain_ref[...], beta_ref[...]
-
-    def white_of(x):
-        x = x.astype(f32)
-        centered = x - jnp.mean(x, axis=-1, keepdims=True)
-        inv = lax.rsqrt(jnp.mean(centered * centered, axis=-1, keepdims=True) + epsilon)
-        return centered * inv, inv
-
-    def norm_rows(i, _):
-        q, r = i // 4, (i % 4) * 32
-        rows = lanes(i * 32, 32)
-        w, inv = white_of(tok_ref[q, lanes(r, 32)])
-        white[rows] = w
-        istd[rows] = jnp.broadcast_to(inv, (32, 128))
-        normed[rows] = (w * gain + beta).astype(bf16)
+    order = (2, 1, 3, 0)
+    x, y = b % 2, b // 2
+    beside = (y * 2 + 1 - x, (1 - y) * 2 + x)
+    for k in range(2):
+        moves["n", k] = remote(nt.at[b], nt.at[b], b_sem, (0, k), (s, beside[k]))
+    for k in range(2):
+        moves["c", k] = remote(cot_ref, cot.at[b], b_sem, (1, k), (s, beside[k]))
+
+    loads[0].wait()
+    cot_here = cot_ref[...]
+    cot[b] = cot_here
+
+    def backproject(t, _):
+        m = mm(cot_here, w_out[lanes(t * 256, 256)], NT).astype(bf16)
+        for h in range(2):
+            at = slice(h * 128, h * 128 + 128)
+            dpr[2 * t + h] = jnp.concatenate([m[0:128, at], m[128:256, at]], axis=1)
         return 0
 
-    lax.fori_loop(0, 8, norm_rows, 0)
+    lax.fori_loop(0, 4, backproject, 0)
+    sa[...] = jnp.zeros(sa.shape, f32)
+    sa[5:6, 2048:3072] = jnp.sum(cot_here.astype(f32), axis=0, keepdims=True)
 
     @pl.when(s == 0)
     def _():
@@ -452,7 +484,7 @@
     w, _inv = white_of(halo[...].reshape(32, 1024))
     normed[256:288] = (w * gain + beta).astype(bf16)
 
-    pairs = ((gsend, gch), (dsend, dch), (ysend, yrecv), (qsend, qrecv))
+    pairs = ((gsend, gch), (dsend, dch), (gsend, yrecv), (dsend, qrecv))
 
     def exchange(kind, p):
         src, dst = pairs[kind]
@@ -471,15 +503,19 @@
             src, dst = pairs[kind]
             dst[s] = src[s]
 
+    def sent_tiles(kind):
+        for p in range(1, 8):
+            exchange(kind, p).wait_send()
+
     def wait_tiles(kind):
         for p in range(1, 8):
             exchange(kind, p).wait_recv()
 
-    loads[0].wait()
 
     def project(i, _):
         t = (zed + 2 + i) % 4
         for g in range(3):
+            load_in(g, i).wait()
             cols = lanes(g * 1024 + t * 256, 256)
             m = mm(normed[...], w_in[:, cols]) + bin_ref[:, cols]
             for h in range(2):
@@ -504,33 +540,10 @@
                 got.append(value)
             gsend[tile] = (got[2] * got[1]).astype(bf16)
             send_tile(0, tile)
+            dsend[tile] = (dpr[tile].astype(f32) * got[0]).astype(bf16)
         return 0
 
     lax.fori_loop(0, 4, project, 0)
-
-    loads[1].wait()
-    cot_here = cot_ref[...]
-
-    def backproject(i, _):
-        t = (zed + 2 + i) % 4
-        m = mm(cot_here, w_out[lanes(t * 256, 256)], NT).astype(bf16)
-        for h in range(2):
-            at = slice(h * 128, h * 128 + 128)
-            tile = 2 * t + h
-            value = jnp.concatenate([m[0:128, at], m[128:256, at]], axis=1)
-            dpr[tile] = value
-            dsend[tile] = (value.astype(f32) * oiv[0, tile]).astype(bf16)
-            send_tile(1, tile)
-        return 0
-
-    lax.fori_loop(0, 4, backproject, 0)
-
-    nt[b] = normed[0:256].T
-    for p in (1, 2, 3):
-        moves["n", p] = remote(nt.at[b], nt.at[b], b_sem, (0, p), batch_peer(p))
-    cot[b] = cot_here
-    sa[0] = jnp.zeros(sa.shape[1:], f32)
-    sa[0, 2:3] = jnp.sum(cot_here.astype(f32), axis=0, keepdims=True)
 
     mine = lanes(s * 128, 128)
     pos = pos_ref[...]
@@ -544,7 +557,7 @@
     wind = jnp.exp(-fraction * decay_ref[:, mine])
     window[...] = wind
     taps_bf = (mm_full(two, w3_ref[:, mine]) * wind).astype(bf16)
-    loads[2].wait()
+    loads[1].wait()
 
     def filter_rows(i, _):
         rows = lanes(i * 256, 256)
@@ -554,6 +567,8 @@
     lax.fori_loop(0, 8, filter_rows, 0)
 
     bias = twice(fb_ref[:, mine])
+    for i in range(8):
+        send_tile(1, (2 * zed + 4 + i) % 8)
     wait_tiles(0)
     gated = gch[...].reshape(1024, 256)
 
@@ -568,7 +583,7 @@
         return 0
 
     lax.fori_loop(0, 4, forward_rows, 0)
-    loads[3].wait()
+    loads[2].wait()
 
     def inverse_to(kind, send, inputs):
         def rows_of(i, _):
@@ -583,7 +598,19 @@
 
         lax.fori_loop(0, 4, rows_of, 0)
 
-    inverse_to(2, ysend, gch)
+    sent_tiles(0)
+    inverse_to(2, gsend, gch)
+
+    for k in range(2):
+        near, far = beside[k], (s, beside[1 - k])
+        moves["n", k].wait()
+        part = nt.at[near, 512 * k : 512 * k + 512]
+        moves["n", 2 + k] = remote(part, part, b_sem, (0, 2 + k), far)
+    for k in range(2):
+        near, far = beside[k], (s, beside[1 - k])
+        moves["c", k].wait()
+        part = cot.at[near, 128 * k : 128 * k + 128]
+        moves["c", 2 + k] = remote(part, part, b_sem, (1, 2 + k), far)
 
     wait_tiles(1)
     d_here = dch[...].reshape(1024, 256)
@@ -601,7 +628,8 @@
         return 0
 
     lax.fori_loop(0, 4, backward_rows, 0)
-    inverse_to(3, qsend, dch)
+    sent_tiles(1)
+    inverse_to(3, dsend, dch)
 
     def kernel_rows(i, total):
         rows = lanes(i * 256, 256)
@@ -624,7 +652,6 @@
     sc[0, 0:33, 0:64] = mm_full(pos_ref[...], d_one, TN)
     sc[0, 105:106, 0:64] = jnp.sum(d_one, axis=0, keepdims=True)
 
-    x, y = b % 2, b // 2
     steps = [
         other,
         (s, y * 2 + 1 - x),
@@ -690,41 +717,37 @@
     for half in range(2):
         pt[b, half] = pts[:, half, b]
 
-    def out_cols(i, _):
-        cols = lanes(i * 256, 256)
-        r = mm(product[...], w_out[:, cols]) + bout_ref[:, cols]
-        for q in range(2):
-            rows = slice(q * 128, q * 128 + 128)
-            out_ref[q, :, cols] = (tok_ref[q, :, cols].astype(f32) + r[rows]).astype(bf16)
+    def column_sum(v):
+        v = jnp.sum(v, axis=0, keepdims=True)
+        return v[:, :128] + v[:, 128:]
+
+    def short_sums(g, j):
+        wide = lanes(g * 1024 + j * 128, 128)
+        here = dsx[g, j, 0:128]
+        for k in range(3):
+            sa[1 + k : 2 + k, wide] = column_sum(here * mx[g, j, 8 - k : 136 - k])
+        sa[4:5, wide] = column_sum(here)
+
+    def first_sums(j, _):
+        short_sums(0, j)
         return 0
 
-    lax.fori_loop(0, 4, out_cols, 0)
+    lax.fori_loop(0, 8, first_sums, 0)
     wait_edges(slice(0, 1), 1)
 
     def mixed_tile(g):
         def one_tile(j, _):
             q, cols = j // 2, lanes((j % 2) * 128, 128)
             wide = lanes(g * 1024 + j * 128, 128)
-            narrow = lanes(j * 128, 128)
             taps = sw_ref[:, wide]
-            here = dsx[g, j, 0:128]
             value = (
-                twice(taps[0:1]) * here
+                twice(taps[0:1]) * dsx[g, j, 0:128]
                 + twice(taps[1:2]) * dsx[g, j, 1:129]
                 + twice(taps[2:3]) * dsx[g, j, 2:130]
             ).astype(bf16)
             dms[g, q, 0:128, cols] = value[:, :128]
             dms[g, q, 128:256, cols] = value[:, 128:]
-
-            def column_sum(v):
-                v = jnp.sum(v, axis=0, keepdims=True)
-                return v[:, :128] + v[:, 128:]
-
-            sa[0, 3 + g : 4 + g, narrow] = column_sum(value.astype(f32))
-            for k in range(3):
-                row = 6 + 3 * k + g
-                sa[0, row : row + 1, narrow] = column_sum(here * mx[g, j, 8 - k : 136 - k])
-            sa[0, 15 + g : 16 + g, narrow] = column_sum(here)
+            sa[0:1, wide] = column_sum(value.astype(f32))
             return 0
 
         lax.fori_loop(0, 8, one_tile, 0)
@@ -736,7 +759,42 @@
         dm[g, b] = dms[g, b]
 
     mixed_tile(0)
-    mb, mc = None, small_start(sc, 1, 0, 0)
+    mb, mc = small_start(sb, 0, 1, 0), small_start(sc, 1, 0, 0)
+
+    def out_cols(i, _):
+        cols = lanes(i * 256, 256)
+        r = mm(product[...], w_out[:, cols]) + bout_ref[:, cols]
+        for q in range(2):
+            rows = slice(q * 128, q * 128 + 128)
+            outv[q, :, cols] = (tok_ref[q, :, cols].astype(f32) + r[rows]).astype(bf16)
+        return 0
+
+    lax.fori_loop(0, 4, out_cols, 0)
+    store_out = pltpu.make_async_copy(outv, out_ref, load_sem.at[3])
+    store_out.start()
+
+    def normed_cols(groups):
+        def one(i, _):
+            at = lanes(i * 256, 256)
+            total = jnp.zeros((256, 256), f32)
+            for g in groups:
+                for q in range(4):
+                    c = g * 1024 + q * 256
+                    total += mm(dms[g, q], w_in[at, c : c + 256], NT)
+            for q in range(2):
+                rows = slice(q * 128, q * 128 + 128)
+                before = 0.0 if 0 in groups else gtokv[q, :, at]
+                gtokv[q, :, at] = before + total[rows]
+            return 0
+
+        lax.fori_loop(0, 4, one, 0)
+
+    normed_cols((0,))
+    small_end(sc, 0, mc)
+    mc = small_start(sc, 1, 1, 1)
+
+    def done(key):
+        moves[key].wait()
 
     def part_out(half):
         total = jnp.zeros((128, 1024), f32)
@@ -750,11 +808,6 @@
         for i in range(4):
             total += mm(nt[i, rows], dm[g, i])
         return total
-
-    order = (2, 1, 3, 0)
-
-    def done(key):
-        moves[key].wait()
 
     def core_half(g):
         for p in (1, 2, 3):
@@ -782,22 +835,13 @@
         for p in (2, 1, 3):
             done(("z", g, p))
             total += z_recv[g, p].astype(f32)
-        last_send[g] = total.reshape(4, 32, 256)
+        last_send[g] = total.astype(bf16).reshape(4, 32, 256)
         for p in (1, 2, 3):
             moves["l", g, p] = remote(
                 last_send.at[g, (b + p) % 4], last_recv.at[g, b], l_sem, (g, p), batch_peer(p)
             )
         last_recv[g, b] = last_send[g, b]
 
-    for p in (1, 2, 3):
-        for key in (("n", p), ("c", p), ("p", 0, p), ("p", 1, p)):
-            done(key)
-    core_send_o[...] = part_out(1 - core).astype(bf16)
-    moves["co"] = remote(core_send_o, core_recv_o, c_sem, (3, 0), other)
-    core_half(0)
-    small_end(sc, 0, mc)
-    mb, mc = small_start(sb, 0, 1, 0), small_start(sc, 1, 1, 1)
-
     wait_tiles(3)
 
     def gate_tile(j, _):
@@ -808,39 +852,43 @@
 
     lax.fori_loop(0, 8, gate_tile, 0)
     send_edges(slice(1, 3), 2)
+
+    def other_sums(j, _):
+        short_sums(1, j)
+        short_sums(2, j)
+        return 0
+
+    lax.fori_loop(0, 8, other_sums, 0)
+    wait_edges(slice(1, 3), 2)
+    mixed_tile(1)
+    mixed_tile(2)
+    for k in (2, 3):
+        done(("n", k))
+        done(("c", k))
+    for p in (1, 2, 3):
+        done(("p", 0, p))
+        done(("p", 1, p))
+    core_send_o[...] = part_out(1 - core).astype(bf16)
+    moves["co"] = remote(core_send_o, core_recv_o, c_sem, (3, 0), other)
+    core_half(0)
+    small_end(sb, 0, mb)
+    small_end(sc, 1, mc)
+    mb, mc = small_start(sb, 0, 2, 1), small_start(sc, 1, 2, 2)
     done("co")
-    out_own = part_out(core) + core_recv_o[...].astype(f32)
-    z_send_o[...] = out_own.astype(bf16).reshape(4, 32, 1024)
+    own_o[...] = (part_out(core) + core_recv_o[...].astype(f32)).reshape(4, 32, 1024)
+    z_send_o[...] = own_o[...].astype(bf16)
     for p in (2, 1, 3):
         moves["zo", p] = remote(
             z_send_o.at[(zed + p) % 4], z_recv_o.at[p], zed_sem, (3, p), zed_peer(p)
         )
-    wait_edges(slice(1, 3), 2)
-    mixed_tile(1)
-    mixed_tile(2)
-    small_end(sb, 0, mb)
-    small_end(sc, 1, mc)
-    mb, mc = small_start(sb, 0, 2, 1), small_start(sc, 1, 2, 2)
     zed_half(0)
 
-    def normed_cols(i, _):
-        at = lanes(i * 256, 256)
-        total = jnp.zeros((256, 256), f32)
-        for g in range(3):
-            for q in range(4):
-                c = g * 1024 + q * 256
-                total += mm(dms[g, q], w_in[at, c : c + 256], NT)
-        dn[:, at] = total
-        return 0
-
-    lax.fori_loop(0, 4, normed_cols, 0)
-    core_half(1)
-    core_half(2)
+    normed_cols((1, 2))
 
     def token_rows(i, sums):
         q, r = i // 4, lanes((i % 4) * 32, 32)
         rows = lanes(i * 32, 32)
-        d, w = dn[rows], white[rows]
+        d, w = gtokv[q, r], white[rows]
         dw = d * w
         d_white = d * gain
         grad = cot_ref[rows].astype(f32) + istd[rows, 0:1] * (
@@ -848,7 +896,7 @@
             - jnp.mean(d_white, axis=-1, keepdims=True)
             - w * jnp.mean(d_white * w, axis=-1, keepdims=True)
         )
-        gtok_ref[q, r] = grad
+        gtokv[q, r] = grad
         return (
             sums[0] + jnp.sum(dw, axis=0, keepdims=True),
             sums[1] + jnp.sum(d, axis=0, keepdims=True),
@@ -856,45 +904,59 @@
 
     zero = jnp.zeros((1, 1024), f32)
     sums = lax.fori_loop(0, 8, token_rows, (zero, zero))
-    sa[0, 0:1] = sums[0]
-    sa[0, 1:2] = sums[1]
-    ma = small_start(sa, 2, 0, 0)
+    store_tok = pltpu.make_async_copy(gtokv, gtok_ref, load_sem.at[4])
+    store_tok.start()
+    sa[5:6, 0:1024] = sums[0]
+    sa[5:6, 1024:2048] = sums[1]
+
+    def half_at(k):
+        return lanes(k * 1536, 1536)
+
+    vec = remote(sa.at[:, half_at(1 - core)], sr.at[0], v_sem, (0,), other)
     small_end(sb, 1, mb)
     small_end(sc, 2, mc)
     mc = small_start(sc, 1, 3, 3)
+    core_half(1)
+    vec.wait()
+    sr[1] = sa[:, half_at(core)] + sr[0]
+    vecs = [remote(sr.at[1], sr.at[1 + p], v_sem, (p,), batch_peer(p)) for p in (1, 2, 3)]
     zed_half(1)
-    small_end(sa, 0, ma)
-    ma = small_start(sa, 2, 1, 1)
+    core_half(2)
+    for vec in vecs:
+        vec.wait()
+    sr[5] = sr[1] + sr[2] + sr[3] + sr[4]
+    vecs = [remote(sr.at[5], sr.at[5 + p], v_sem, (3 + p,), zed_peer(p)) for p in (1, 2, 3)]
     zed_half(2)
-    small_end(sa, 1, ma)
-    ma = small_start(sa, 2, 2, 2)
     small_end(sc, 3, mc)
     mc = small_start(sc, 1, 4, 4)
-    total = z_send_o[zed].astype(f32)
+    total = own_o[zed]
     for p in (2, 1, 3):
         done(("zo", p))
         total += z_recv_o[p].astype(f32)
     gwout_ref[...] = total
     last_half(0)
-    small_end(sa, 2, ma)
-    ma = small_start(sa, 2, 3, 3)
+    for vec in vecs:
+        vec.wait()
+    oa_ref[:, half_at(core)] = sr[5] + sr[6] + sr[7] + sr[8]
+    sf[...] = sr[5] + sr[6] + sr[7] + sr[8]
+    vec = remote(sf, sr.at[9], v_sem, (7,), other)
     last_half(1)
     last_half(2)
-    small_end(sa, 3, ma)
-    ma = small_start(sa, 2, 4, 4)
     small_end(sc, 4, mc)
+    vec.wait()
+    oa_ref[:, half_at(1 - core)] = sr[9]
+    ob_ref[...] = sb[4]
+    oc_ref[...] = sc[10]
     for g in range(3):
         for p in (1, 2, 3):
             done(("l", g, p))
         for i in range(4):
-            gwin_ref[:, g * 1024 + i * 256 : g * 1024 + (i + 1) * 256] = last_recv[g, i]
-    small_end(sa, 4, ma)
-    oa_ref[...] = sa[10]
-    ob_ref[...] = sb[4]
-    oc_ref[...] = sc[10]
-    for kind in range(4):
-        for p in range(1, 8):
-            exchange(kind, p).wait_send()
+            c = g * 1024 + i * 256
+            gwin_ref[:, c : c + 256] = last_recv[g, i].astype(f32)
+    store_out.wait()
+    store_tok.wait()
+    sent_tiles(2)
+    sent_tiles(3)
 
     @pl.when(s < 7)
     def _():
@@ -924,12 +986,12 @@
             shape((2, 128, 1024), f32),
             shape((32, 3072), f32),
             shape((32, 1024), f32),
-            shape((24, 1024), f32),
+            shape((8, 3072), f32),
             shape((72, 128), f32),
             shape((112, 128), f32),
         ),
         in_specs=specs,
-        out_specs=(vmem,) * 7,
+        out_specs=(anywhere,) * 2 + (vmem,) * 5,
         scratch_shapes=[
             v(bf16, 1024, 3072),
             v(bf16, 1024, 1024),
@@ -941,8 +1003,6 @@
             v(bf16, 288, 1024),
             v(f32, 3, 8, 136, 256),
             v(f32, 3, 8, 128, 256),
-            v(bf16, 8, 128, 256),
-            v(bf16, 8, 128, 256),
             v(bf16, 8, 128, 256),
             v(bf16, 8, 128, 256),
             v(bf16, 8, 128, 256),
@@ -964,7 +1024,6 @@
             v(bf16, 4, 2, 4, 32, 256),
             v(f32, 3, 8, 136, 256),
             v(bf16, 3, 4, 256, 256),
-            v(f32, 256, 1024),
             v(bf16, 4, 1024, 256),
             v(bf16, 4, 2, 4, 32, 256),
             v(bf16, 3, 4, 256, 256),
@@ -973,17 +1032,24 @@
             v(bf16, 3, 4, 128, 256),
             v(bf16, 128, 1024),
             v(bf16, 128, 1024),
+            v(f32, 4, 32, 1024),
+            v(bf16, 2, 128, 1024),
+            v(f32, 2, 128, 1024),
             v(bf16, 3, 4, 128, 256),
             v(bf16, 3, 4, 128, 256),
             v(bf16, 4, 32, 1024),
             v(bf16, 4, 32, 1024),
             v(f32, 3, 128, 256),
-            v(f32, 3, 4, 32, 256),
-            v(f32, 3, 4, 32, 256),
-            v(f32, 11, 24, 1024),
+            v(bf16, 3, 4, 32, 256),
+            v(bf16, 3, 4, 32, 256),
+            v(f32, 8, 3072),
+            v(f32, 10, 8, 1536),
+            v(f32, 8, 1536),
             v(f32, 5, 72, 128),
             v(f32, 11, 112, 128),
-            dma((4,)),
+            dma((5,)),
+            dma((3, 4)),
+            dma((2, 8)),
             dma((2, 3)),
             dma((2, 4, 8)),
             dma((2, 7, 4)),
@@ -998,38 +1064,101 @@
     )(*args, positions, matrix, np.ascontiguousarray(matrix.T))
 
 
+def settle_kernel(
+    out_ref,
+    gtok_ref,
+    gwin_ref,
+    gwout_ref,
+    sa_ref,
+    sb_ref,
+    sc_ref,
+    out,
+    gtok,
+    ln_gain,
+    ln_bias,
+    gwin,
+    b_in,
+    short_w,
+    short_b,
+    w_one,
+    b_one,
+    w_two,
+    b_two,
+    w_three,
+    filt,
+    gwout,
+    b_out,
+    sems,
+):
+    copies = [
+        pltpu.make_async_copy(src, dst, sems.at[i])
+        for i, (src, dst) in enumerate(
+            ((out_ref, out), (gtok_ref, gtok), (gwin_ref, gwin), (gwout_ref, gwout))
+        )
+    ]
+    for copy in copies:
+        copy.start()
+    b = lax.axis_index("batch")
+    place = lax.axis_index("seq") * 4 + b
+    sa = sa_ref[...]
+    wide = pltpu.roll(sa, (32 - place) * 96, 1)
+    b_in[...] = wide[0:1, :96]
+    short_w[...] = wide[1:4, :96]
+    short_b[...] = wide[4:5, :96]
+    thin = pltpu.roll(sa, (96 - place) * 32, 1)
+    ln_gain[...] = thin[5:6, 0:32]
+    ln_bias[...] = thin[5:6, 1024:1056]
+    b_out[...] = thin[5:6, 2048:2080]
+    third = pltpu.roll(sb_ref[...], (4 - b) * 32, 1)
+    w_three[...] = third[0:64, 0:32]
+    filt[...] = third[64:65, 0:32]
+    w_one[...] = sc_ref[0:33, 0:64]
+    w_two[...] = sc_ref[40:104, 0:64]
+    b_two[...] = sc_ref[104:105, 0:64]
+    b_one[...] = sc_ref[105:106, 0:64]
+    for copy in copies:
+        copy.wait()
+
+
+def settle(parts):
+    vmem, anywhere = (pl.BlockSpec(memory_space=m) for m in (pltpu.VMEM, pl.ANY))
+    sizes = (
+        (2, 128, 1024),
+        (2, 128, 1024),
+        (1, 32),
+        (1, 32),
+        (32, 3072),
+        (1, 96),
+        (3, 96),
+        (1, 96),
+        (33, 64),
+        (1, 64),
+        (64, 64),
+        (1, 64),
+        (64, 32),
+        (1, 32),
+        (32, 1024),
+        (1, 32),
+    )
+    flat = (2, 3, 5, 7, 9, 11, 13, 15)
+    outs = pl.pallas_call(
+        settle_kernel,
+        out_shape=tuple(
+            jax.ShapeDtypeStruct(size, f32 if i else bf16) for i, size in enumerate(sizes)
+        ),
+        in_specs=[anywhere] * 4 + [vmem] * 3,
+        out_specs=(vmem,) * 16,
+        scratch_shapes=[pltpu.SemaphoreType.DMA((4,))],
+    )(*parts)
+    return tuple(o.reshape(-1) if i in flat else o for i, o in enumerate(outs))
+
+
 def local_small(*args):
-    tokens, cotangent = args[:2]
-    row = lambda v: v.reshape(1, -1)
+    cotangent = args[1]
     vectors = {2, 3, 5, 7, 9, 11, 13, 14, 16}
-    given = [row(a) if i in vectors else a for i, a in enumerate(args)]
+    given = [a.reshape(1, -1) if i in vectors else a for i, a in enumerate(args)]
     given[1] = cotangent.reshape(256, 1024)
-    features, hidden = args[8].shape
-    out, gtok, gwin, gwout, sa, sb, sc = whole(
-        given, position_features(1024, features), dft_matrix(1024)
-    )
-    place = lax.axis_index("seq") * 4 + lax.axis_index("batch")
-    narrow = lax.dynamic_slice_in_dim(sa[:3], place * 32, 32, 1)
-    wide = lax.dynamic_slice_in_dim(sa[3:18].reshape(5, 3072), place * 96, 96, 1)
-    third = lax.dynamic_slice_in_dim(sb, lax.axis_index("batch") * 32, 32, 1)
-    return (
-        out,
-        gtok,
-        narrow[0],
-        narrow[1],
-        gwin,
-        wide[0],
-        wide[1:4],
-        wide[4],
-        sc[0:features, :hidden],
-        sc[105, :hidden],
-        sc[40 : 40 + hidden, :hidden],
-        sc[104, :hidden],
-        third[:hidden],
-        third[hidden],
-        gwout,
-        narrow[2],
-    )
+    return settle(whole(given, position_features(1024, args[8].shape[0]), dft_matrix(1024)))
 
 
 def solution(mesh):

time: 127 us -> 108 us (0.85)
  local copies, waits for them, and re-layouts: 16.3 us -> 1.44 us
  Pallas kernels: 109 us -> 106 us
    pallas_call x1, Pallas kernels: 109 us -> 102 us  [whole(): pl.pallas_call(whole_kernel, out_shape=(shape((2, 128, 1024), bf16), shap...]
    unnamed x7 -> x1, local copies, waits for them, and re-layouts: 7.28 us -> 1.44 us
    slice x6 -> x0, local copies, waits for them, and re-layouts: 5.78 us -> none  [the longest x1 1.37 us: local_small(): sc[40:40 + hidden, :hidden]]
    pallas_call x0 -> x1, Pallas kernels: none -> 3.84 us  [settle(): pl.pallas_call(settle_kernel, out_shape=tuple((jax.ShapeDtypeStruct(size,...]
    squeeze x3 -> x0, local copies, waits for them, and re-layouts: 3.04 us -> none  [the longest x1 1.27 us: local_small(): sc[104, :hidden]]
where the time goes in v3:
time: 108 us
  Pallas kernels  106 us (98%)
  local copies, waits for them, and re-layouts  1.44 us (1%)
    pallas_call x1, Pallas kernels, whole(): pl.pallas_call(whole_kernel, out_shape=(shape((2, 128, 1024), bf16), shap...  102 us
    pallas_call x1, Pallas kernels, settle(): pl.pallas_call(settle_kernel, out_shape=tuple((jax.ShapeDtypeStruct(size,...  3.84 us

profile of v3, /device:TPU:0, one launch (start us, length us, event | category | flops | bytes accessed | tf_op | source)
XLA Modules:
  0.0 107.7 jit_solution(4816724594519724157)
XLA Ops:
  0.7 101.7 %shard_map.315 = (bf16[2,128,1024]{2,1,0:T(8,128)(2,1)}, f32[2,128,1024]{2,1,0:T(8,128)}, f32[32,3072]{1,0:T(8,128)}, f32[32,1024]{1,0:T(8,128)}, f32[8,3072]{1,...) custom-call(bf16[2,128,1024]{2,1,0:T(8,128)(2,1)} %tok_ref.1, bf16[256,1024]{1,0:T(8,128)(2,1)} %bitcast.18, ...), custom_call_target="tpu_custom_call" | custom-call | tf_op jit(solution)/shard_map/pallas_call | solution.py:982
  102.4 3.8 %shard_map.316 = (bf16[2,128,1024]{2,1,0:T(8,128)(2,1)}, f32[2,128,1024]{2,1,0:T(8,128)}, f32[1,32]{1,0:T(1,128)}, f32[1,32]{1,0:T(1,128)}, f32[32,3072]{1,0:T(8...) custom-call(bf16[2,128,1024]{2,1,0:T(8,128)(2,1)} %get-tuple-element, ...), custom_call_target="tpu_custom_call" | custom-call | tf_op jit(solution)/shard_map/pallas_call | solution.py:1144
  106.3 1.4 %copy.36 = f32[64,32]{0,1:T(8,128)} copy(f32[64,32]{1,0:T(8,128)} %get-tuple-element.74) | data formatting | bytes 16384

commit v4 on v3

--- a/solution.py
+++ b/solution.py
@@ -314,22 +314,21 @@
     mx,
     oiv,
     dpr,
-    gsend,
-    gch,
-    dsend,
-    dch,
-    yrecv,
-    qrecv,
+    a1,
+    a2,
+    xs,
+    yo,
+    yx,
+    r1s,
+    r1,
+    r2,
     first,
-    first_c,
     second,
-    second_c,
     window,
     ksp,
-    gsp,
+    xsp,
     zs,
     es,
-    dk,
     product,
     pts,
     dsx,
@@ -345,18 +344,20 @@
     own_o,
     outv,
     gtokv,
-    z_send,
     z_recv,
-    z_send_o,
     z_recv_o,
-    own,
     last_send,
     last_recv,
     sa,
     sr,
     sf,
     sb,
+    sp,
+    vb,
+    sg,
     sc,
+    sq,
+    sh,
     load_sem,
     in_sem,
     v_sem,
@@ -366,10 +367,12 @@
     c_sem,
     zed_sem,
     l_sem,
-    s_sem,
 ):
     s, b = lax.axis_index("seq"), lax.axis_index("batch")
     zed, core = s // 2, s % 2
+    side, quarter = s // 4, s % 4
+    pair, cross = zed // 2 * 2 + 1 - zed % 2, (zed + 2) % 4
+    pair_cross = (pair + 2) % 4
     other = (zed * 2 + 1 - core, b)
 
     loads = [
@@ -378,7 +381,7 @@
     ]
 
     def load_in(g, i):
-        cols = lanes(g * 1024 + (zed + 2 + i) % 4 * 256, 256)
+        cols = lanes(g * 1024 + (quarter + 2 + i) % 4 * 256, 256)
         return pltpu.make_async_copy(win_ref.at[:, cols], w_in.at[:, cols], in_sem.at[g, i])
 
     loads[0].start()
@@ -448,9 +451,9 @@
     def _():
         edge.start()
 
-    nt[b] = normed[0:256].T
+    nt[b] = normed[0:256].T.reshape(4, 2, 128, 256)
     moves = {}
-    order = (2, 1, 3, 0)
+    shards = (pair_cross, pair, cross, zed)
     x, y = b % 2, b // 2
     beside = (y * 2 + 1 - x, (1 - y) * 2 + x)
     for k in range(2):
@@ -484,15 +487,23 @@
     w, _inv = white_of(halo[...].reshape(32, 1024))
     normed[256:288] = (w * gain + beta).astype(bf16)
 
-    pairs = ((gsend, gch), (dsend, dch), (gsend, yrecv), (dsend, qrecv))
-
     def exchange(kind, p):
-        src, dst = pairs[kind]
-        to = (s + p) % 8
-        return remote(src.at[to], dst.at[s], a_sem, (kind, p), (to, b), start=False)
-
-    def send_tile(kind, tile):
-        p = (tile - s + 8) % 8
+        to = (quarter + p) % 4
+        target = side * 4 + to
+        if kind == 0:
+            src, dst = a1.at[to], xs.at[quarter]
+        elif kind == 1:
+            src, dst, target = a1.at[to], yx.at[quarter], (1 - side) * 4 + to
+        elif kind == 2:
+            src, dst = a2.at[to], yo.at[quarter]
+        else:
+            u = (kind - 3) % 2
+            send, recv = ((r1s, r1), (a2, r2))[(kind - 3) // 2]
+            src, dst = send.at[to, u], recv.at[2 * quarter + u]
+        return remote(src, dst, a_sem, (kind, p), (target, b), start=False)
+
+    def send_to(kind, to):
+        p = (to - quarter + 4) % 4
 
         @pl.when(p != 0)
         def _():
@@ -500,20 +511,26 @@
 
         @pl.when(p == 0)
         def _():
-            src, dst = pairs[kind]
-            dst[s] = src[s]
+            if kind == 0:
+                xs[quarter] = a1[quarter]
+            elif kind == 2:
+                yo[quarter] = a2[quarter]
+            else:
+                u = (kind - 3) % 2
+                send, recv = ((r1s, r1), (a2, r2))[(kind - 3) // 2]
+                recv[2 * quarter + u] = send[quarter, u]
 
     def sent_tiles(kind):
-        for p in range(1, 8):
+        for p in range(0 if kind == 1 else 1, 4):
             exchange(kind, p).wait_send()
 
     def wait_tiles(kind):
-        for p in range(1, 8):
+        for p in range(0 if kind == 1 else 1, 4):
             exchange(kind, p).wait_recv()
 
 
     def project(i, _):
-        t = (zed + 2 + i) % 4
+        t = (quarter + 2 + i) % 4
         for g in range(3):
             load_in(g, i).wait()
             cols = lanes(g * 1024 + t * 256, 256)
@@ -538,22 +555,23 @@
                 )
                 oiv[g, tile] = value
                 got.append(value)
-            gsend[tile] = (got[2] * got[1]).astype(bf16)
-            send_tile(0, tile)
-            dsend[tile] = (dpr[tile].astype(f32) * got[0]).astype(bf16)
+            gated = got[2] * got[1]
+            d_summed = dpr[tile].astype(f32) * got[0]
+            a1[t, h] = jnp.where(side == 0, gated, d_summed).astype(bf16)
+            a2[t, h] = jnp.where(side == 0, d_summed, gated).astype(bf16)
+        exchange(1, (t - quarter + 4) % 4).start()
+        send_to(0, t)
         return 0
 
     lax.fori_loop(0, 4, project, 0)
 
-    mine = lanes(s * 128, 128)
+    mine = lanes(quarter * 256, 256)
     pos = pos_ref[...]
     one, one_c = sin_cos(mm_full(pos, w1_ref[...]) + b1_ref[...])
-    first[...] = one
-    first_c[...] = one_c
+    first[...] = jnp.concatenate([one, one_c], axis=1)
     two, two_c = sin_cos(mm_full(one, w2_ref[...]) + b2_ref[...])
-    second[...] = two
-    second_c[...] = two_c
-    fraction = lax.broadcasted_iota(jnp.int32, (1024, 128), 0).astype(f32) * (1.0 / 1024)
+    second[...] = jnp.concatenate([two, two_c], axis=1)
+    fraction = lax.broadcasted_iota(jnp.int32, (1024, 256), 0).astype(f32) * (1.0 / 1024)
     wind = jnp.exp(-fraction * decay_ref[:, mine])
     window[...] = wind
     taps_bf = (mm_full(two, w3_ref[:, mine]) * wind).astype(bf16)
@@ -566,119 +584,96 @@
 
     lax.fori_loop(0, 8, filter_rows, 0)
 
-    bias = twice(fb_ref[:, mine])
-    for i in range(8):
-        send_tile(1, (2 * zed + 4 + i) % 8)
+    turn = jnp.where(side == 0, 1.0, -1.0)
+    bias = fb_ref[:, mine]
+    here = side * 512
+    near, far_half = lanes(here, 512), lanes(512 - here, 512)
     wait_tiles(0)
-    gated = gch[...].reshape(1024, 256)
-
-    def forward_rows(i, _):
-        lo, hi = lanes(i * 256, 256), lanes(1024 + i * 256, 256)
-        gc, gs = mm(fm[lo], gated), mm(fm[hi], gated)
-        kc, ks = twice(ksp[lo]), twice(ksp[hi])
-        gsp[lo] = gc
-        gsp[hi] = gs
-        zs[lo] = (gc * kc - gs * ks).astype(bf16)
-        zs[hi] = (gc * ks + gs * kc).astype(bf16)
-        return 0
-
-    lax.fori_loop(0, 4, forward_rows, 0)
-    loads[2].wait()
-
-    def inverse_to(kind, send, inputs):
-        def rows_of(i, _):
-            t = (zed + 2 + i) % 4
-            y = mm(ft[lanes(t * 256, 256)], zs[...]) * (1.0 / 1024)
+    for p in range(4):
+        send_to(2, (quarter + p + 2) % 4)
+
+    def inverse_to(kind, u, send, given):
+        for k in range(2):
+            y = mm(ft[lanes(here + k * 256, 256)], zs[...]) * (1.0 / 1024)
             for h in range(2):
-                tile = 2 * t + h
-                here = y[h * 128 : h * 128 + 128] + bias * inputs[tile].astype(f32)
-                send[tile] = here.astype(bf16)
-                send_tile(kind, tile)
+                block = 2 * k + h
+                scale = twice(bias[:, u * 128 : u * 128 + 128])
+                value = y[h * 128 : h * 128 + 128] + scale * given[block, u].astype(f32)
+                send[block, u] = value.astype(bf16)
+        for k in range(4):
+            send_to(kind + u, (quarter + 2 + k) % 4)
+
+    for u in range(2):
+        at = slice(u * 128, u * 128 + 128)
+        x_u = xs[:, u].reshape(512, 256)
+
+        def first_rows(i, _):
+            lo, hi = lanes(i * 256, 256), lanes(1024 + i * 256, 256)
+            xc, x_s = mm(fm[lo, near], x_u), mm(fm[hi, near], x_u)
+            kc, ks = twice(ksp[lo, at]), twice(ksp[hi, at] * turn)
+            xsp[u, lo] = xc.astype(bf16)
+            xsp[u, hi] = x_s.astype(bf16)
+            zs[lo] = (kc * xc - ks * x_s).astype(bf16)
+            zs[hi] = (kc * x_s + ks * xc).astype(bf16)
             return 0
 
-        lax.fori_loop(0, 4, rows_of, 0)
-
-    sent_tiles(0)
-    inverse_to(2, gsend, gch)
+        lax.fori_loop(0, 4, first_rows, 0)
+        if u == 0:
+            loads[2].wait()
+        inverse_to(3, u, r1s, xs)
 
     for k in range(2):
-        near, far = beside[k], (s, beside[1 - k])
+        by, on = beside[k], (s, beside[1 - k])
         moves["n", k].wait()
-        part = nt.at[near, 512 * k : 512 * k + 512]
-        moves["n", 2 + k] = remote(part, part, b_sem, (0, 2 + k), far)
+        part = nt.at[by, 2 * k : 2 * k + 2]
+        moves["n", 2 + k] = remote(part, part, b_sem, (0, 2 + k), on)
     for k in range(2):
-        near, far = beside[k], (s, beside[1 - k])
+        by, on = beside[k], (s, beside[1 - k])
         moves["c", k].wait()
-        part = cot.at[near, 128 * k : 128 * k + 128]
-        moves["c", 2 + k] = remote(part, part, b_sem, (1, 2 + k), far)
-
+        part = cot.at[by, 128 * k : 128 * k + 128]
+        moves["c", 2 + k] = remote(part, part, b_sem, (1, 2 + k), on)
+
+    wait_tiles(2)
     wait_tiles(1)
-    d_here = dch[...].reshape(1024, 256)
-
-    def backward_rows(i, _):
-        lo, hi = lanes(i * 256, 256), lanes(1024 + i * 256, 256)
-        dc, ds = mm(fm[lo], d_here), mm(fm[hi], d_here)
-        kc, ks = twice(ksp[lo]), twice(ksp[hi])
-        gc, gs = gsp[lo], gsp[hi]
-        zs[lo] = (kc * dc + ks * ds).astype(bf16)
-        zs[hi] = (kc * ds - ks * dc).astype(bf16)
-        ec, e_s = gc * dc + gs * ds, gc * ds - gs * dc
-        es[lo] = (ec[:, :128] + ec[:, 128:]).astype(bf16)
-        es[hi] = (e_s[:, :128] + e_s[:, 128:]).astype(bf16)
-        return 0
-
-    lax.fori_loop(0, 4, backward_rows, 0)
-    sent_tiles(1)
-    inverse_to(3, dsend, dch)
-
-    def kernel_rows(i, total):
-        rows = lanes(i * 256, 256)
-        dk[rows] = mm(ft[rows], es[...]) * (1.0 / 1024) * window[rows]
-        for h in range(2):
-            tile = 2 * i + h
-            total += jnp.sum(dch[tile].astype(f32) * gch[tile].astype(f32), axis=0, keepdims=True)
-        return total
-
-    total = lax.fori_loop(0, 4, kernel_rows, jnp.zeros((1, 256), f32))
-    sb[0] = jnp.zeros(sb.shape[1:], f32)
-    sc[0] = jnp.zeros(sc.shape[1:], f32)
-    sb[0, 64:65] = total[:, :128] + total[:, 128:]
-    d_shaped = dk[...]
-    sb[0, 0:64] = mm_full(second[...], d_shaped, TN)
-    d_two = mm_full(d_shaped, w3_ref[:, mine], NT) * second_c[...]
-    sc[0, 40:104, 0:64] = mm_full(first[...], d_two, TN)
-    sc[0, 104:105, 0:64] = jnp.sum(d_two, axis=0, keepdims=True)
-    d_one = mm_full(d_two, w2_ref[...], NT) * first_c[...]
-    sc[0, 0:33, 0:64] = mm_full(pos_ref[...], d_one, TN)
-    sc[0, 105:106, 0:64] = jnp.sum(d_one, axis=0, keepdims=True)
-
-    steps = [
-        other,
-        (s, y * 2 + 1 - x),
-        (s, (1 - y) * 2 + x),
-        (((zed // 2) * 2 + 1 - zed % 2) * 2 + core, b),
-        (((1 - zed // 2) * 2 + zed % 2) * 2 + core, b),
-    ]
-
-    def small_start(array, which, i, k):
-        return remote(array.at[2 * k], array.at[2 * k + 1], s_sem, (which, i), steps[i])
-
-    def small_end(array, k, move):
-        move.wait()
-        array[2 * k + 2] = array[2 * k] + array[2 * k + 1]
-
-    wait_tiles(2)
-
-    def product_tile(j, _):
-        value = yrecv[j].astype(f32)
-        made = (value * oiv[0, j]).astype(bf16)
-        cols = lanes(j * 128, 128)
-        product[0:128, cols] = made[:, :128]
-        product[128:256, cols] = made[:, 128:]
-        dsx[0, j, 0:128] = dpr[j].astype(f32) * value
-        return 0
-
-    lax.fori_loop(0, 8, product_tile, 0)
+    sent_tiles(2)
+    for u in range(2):
+        at = slice(u * 128, u * 128 + 128)
+        y_near = yo[:, u].reshape(512, 256)
+        y_far = yx[:, u].reshape(512, 256)
+
+        def second_rows(i, _):
+            lo, hi = lanes(i * 256, 256), lanes(1024 + i * 256, 256)
+            nc, n_s = mm(fm[lo, near], y_near), mm(fm[hi, near], y_near)
+            yc = nc + mm(fm[lo, far_half], y_far)
+            y_s = n_s + mm(fm[hi, far_half], y_far)
+            kc, ks = twice(ksp[lo, at]), twice(ksp[hi, at] * turn)
+            zs[lo] = (kc * yc + ks * y_s).astype(bf16)
+            zs[hi] = (kc * y_s - ks * yc).astype(bf16)
+            pc = jnp.where(side == 0, nc, yc)
+            p_s = jnp.where(side == 0, n_s, y_s)
+            xc, x_s = xsp[u, lo].astype(f32), xsp[u, hi].astype(f32)
+            ec, e_s = xc * pc + x_s * p_s, (xc * p_s - x_s * pc) * turn
+            es[lo, at] = (ec[:, :128] + ec[:, 128:]).astype(bf16)
+            es[hi, at] = (e_s[:, :128] + e_s[:, 128:]).astype(bf16)
+            return 0
+
+        lax.fori_loop(0, 4, second_rows, 0)
+        inverse_to(5, u, a2, yo)
+
+    def product_moves(half, p):
+        return remote(
+            pts.at[:, half, (b + p) % 4],
+            pt.at[b, half],
+            b_sem,
+            (2 + half, p),
+            batch_peer(p),
+            start=False,
+        )
+
+    def mixed_moves(g, p):
+        return remote(
+            dms.at[g, (b + p) % 4], dm.at[g, b], b_sem, (4 + g, p), batch_peer(p), start=False
+        )
 
     def edges_of(groups, index):
         return remote(
@@ -706,34 +701,21 @@
         def _():
             edges_of(groups, index).wait_recv()
 
-    send_edges(slice(0, 1), 1)
-    pts[...] = product[...].T.reshape(4, 2, 4, 32, 256)
-    for p in (1, 2, 3):
-        peer, to = batch_peer(p), (b + p) % 4
-        for half in range(2):
-            moves["p", half, p] = remote(
-                pts.at[:, half, to], pt.at[b, half], b_sem, (2 + half, p), peer
-            )
-    for half in range(2):
-        pt[b, half] = pts[:, half, b]
-
     def column_sum(v):
         v = jnp.sum(v, axis=0, keepdims=True)
         return v[:, :128] + v[:, 128:]
 
-    def short_sums(g, j):
-        wide = lanes(g * 1024 + j * 128, 128)
-        here = dsx[g, j, 0:128]
-        for k in range(3):
-            sa[1 + k : 2 + k, wide] = column_sum(here * mx[g, j, 8 - k : 136 - k])
-        sa[4:5, wide] = column_sum(here)
-
-    def first_sums(j, _):
-        short_sums(0, j)
-        return 0
-
-    lax.fori_loop(0, 8, first_sums, 0)
-    wait_edges(slice(0, 1), 1)
+    def short_sums(groups):
+        def one_tile(j, _):
+            for g in groups:
+                wide = lanes(g * 1024 + j * 128, 128)
+                value = dsx[g, j, 0:128]
+                for k in range(3):
+                    sa[1 + k : 2 + k, wide] = column_sum(value * mx[g, j, 8 - k : 136 - k])
+                sa[4:5, wide] = column_sum(value)
+            return 0
+
+        lax.fori_loop(0, 8, one_tile, 0)
 
     def mixed_tile(g):
         def one_tile(j, _):
@@ -751,139 +733,112 @@
             return 0
 
         lax.fori_loop(0, 8, one_tile, 0)
+        dm[g, b] = dms[g, b]
+
+    def send_mixed(g):
         for p in (1, 2, 3):
-            to = (b + p) % 4
-            moves["d", g, p] = remote(
-                dms.at[g, to], dm.at[g, b], b_sem, (4 + g, p), batch_peer(p)
-            )
-        dm[g, b] = dms[g, b]
-
-    mixed_tile(0)
-    mb, mc = small_start(sb, 0, 1, 0), small_start(sc, 1, 0, 0)
-
-    def out_cols(i, _):
-        cols = lanes(i * 256, 256)
-        r = mm(product[...], w_out[:, cols]) + bout_ref[:, cols]
-        for q in range(2):
-            rows = slice(q * 128, q * 128 + 128)
-            outv[q, :, cols] = (tok_ref[q, :, cols].astype(f32) + r[rows]).astype(bf16)
-        return 0
-
-    lax.fori_loop(0, 4, out_cols, 0)
+            mixed_moves(g, p).start()
+
+    def send_product():
+        for half in range(2):
+            for p in (1, 2, 3):
+                product_moves(half, p).start()
+
     store_out = pltpu.make_async_copy(outv, out_ref, load_sem.at[3])
-    store_out.start()
-
-    def normed_cols(groups):
-        def one(i, _):
-            at = lanes(i * 256, 256)
-            total = jnp.zeros((256, 256), f32)
-            for g in groups:
-                for q in range(4):
-                    c = g * 1024 + q * 256
-                    total += mm(dms[g, q], w_in[at, c : c + 256], NT)
+
+    def with_summed(back, early):
+        def product_tile(j, _):
+            value = back[j].astype(f32)
+            made = (value * oiv[0, j]).astype(bf16)
+            cols = lanes(j * 128, 128)
+            product[0:128, cols] = made[:, :128]
+            product[128:256, cols] = made[:, 128:]
+            dsx[0, j, 0:128] = dpr[j].astype(f32) * value
+            return 0
+
+        lax.fori_loop(0, 8, product_tile, 0)
+        send_edges(slice(0, 1), 1)
+        pts[...] = product[...].T.reshape(4, 2, 4, 32, 256)
+        send_product()
+        for half in range(2):
+            pt[b, half] = pts[:, half, b]
+        short_sums((0,))
+
+        @pl.when(s != 3)
+        def _():
+            wait_edges(slice(0, 1), 1)
+            mixed_tile(0)
+            if early:
+                send_mixed(0)
+
+        def out_cols(i, _):
+            cols = lanes(i * 256, 256)
+            r = mm(product[...], w_out[:, cols]) + bout_ref[:, cols]
             for q in range(2):
                 rows = slice(q * 128, q * 128 + 128)
-                before = 0.0 if 0 in groups else gtokv[q, :, at]
-                gtokv[q, :, at] = before + total[rows]
+                outv[q, :, cols] = (tok_ref[q, :, cols].astype(f32) + r[rows]).astype(bf16)
             return 0
 
-        lax.fori_loop(0, 4, one, 0)
-
-    normed_cols((0,))
-    small_end(sc, 0, mc)
-    mc = small_start(sc, 1, 1, 1)
-
-    def done(key):
-        moves[key].wait()
-
-    def part_out(half):
-        total = jnp.zeros((128, 1024), f32)
-        for i in range(4):
-            total += mm(pt[i, half].reshape(128, 256), cot[i])
-        return total
-
-    def part_in(g, to, half):
-        rows = lanes(to * 256 + half * 128, 128)
-        total = jnp.zeros((128, 256), f32)
-        for i in range(4):
-            total += mm(nt[i, rows], dm[g, i])
-        return total
-
-    def core_half(g):
-        for p in (1, 2, 3):
-            done(("d", g, p))
-        for p in order:
-            core_send[g, p] = part_in(g, (zed + p) % 4, 1 - core).astype(bf16)
-            moves["e", g, p] = remote(
-                core_send.at[g, p], core_recv.at[g, p], c_sem, (g, p), other
-            )
-
-    def zed_half(g):
-        for p in order:
-            done(("e", g, p))
-            total = part_in(g, (zed + p) % 4, core) + core_recv[g, p].astype(f32)
-            if p == 0:
-                own[g] = total
-            else:
-                z_send[g, p] = total.astype(bf16)
-                moves["z", g, p] = remote(
-                    z_send.at[g, p], z_recv.at[g, p], zed_sem, (g, p), zed_peer(p)
-                )
-
-    def last_half(g):
-        total = own[g]
-        for p in (2, 1, 3):
-            done(("z", g, p))
-            total += z_recv[g, p].astype(f32)
-        last_send[g] = total.astype(bf16).reshape(4, 32, 256)
-        for p in (1, 2, 3):
-            moves["l", g, p] = remote(
-                last_send.at[g, (b + p) % 4], last_recv.at[g, b], l_sem, (g, p), batch_peer(p)
-            )
-        last_recv[g, b] = last_send[g, b]
+        lax.fori_loop(0, 4, out_cols, 0)
+        store_out.start()
+
+    def with_gated(back, early):
+        def gate_tile(j, _):
+            value = back[j].astype(f32)
+            dsx[1, j, 0:128] = value * oiv[2, j]
+            dsx[2, j, 0:128] = value * oiv[1, j]
+            return 0
+
+        lax.fori_loop(0, 8, gate_tile, 0)
+        send_edges(slice(1, 3), 2)
+        short_sums((1, 2))
+        wait_edges(slice(1, 3), 2)
+        mixed_tile(1)
+        send_mixed(1)
+        mixed_tile(2)
+        if early:
+            send_mixed(2)
+
+        @pl.when(s == 3)
+        def _():
+            wait_edges(slice(0, 1), 1)
+            mixed_tile(0)
+            send_mixed(0)
 
     wait_tiles(3)
-
-    def gate_tile(j, _):
-        value = qrecv[j].astype(f32)
-        dsx[1, j, 0:128] = value * oiv[2, j]
-        dsx[2, j, 0:128] = value * oiv[1, j]
+    wait_tiles(4)
+
+    @pl.when(side == 0)
+    def _():
+        with_summed(r1, True)
+
+    @pl.when(side == 1)
+    def _():
+        with_gated(r1, True)
+
+    wait_tiles(5)
+    wait_tiles(6)
+
+    @pl.when(side == 0)
+    def _():
+        with_gated(r2, False)
+
+    @pl.when(side == 1)
+    def _():
+        with_summed(r2, False)
+
+    def normed_cols(i, _):
+        at = lanes(i * 256, 256)
+        total = jnp.zeros((256, 256), f32)
+        for g in range(3):
+            for q in range(4):
+                c = g * 1024 + q * 256
+                total += mm(dms[g, q], w_in[at, c : c + 256], NT)
+        for q in range(2):
+            gtokv[q, :, at] = total[q * 128 : q * 128 + 128]
         return 0
 
-    lax.fori_loop(0, 8, gate_tile, 0)
-    send_edges(slice(1, 3), 2)
-
-    def other_sums(j, _):
-        short_sums(1, j)
-        short_sums(2, j)
-        return 0
-
-    lax.fori_loop(0, 8, other_sums, 0)
-    wait_edges(slice(1, 3), 2)
-    mixed_tile(1)
-    mixed_tile(2)
-    for k in (2, 3):
-        done(("n", k))
-        done(("c", k))
-    for p in (1, 2, 3):
-        done(("p", 0, p))
-        done(("p", 1, p))
-    core_send_o[...] = part_out(1 - core).astype(bf16)
-    moves["co"] = remote(core_send_o, core_recv_o, c_sem, (3, 0), other)
-    core_half(0)
-    small_end(sb, 0, mb)
-    small_end(sc, 1, mc)
-    mb, mc = small_start(sb, 0, 2, 1), small_start(sc, 1, 2, 2)
-    done("co")
-    own_o[...] = (part_out(core) + core_recv_o[...].astype(f32)).reshape(4, 32, 1024)
-    z_send_o[...] = own_o[...].astype(bf16)
-    for p in (2, 1, 3):
-        moves["zo", p] = remote(
-            z_send_o.at[(zed + p) % 4], z_recv_o.at[p], zed_sem, (3, p), zed_peer(p)
-        )
-    zed_half(0)
-
-    normed_cols((1, 2))
+    lax.fori_loop(0, 4, normed_cols, 0)
 
     def token_rows(i, sums):
         q, r = i // 4, lanes((i % 4) * 32, 32)
@@ -909,54 +864,270 @@
     sa[5:6, 0:1024] = sums[0]
     sa[5:6, 1024:2048] = sums[1]
 
+    def part_out(half):
+        total = jnp.zeros((128, 1024), f32)
+        for i in range(4):
+            total += mm(pt[i, half].reshape(128, 256), cot[i])
+        return total
+
+    def part_in(g, half):
+        total = jnp.zeros((512, 256), f32)
+        for i in range(4):
+            total += mm(nt[i, :, half].reshape(512, 256), dm[g, i])
+        return total
+
+    def shard_of(g, z):
+        return lanes(g * 512 + z * 128, 128)
+
+    beside_z, across_z = (pair * 2 + core, b), (cross * 2 + core, b)
+
+    def core_move(g):
+        return remote(core_send.at[g], core_recv.at[g], c_sem, (g, 0), other, start=False)
+
+    def zed_move(g, k):
+        to = across_z if k == 2 else beside_z
+        src = core_send.at[g, shards[k]]
+        return remote(src, z_recv.at[g, k], zed_sem, (g, k), to, start=False)
+
+    def core_move_o():
+        return remote(core_send_o, core_recv_o, c_sem, (3, 0), other, start=False)
+
+    def zed_move_o(k):
+        to = across_z if k == 2 else beside_z
+        src = core_send_o.at[32 * k : 32 * k + 32]
+        return remote(src, z_recv_o.at[k], zed_sem, (3, k), to, start=False)
+
+    def core_half_o():
+        core_send_o[...] = part_out(1 - core).astype(bf16)
+        core_move_o().start()
+
+    def core_half(g):
+        core_send[g] = part_in(g, 1 - core).astype(bf16).reshape(4, 128, 256)
+        core_move(g).start()
+
+    def zed_half_o():
+        total = part_out(core)
+        core_move_o().wait()
+        own_o[...] = (total + core_recv_o[...].astype(f32)).reshape(4, 32, 1024)
+        for k in range(2):
+            core_send_o[32 * k : 32 * k + 32] = own_o[shards[k]].astype(bf16)
+            zed_move_o(k).start()
+
+    def zed_half(g):
+        total = part_in(g, core)
+        core_move(g).wait()
+        ksp[512 * g : 512 * g + 512] = total + core_recv[g].astype(f32).reshape(512, 256)
+        for k in range(2):
+            core_send[g, shards[k]] = ksp[shard_of(g, shards[k])].astype(bf16)
+            zed_move(g, k).start()
+
+    def cross_half_o():
+        zed_move_o(0).wait()
+        core_send_o[64:96] = (own_o[cross] + z_recv_o[0].astype(f32)).astype(bf16)
+        zed_move_o(2).start()
+
+    def cross_half(g):
+        zed_move(g, 0).wait()
+        total = ksp[shard_of(g, cross)] + z_recv[g, 0].astype(f32)
+        core_send[g, cross] = total.astype(bf16)
+        zed_move(g, 2).start()
+
+    def last_half(g):
+        zed_move(g, 1).wait()
+        zed_move(g, 2).wait()
+        total = ksp[shard_of(g, zed)] + z_recv[g, 1].astype(f32) + z_recv[g, 2].astype(f32)
+        last_send[g] = total.astype(bf16).reshape(4, 32, 256)
+        for p in (1, 2, 3):
+            moves["l", g, p] = remote(
+                last_send.at[g, (b + p) % 4], last_recv.at[g, b], l_sem, (g, p), batch_peer(p)
+            )
+        last_recv[g, b] = last_send[g, b]
+
     def half_at(k):
         return lanes(k * 1536, 1536)
 
-    vec = remote(sa.at[:, half_at(1 - core)], sr.at[0], v_sem, (0,), other)
-    small_end(sb, 1, mb)
-    small_end(sc, 2, mc)
-    mc = small_start(sc, 1, 3, 3)
-    core_half(1)
-    vec.wait()
-    sr[1] = sa[:, half_at(core)] + sr[0]
-    vecs = [remote(sr.at[1], sr.at[1 + p], v_sem, (p,), batch_peer(p)) for p in (1, 2, 3)]
-    zed_half(1)
-    core_half(2)
-    for vec in vecs:
-        vec.wait()
-    sr[5] = sr[1] + sr[2] + sr[3] + sr[4]
-    vecs = [remote(sr.at[5], sr.at[5 + p], v_sem, (3 + p,), zed_peer(p)) for p in (1, 2, 3)]
-    zed_half(2)
-    small_end(sc, 3, mc)
-    mc = small_start(sc, 1, 4, 4)
-    total = own_o[zed]
-    for p in (2, 1, 3):
-        done(("zo", p))
-        total += z_recv_o[p].astype(f32)
-    gwout_ref[...] = total
+    def kernel_rows(i, _):
+        rows = lanes(i * 256, 256)
+        window[rows] = mm(ft[rows], es[...]) * (1.0 / 1024) * window[rows]
+        return 0
+
+    lax.fori_loop(0, 4, kernel_rows, 0)
+    sb[...] = jnp.zeros(sb.shape, f32)
+    sc[...] = jnp.zeros(sc.shape, f32)
+    for u in range(2):
+        both = xs[:, u].astype(f32) * yo[:, u].astype(f32)
+        both = jnp.sum(both.reshape(512, 256), axis=0, keepdims=True)
+        sb[64:65, u * 128 : u * 128 + 128] = both[:, :128] + both[:, 128:]
+    def low(v):
+        return v.astype(bf16)
+
+    d_shaped = low(window[...])
+    sb[0:64] = mm(low(second[:, 0:64]), d_shaped, TN)
+    d_two = mm(d_shaped, low(w3_ref[:, mine]), NT) * second[:, 64:128]
+    sc[0:64, 64:128] = mm(low(first[:, 0:64]), low(d_two), TN)
+    sc[40:41, 0:64] = jnp.sum(d_two, axis=0, keepdims=True)
+    d_one = mm(low(d_two), low(w2_ref[...]), NT) * first[:, 64:128]
+    sc[0:33, 0:64] = mm(low(pos_ref[...]), low(d_one), TN)
+    sc[41:42, 0:64] = jnp.sum(d_one, axis=0, keepdims=True)
+    def rows_at(k):
+        return pl.ds(pl.multiple_of(k * 32, 32), 32)
+
+    def small_remote(src, dst, index, peer):
+        return remote(src, dst, v_sem, (index,), peer)
+
+    smalls = [
+        small_remote(sa.at[:, half_at(1 - core)], sr.at[0], 0, other),
+        small_remote(sc.at[rows_at(1 - core)], sq.at[8], 1, other),
+    ]
+    for k in (2, 3):
+        moves["n", k].wait()
+        moves["c", k].wait()
+
+    def arrived(g):
+        for p in (1, 2, 3):
+            mixed_moves(g, p).wait()
+
+    def arrived_o():
+        for p in (1, 2, 3):
+            product_moves(0, p).wait()
+            product_moves(1, p).wait()
+
+    @pl.when(side == 0)
+    def _():
+        arrived_o()
+        send_mixed(2)
+        core_half_o()
+        arrived(0)
+        core_half(0)
+        zed_half_o()
+        zed_half(0)
+
+    @pl.when(side == 1)
+    def _():
+        arrived(1)
+        send_mixed(0)
+        core_half(1)
+        arrived(2)
+        core_half(2)
+        zed_half(1)
+        zed_half(2)
+
+    for move in smalls:
+        move.wait()
+    def fold(v):
+        return jnp.concatenate([v[:, :768], v[:, 768:]], axis=0).astype(bf16)
+
+    def total_of(array, first):
+        return sum(array[first + i].astype(f32) for i in range(1, 4)) + array[first].astype(f32)
+
+    vb[b] = fold(sa[:, half_at(core)] + sr[0])
+    sq[b] = sc[rows_at(core)] + sq[8]
+    sp[b] = sb[...].astype(bf16)
+    smalls = []
+    for p in (1, 2, 3):
+        smalls += [
+            small_remote(vb.at[b], vb.at[b], 1 + p, batch_peer(p)),
+            small_remote(sq.at[b], sq.at[b], 4 + p, batch_peer(p)),
+            small_remote(sp.at[b], sp.at[b], 7 + p, batch_peer(p)),
+        ]
+
+    @pl.when(side == 0)
+    def _():
+        arrived(1)
+        core_half(1)
+        cross_half_o()
+        cross_half(0)
+        zed_half(1)
+
+    @pl.when(side == 1)
+    def _():
+        arrived_o()
+        core_half_o()
+        cross_half(1)
+        cross_half(2)
+        zed_half_o()
+
+    for move in smalls:
+        move.wait()
+    vb[4 + zed] = total_of(vb, 0).astype(bf16)
+    sq[4 + zed] = total_of(sq, 0)
+    sb[...] = total_of(sp, 0)
+    sp[4] = sb[...].astype(bf16)
+    smalls = [small_remote(sp.at[4], sp.at[5], 17, across_z)]
+    for p in (1, 2, 3):
+        smalls += [
+            small_remote(vb.at[4 + zed], vb.at[4 + zed], 10 + p, zed_peer(p)),
+            small_remote(sq.at[4 + zed], sq.at[4 + zed], 13 + p, zed_peer(p)),
+        ]
+    @pl.when(side == 0)
+    def _():
+        arrived(2)
+        core_half(2)
+        cross_half(1)
+        zed_half(2)
+        cross_half(2)
+
+    @pl.when(side == 1)
+    def _():
+        arrived(0)
+        core_half(0)
+        cross_half_o()
+        zed_half(0)
+        cross_half(0)
+
+    for move in smalls:
+        move.wait()
+    sb[...] = sb[...] + sp[5].astype(f32)
+    folded = total_of(vb, 4)
+    sf[...] = jnp.concatenate([folded[:8], folded[8:]], axis=1)
+    sh[...] = total_of(sq, 4)
+    smalls = [
+        small_remote(sf, sr.at[1], 18, other),
+        small_remote(sh, sq.at[9], 19, other),
+    ]
+    owner = quarter * 2 + side
+
+    def give():
+        return remote(
+            sb.at[:, lanes(side * 128, 128)], sg, v_sem, (20,), (owner, b), start=False
+        )
+
+    @pl.when(owner != s)
+    def _():
+        give().start()
+
+    @pl.when(owner == s)
+    def _():
+        sg[...] = sb[:, lanes(side * 128, 128)]
+
     last_half(0)
-    for vec in vecs:
-        vec.wait()
-    oa_ref[:, half_at(core)] = sr[5] + sr[6] + sr[7] + sr[8]
-    sf[...] = sr[5] + sr[6] + sr[7] + sr[8]
-    vec = remote(sf, sr.at[9], v_sem, (7,), other)
+    zed_move_o(1).wait()
+    zed_move_o(2).wait()
+    gwout_ref[...] = own_o[zed] + z_recv_o[1].astype(f32) + z_recv_o[2].astype(f32)
     last_half(1)
     last_half(2)
-    small_end(sc, 4, mc)
-    vec.wait()
-    oa_ref[:, half_at(1 - core)] = sr[9]
-    ob_ref[...] = sb[4]
-    oc_ref[...] = sc[10]
+    for move in smalls:
+        move.wait()
+    oa_ref[:, half_at(core)] = sf[...]
+    oa_ref[:, half_at(1 - core)] = sr[1]
+    oc_ref[rows_at(core)] = sh[...]
+    oc_ref[rows_at(1 - core)] = sq[9]
+
+    @pl.when(owner != s)
+    def _():
+        give().wait()
+
+    ob_ref[...] = sg[...]
     for g in range(3):
         for p in (1, 2, 3):
-            done(("l", g, p))
+            moves["l", g, p].wait()
         for i in range(4):
             c = g * 1024 + i * 256
             gwin_ref[:, c : c + 256] = last_recv[g, i].astype(f32)
     store_out.wait()
     store_tok.wait()
-    sent_tiles(2)
-    sent_tiles(3)
+    for kind in (0, 1, 3, 4, 5, 6):
+        sent_tiles(kind)
 
     @pl.when(s < 7)
     def _():
@@ -987,8 +1158,8 @@
             shape((32, 3072), f32),
             shape((32, 1024), f32),
             shape((8, 3072), f32),
-            shape((72, 128), f32),
-            shape((112, 128), f32),
+            shape((80, 128), f32),
+            shape((64, 128), f32),
         ),
         in_specs=specs,
         out_specs=(anywhere,) * 2 + (vmem,) * 5,
@@ -1004,27 +1175,26 @@
             v(f32, 3, 8, 136, 256),
             v(f32, 3, 8, 128, 256),
             v(bf16, 8, 128, 256),
+            v(bf16, 4, 2, 128, 256),
+            v(bf16, 4, 2, 128, 256),
+            v(bf16, 4, 2, 128, 256),
+            v(bf16, 4, 2, 128, 256),
+            v(bf16, 4, 2, 128, 256),
+            v(bf16, 4, 2, 128, 256),
             v(bf16, 8, 128, 256),
             v(bf16, 8, 128, 256),
-            v(bf16, 8, 128, 256),
-            v(bf16, 8, 128, 256),
-            v(bf16, 8, 128, 256),
-            v(bf16, 8, 128, 256),
-            v(f32, 1024, 64),
-            v(f32, 1024, 64),
-            v(f32, 1024, 64),
-            v(f32, 1024, 64),
             v(f32, 1024, 128),
-            v(f32, 2048, 128),
+            v(f32, 1024, 128),
+            v(f32, 1024, 256),
             v(f32, 2048, 256),
+            v(bf16, 2, 2048, 256),
             v(bf16, 2048, 256),
-            v(bf16, 2048, 128),
-            v(f32, 1024, 128),
+            v(bf16, 2048, 256),
             v(bf16, 256, 1024),
             v(bf16, 4, 2, 4, 32, 256),
             v(f32, 3, 8, 136, 256),
             v(bf16, 3, 4, 256, 256),
-            v(bf16, 4, 1024, 256),
+            v(bf16, 4, 4, 2, 128, 256),
             v(bf16, 4, 2, 4, 32, 256),
             v(bf16, 3, 4, 256, 256),
             v(bf16, 4, 256, 1024),
@@ -1035,28 +1205,29 @@
             v(f32, 4, 32, 1024),
             v(bf16, 2, 128, 1024),
             v(f32, 2, 128, 1024),
-            v(bf16, 3, 4, 128, 256),
-            v(bf16, 3, 4, 128, 256),
-            v(bf16, 4, 32, 1024),
-            v(bf16, 4, 32, 1024),
-            v(f32, 3, 128, 256),
+            v(bf16, 3, 3, 128, 256),
+            v(bf16, 3, 32, 1024),
             v(bf16, 3, 4, 32, 256),
             v(bf16, 3, 4, 32, 256),
             v(f32, 8, 3072),
-            v(f32, 10, 8, 1536),
+            v(f32, 2, 8, 1536),
             v(f32, 8, 1536),
-            v(f32, 5, 72, 128),
-            v(f32, 11, 112, 128),
+            v(f32, 80, 256),
+            v(bf16, 6, 80, 256),
+            v(bf16, 8, 16, 768),
+            v(f32, 80, 128),
+            v(f32, 64, 128),
+            v(f32, 10, 32, 128),
+            v(f32, 32, 128),
             dma((5,)),
             dma((3, 4)),
-            dma((2, 8)),
+            dma((2, 21)),
             dma((2, 3)),
-            dma((2, 4, 8)),
+            dma((2, 7, 4)),
             dma((2, 7, 4)),
             dma((2, 4, 4)),
             dma((2, 4, 4)),
             dma((2, 3, 4)),
-            dma((2, 3, 5)),
         ],
         compiler_params=pltpu.CompilerParams(
             collective_id=0, has_side_effects=True, vmem_limit_bytes=63 * 1024 * 1024
@@ -1110,12 +1281,12 @@
     ln_bias[...] = thin[5:6, 1024:1056]
     b_out[...] = thin[5:6, 2048:2080]
     third = pltpu.roll(sb_ref[...], (4 - b) * 32, 1)
-    w_three[...] = third[0:64, 0:32]
+    w_three[...] = third.T[0:32, 0:64]
     filt[...] = third[64:65, 0:32]
     w_one[...] = sc_ref[0:33, 0:64]
-    w_two[...] = sc_ref[40:104, 0:64]
-    b_two[...] = sc_ref[104:105, 0:64]
-    b_one[...] = sc_ref[105:106, 0:64]
+    w_two[...] = sc_ref[0:64, 64:128]
+    b_two[...] = sc_ref[40:41, 0:64]
+    b_one[...] = sc_ref[41:42, 0:64]
     for copy in copies:
         copy.wait()
 
@@ -1135,7 +1306,7 @@
         (1, 64),
         (64, 64),
         (1, 64),
-        (64, 32),
+        (32, 64),
         (1, 32),
         (32, 1024),
         (1, 32),
@@ -1150,7 +1321,9 @@
         out_specs=(vmem,) * 16,
         scratch_shapes=[pltpu.SemaphoreType.DMA((4,))],
     )(*parts)
-    return tuple(o.reshape(-1) if i in flat else o for i, o in enumerate(outs))
+    return tuple(
+        o.reshape(-1) if i in flat else o.T if i == 12 else o for i, o in enumerate(outs)
+    )
 
 
 def local_small(*args):

time: 108 us -> 102 us (0.944)
  Pallas kernels: 106 us -> 101 us
  local copies, waits for them, and re-layouts: 1.44 us -> 0 us
    pallas_call x1, Pallas kernels: 102 us -> 96.8 us  [whole(): pl.pallas_call(whole_kernel, out_shape=(shape((2, 128, 1024), bf16), shap...]
    unnamed x1 -> x0, local copies, waits for them, and re-layouts: 1.44 us -> none
where the time goes in v4:
time: 102 us; the launch traced here: 101 us
  Pallas kernels  101 us (99%)
    pallas_call x1, Pallas kernels, whole(): pl.pallas_call(whole_kernel, out_shape=(shape((2, 128, 1024), bf16), shap...  96.8 us
    pallas_call x1, Pallas kernels, settle(): pl.pallas_call(settle_kernel, out_shape=tuple((jax.ShapeDtypeStruct(size,...  3.87 us

profile of v4, /device:TPU:0, one launch (start us, length us, event | category | flops | bytes accessed | tf_op | source)
XLA Modules:
  0.0 101.5 jit_solution(16801298592678444106)
XLA Ops:
  0.7 96.8 %shard_map.315 = (bf16[2,128,1024]{2,1,0:T(8,128)(2,1)}, f32[2,128,1024]{2,1,0:T(8,128)}, f32[32,3072]{1,0:T(8,128)}, f32[32,1024]{1,0:T(8,128)}, f32[8,3072]{1,...) custom-call(bf16[2,128,1024]{2,1,0:T(8,128)(2,1)} %tok_ref.1, bf16[256,1024]{1,0:T(8,128)(2,1)} %bitcast.19, ...), custom_call_target="tpu_custom_call" | custom-call | tf_op jit(solution)/shard_map/pallas_call | solution.py:1153
  97.4 3.9 %shard_map.316 = (bf16[2,128,1024]{2,1,0:T(8,128)(2,1)}, f32[2,128,1024]{2,1,0:T(8,128)}, f32[1,32]{1,0:T(1,128)}, f32[1,32]{1,0:T(1,128)}, f32[32,3072]{1,0:T(8...) custom-call(bf16[2,128,1024]{2,1,0:T(8,128)(2,1)} %get-tuple-element, ...), custom_call_target="tpu_custom_call" | custom-call | tf_op jit(solution)/shard_map/pallas_call | solution.py:1315

commit v5 on v4

--- a/solution.py
+++ b/solution.py
@@ -357,6 +357,7 @@
     sg,
     sc,
     sq,
+    st,
     sh,
     load_sem,
     in_sem,
@@ -946,23 +947,32 @@
     def half_at(k):
         return lanes(k * 1536, 1536)
 
+    @pl.when(side == 0)
+    def _():
+        send_mixed(2)
+
+    @pl.when(side == 1)
+    def _():
+        send_mixed(0)
+
     def kernel_rows(i, _):
         rows = lanes(i * 256, 256)
         window[rows] = mm(ft[rows], es[...]) * (1.0 / 1024) * window[rows]
         return 0
 
     lax.fori_loop(0, 4, kernel_rows, 0)
-    sb[...] = jnp.zeros(sb.shape, f32)
     sc[...] = jnp.zeros(sc.shape, f32)
+    direct = []
     for u in range(2):
         both = xs[:, u].astype(f32) * yo[:, u].astype(f32)
-        both = jnp.sum(both.reshape(512, 256), axis=0, keepdims=True)
-        sb[64:65, u * 128 : u * 128 + 128] = both[:, :128] + both[:, 128:]
+        direct.append(column_sum(both.reshape(512, 256)))
+    direct = jnp.broadcast_to(jnp.concatenate(direct, axis=1), (64, 256)).T
+
     def low(v):
         return v.astype(bf16)
 
     d_shaped = low(window[...])
-    sb[0:64] = mm(low(second[:, 0:64]), d_shaped, TN)
+    sb[...] = jnp.concatenate([mm(d_shaped, low(second[:, 0:64]), TN), direct], axis=1)
     d_two = mm(d_shaped, low(w3_ref[:, mine]), NT) * second[:, 64:128]
     sc[0:64, 64:128] = mm(low(first[:, 0:64]), low(d_two), TN)
     sc[40:41, 0:64] = jnp.sum(d_two, axis=0, keepdims=True)
@@ -977,7 +987,7 @@
 
     smalls = [
         small_remote(sa.at[:, half_at(1 - core)], sr.at[0], 0, other),
-        small_remote(sc.at[rows_at(1 - core)], sq.at[8], 1, other),
+        small_remote(sc.at[rows_at(1 - core)], st.at[0], 1, other),
     ]
     for k in (2, 3):
         moves["n", k].wait()
@@ -995,7 +1005,6 @@
     @pl.when(side == 0)
     def _():
         arrived_o()
-        send_mixed(2)
         core_half_o()
         arrived(0)
         core_half(0)
@@ -1005,7 +1014,6 @@
     @pl.when(side == 1)
     def _():
         arrived(1)
-        send_mixed(0)
         core_half(1)
         arrived(2)
         core_half(2)
@@ -1021,14 +1029,17 @@
         return sum(array[first + i].astype(f32) for i in range(1, 4)) + array[first].astype(f32)
 
     vb[b] = fold(sa[:, half_at(core)] + sr[0])
-    sq[b] = sc[rows_at(core)] + sq[8]
-    sp[b] = sb[...].astype(bf16)
+    sq[b] = (sc[rows_at(core)] + st[0]).astype(bf16)
+    sp[4:12] = sb[...].astype(bf16).reshape(8, 32, 128)
+    for u in range(2):
+        sp[2 * b + u + 12] = sp[4 + 4 * u + b]
     smalls = []
     for p in (1, 2, 3):
         smalls += [
             small_remote(vb.at[b], vb.at[b], 1 + p, batch_peer(p)),
             small_remote(sq.at[b], sq.at[b], 4 + p, batch_peer(p)),
-            small_remote(sp.at[b], sp.at[b], 7 + p, batch_peer(p)),
+            small_remote(sp.at[4 + (b + p) % 4], sp.at[12 + 2 * b], 7 + p, batch_peer(p)),
+            small_remote(sp.at[8 + (b + p) % 4], sp.at[13 + 2 * b], 20 + p, batch_peer(p)),
         ]
 
     @pl.when(side == 0)
@@ -1050,10 +1061,12 @@
     for move in smalls:
         move.wait()
     vb[4 + zed] = total_of(vb, 0).astype(bf16)
-    sq[4 + zed] = total_of(sq, 0)
-    sb[...] = total_of(sp, 0)
-    sp[4] = sb[...].astype(bf16)
-    smalls = [small_remote(sp.at[4], sp.at[5], 17, across_z)]
+    sq[4 + zed] = total_of(sq, 0).astype(bf16)
+    for u in range(2):
+        part = sum(sp[12 + 2 * i + u].astype(f32) for i in range(4))
+        sb[32 * u : 32 * u + 32] = part
+        sp[u] = part.astype(bf16)
+    smalls = [small_remote(sp.at[0:2], sp.at[2:4], 17, across_z)]
     for p in (1, 2, 3):
         smalls += [
             small_remote(vb.at[4 + zed], vb.at[4 + zed], 10 + p, zed_peer(p)),
@@ -1077,19 +1090,20 @@
 
     for move in smalls:
         move.wait()
-    sb[...] = sb[...] + sp[5].astype(f32)
+    for u in range(2):
+        sb[32 * u : 32 * u + 32] = sb[32 * u : 32 * u + 32] + sp[2 + u].astype(f32)
     folded = total_of(vb, 4)
     sf[...] = jnp.concatenate([folded[:8], folded[8:]], axis=1)
     sh[...] = total_of(sq, 4)
     smalls = [
         small_remote(sf, sr.at[1], 18, other),
-        small_remote(sh, sq.at[9], 19, other),
+        small_remote(sh, st.at[1], 19, other),
     ]
     owner = quarter * 2 + side
 
     def give():
         return remote(
-            sb.at[:, lanes(side * 128, 128)], sg, v_sem, (20,), (owner, b), start=False
+            sb.at[lanes(side * 32, 32)], sg, v_sem, (24,), (owner, b), start=False
         )
 
     @pl.when(owner != s)
@@ -1098,7 +1112,7 @@
 
     @pl.when(owner == s)
     def _():
-        sg[...] = sb[:, lanes(side * 128, 128)]
+        sg[...] = sb[lanes(side * 32, 32)]
 
     last_half(0)
     zed_move_o(1).wait()
@@ -1111,7 +1125,7 @@
     oa_ref[:, half_at(core)] = sf[...]
     oa_ref[:, half_at(1 - core)] = sr[1]
     oc_ref[rows_at(core)] = sh[...]
-    oc_ref[rows_at(1 - core)] = sq[9]
+    oc_ref[rows_at(1 - core)] = st[1]
 
     @pl.when(owner != s)
     def _():
@@ -1158,7 +1172,7 @@
             shape((32, 3072), f32),
             shape((32, 1024), f32),
             shape((8, 3072), f32),
-            shape((80, 128), f32),
+            shape((32, 128), f32),
             shape((64, 128), f32),
         ),
         in_specs=specs,
@@ -1212,16 +1226,17 @@
             v(f32, 8, 3072),
             v(f32, 2, 8, 1536),
             v(f32, 8, 1536),
-            v(f32, 80, 256),
-            v(bf16, 6, 80, 256),
+            v(f32, 256, 128),
+            v(bf16, 20, 32, 128),
             v(bf16, 8, 16, 768),
-            v(f32, 80, 128),
+            v(f32, 32, 128),
             v(f32, 64, 128),
-            v(f32, 10, 32, 128),
+            v(bf16, 8, 32, 128),
+            v(f32, 2, 32, 128),
             v(f32, 32, 128),
             dma((5,)),
             dma((3, 4)),
-            dma((2, 21)),
+            dma((2, 25)),
             dma((2, 3)),
             dma((2, 7, 4)),
             dma((2, 7, 4)),
@@ -1280,9 +1295,8 @@
     ln_gain[...] = thin[5:6, 0:32]
     ln_bias[...] = thin[5:6, 1024:1056]
     b_out[...] = thin[5:6, 2048:2080]
-    third = pltpu.roll(sb_ref[...], (4 - b) * 32, 1)
-    w_three[...] = third.T[0:32, 0:64]
-    filt[...] = third[64:65, 0:32]
+    w_three[...] = sb_ref[:, 0:64]
+    filt[...] = sb_ref[...].T[64:65, 0:32]
     w_one[...] = sc_ref[0:33, 0:64]
     w_two[...] = sc_ref[0:64, 64:128]
     b_two[...] = sc_ref[40:41, 0:64]

time: 102 us -> 101 us (level)
  Pallas kernels: 101 us -> 99.6 us
where the time goes in v5:
time: 101 us; the launch traced here: 100 us
  Pallas kernels  99.6 us (99%)
    pallas_call x1, Pallas kernels, whole(): pl.pallas_call(whole_kernel, out_shape=(shape((2, 128, 1024), bf16), shap...  95.8 us
    pallas_call x1, Pallas kernels, settle(): pl.pallas_call(settle_kernel, out_shape=tuple((jax.ShapeDtypeStruct(size,...  3.83 us

profile of v5, /device:TPU:0, one launch (start us, length us, event | category | flops | bytes accessed | tf_op | source)
XLA Modules:
  0.0 100.5 jit_solution(5210424322983645625)
XLA Ops:
  0.7 95.8 %shard_map.315 = (bf16[2,128,1024]{2,1,0:T(8,128)(2,1)}, f32[2,128,1024]{2,1,0:T(8,128)}, f32[32,3072]{1,0:T(8,128)}, f32[32,1024]{1,0:T(8,128)}, f32[8,3072]{1,...) custom-call(bf16[2,128,1024]{2,1,0:T(8,128)(2,1)} %tok_ref.1, bf16[256,1024]{1,0:T(8,128)(2,1)} %bitcast.19, ...), custom_call_target="tpu_custom_call" | custom-call | tf_op jit(solution)/shard_map/pallas_call | solution.py:1167
  96.5 3.8 %shard_map.316 = (bf16[2,128,1024]{2,1,0:T(8,128)(2,1)}, f32[2,128,1024]{2,1,0:T(8,128)}, f32[1,32]{1,0:T(1,128)}, f32[1,32]{1,0:T(1,128)}, f32[32,3072]{1,0:T(8...) custom-call(bf16[2,128,1024]{2,1,0:T(8,128)(2,1)} %get-tuple-element, ...), custom_call_target="tpu_custom_call" | custom-call | tf_op jit(solution)/shard_map/pallas_call | solution.py:1329

commit v6 on v5

--- a/solution.py
+++ b/solution.py
@@ -562,6 +562,7 @@
             a2[t, h] = jnp.where(side == 0, d_summed, gated).astype(bf16)
         exchange(1, (t - quarter + 4) % 4).start()
         send_to(0, t)
+        send_to(2, t)
         return 0
 
     lax.fori_loop(0, 4, project, 0)
@@ -590,8 +591,6 @@
     here = side * 512
     near, far_half = lanes(here, 512), lanes(512 - here, 512)
     wait_tiles(0)
-    for p in range(4):
-        send_to(2, (quarter + p + 2) % 4)
 
     def inverse_to(kind, u, send, given):
         for k in range(2):

time: 101 us -> 98.4 us (0.974)
  Pallas kernels: 99.6 us -> 97.4 us
    pallas_call x1, Pallas kernels: 95.8 us -> 93.6 us  [whole(): pl.pallas_call(whole_kernel, out_shape=(shape((2, 128, 1024), bf16), shap...]
where the time goes in v6:
time: 98.4 us; the launch traced here: 98.2 us
  Pallas kernels  97.4 us (99%)
    pallas_call x1, Pallas kernels, whole(): pl.pallas_call(whole_kernel, out_shape=(shape((2, 128, 1024), bf16), shap...  93.6 us
    pallas_call x1, Pallas kernels, settle(): pl.pallas_call(settle_kernel, out_shape=tuple((jax.ShapeDtypeStruct(size,...  3.83 us

profile of v6, /device:TPU:0, one launch (start us, length us, event | category | flops | bytes accessed | tf_op | source)
XLA Modules:
  0.0 98.2 jit_solution(15596842404638429204)
XLA Ops:
  0.7 93.6 %shard_map.315 = (bf16[2,128,1024]{2,1,0:T(8,128)(2,1)}, f32[2,128,1024]{2,1,0:T(8,128)}, f32[32,3072]{1,0:T(8,128)}, f32[32,1024]{1,0:T(8,128)}, f32[8,3072]{1,...) custom-call(bf16[2,128,1024]{2,1,0:T(8,128)(2,1)} %tok_ref.1, bf16[256,1024]{1,0:T(8,128)(2,1)} %bitcast.19, ...), custom_call_target="tpu_custom_call" | custom-call | tf_op jit(solution)/shard_map/pallas_call | solution.py:1166
  94.2 3.8 %shard_map.316 = (bf16[2,128,1024]{2,1,0:T(8,128)(2,1)}, f32[2,128,1024]{2,1,0:T(8,128)}, f32[1,32]{1,0:T(1,128)}, f32[1,32]{1,0:T(1,128)}, f32[32,3072]{1,0:T(8...) custom-call(bf16[2,128,1024]{2,1,0:T(8,128)(2,1)} %get-tuple-element, ...), custom_call_target="tpu_custom_call" | custom-call | tf_op jit(solution)/shard_map/pallas_call | solution.py:1328

commit v7 on v6

--- a/solution.py
+++ b/solution.py
@@ -438,6 +438,7 @@
 
     lax.fori_loop(0, 8, norm_rows, 0)
 
+    nt[b] = normed[0:256].T.reshape(4, 2, 128, 256)
     pl.semaphore_wait(barrier, 10)
     edge = remote(
         tok_ref.at[:, 112:128],
@@ -452,7 +453,6 @@
     def _():
         edge.start()
 
-    nt[b] = normed[0:256].T.reshape(4, 2, 128, 256)
     moves = {}
     shards = (pair_cross, pair, cross, zed)
     x, y = b % 2, b // 2

time: 98.4 us -> 98.7 us (level)
  no operation moved by 1% of the time
where the time goes in v7:
time: 98.7 us; the launch traced here: 98.5 us
  Pallas kernels  97.7 us (99%)
    pallas_call x1, Pallas kernels, whole(): pl.pallas_call(whole_kernel, out_shape=(shape((2, 128, 1024), bf16), shap...  93.9 us
    pallas_call x1, Pallas kernels, settle(): pl.pallas_call(settle_kernel, out_shape=tuple((jax.ShapeDtypeStruct(size,...  3.83 us

profile of v7, /device:TPU:0, one launch (start us, length us, event | category | flops | bytes accessed | tf_op | source)
XLA Modules:
  0.0 98.5 jit_solution(8833838755990166990)
XLA Ops:
  0.7 93.9 %shard_map.315 = (bf16[2,128,1024]{2,1,0:T(8,128)(2,1)}, f32[2,128,1024]{2,1,0:T(8,128)}, f32[32,3072]{1,0:T(8,128)}, f32[32,1024]{1,0:T(8,128)}, f32[8,3072]{1,...) custom-call(bf16[2,128,1024]{2,1,0:T(8,128)(2,1)} %tok_ref.1, bf16[256,1024]{1,0:T(8,128)(2,1)} %bitcast.19, ...), custom_call_target="tpu_custom_call" | custom-call | tf_op jit(solution)/shard_map/pallas_call | solution.py:1166
  94.5 3.8 %shard_map.316 = (bf16[2,128,1024]{2,1,0:T(8,128)(2,1)}, f32[2,128,1024]{2,1,0:T(8,128)}, f32[1,32]{1,0:T(1,128)}, f32[1,32]{1,0:T(1,128)}, f32[32,3072]{1,0:T(8...) custom-call(bf16[2,128,1024]{2,1,0:T(8,128)(2,1)} %get-tuple-element, ...), custom_call_target="tpu_custom_call" | custom-call | tf_op jit(solution)/shard_map/pallas_call | solution.py:1328
